TPU v7x, 256 devices: a whole 4x4x8 slice. The times are simulated.
256 devices in a mesh: member: 8 (over x, core), space: 32 (over z, y).
Axes of the slice: x: 4, y: 4, z: 8, core: 2. Of those that a mesh axis runs over, the one named last changes fastest.
Arguments:
- noisy: float32 [8, 192, 32, 128], P('member', 'space'), may hold values from -12 to 12
- mean_field: float32 [192, 32, 128], P('space'), may hold values from -6 to 6
- coarse: float32 [256, 192], P('space', 'member'), may hold values from -6 to 6
- counts: int32 [32], P('space'), may hold values from 2 to 6, as said below
- src: int32 [192, 4], P('space'), may hold values from 0 to 7
- widx: int32 [192, 4], P('space'), may hold values from 0 to 15
- table: float32 [16], replicated, may hold values from 0.2 to 1
- sigma: float32 [8], P('member'), may hold values from 0.5 to 4
- sigma_next: float32 [8], P('member'), may hold values from 0.1 to 0.4
- w_stem: bfloat16 [180, 128], replicated, may hold values from -0.4375 to 0.4375
- noise_embed: float32 [128], replicated, may hold values from -9 to 9
- w_down: bfloat16 [128, 256], replicated, may hold values from -0.5 to 0.5
- w_query: bfloat16 [256, 256], replicated, may hold values from -0.25 to 0.25
- w_key: bfloat16 [256, 256], replicated, may hold values from -8.125 to 8.125
- w_value: bfloat16 [256, 256], replicated, may hold values from -0.375 to 0.375
- w_attn_out: bfloat16 [256, 256], replicated, may hold values from -0.375 to 0.375
- w_up: bfloat16 [256, 128], replicated, may hold values from -0.375 to 0.375
- w_out: bfloat16 [128, 36], replicated, may hold values from -0.1875 to 0.1875
Outputs:
- denoised: float32 [8, 192, 32, 128], P('member', 'space')
- next_state: float32 [8, 192, 32, 128], P('member', 'space')
Inputs may be any that keep to these rules, and one draw needn't show every extreme that they name: `counts`: live patches of each space device; some device holds 6 and some holds 2. `src`: a patch's coarse blocks are held by the space device that holds the patch; slots that are not live have entries too.
All inputs are finite; a program needn't handle non-finite values.
Results may differ from a plain program's by a relative error of at most 0.006.
Values may be sent and summed in bfloat16 or wider, within the bound.
No kernel may reach another device: no remote copies, remote signals or barrier semaphores. Data moves between devices by JAX's collectives and lax.ppermute only.
A program may use at most 64 MiB of HBM per device.

v0:
```python
import math

import jax
import jax.numpy as jnp
from jax import lax
from jax.sharding import PartitionSpec as P

VARS = 4
CCH = 12
CIN = 20
CH = 128
CH2 = 256
HEAD_DIM = 64
P_SIZE = 32
M = 16
W = 32
SLOTS = 6
FACTOR = 8
POOL = 8
BLK_DEV = 8
NW = 16
DOM = 64
TOKENS = 32
BR = 4
BW = 4


SIGMA_DATA = 0.5
NORM_EPS = 1e-06


def extended_2(cells, sides, width):
    for axis, dim in sides:
        count = lax.axis_size(axis)
        ends = count - 1
        head = lax.slice_in_dim(cells, 0, width, axis=dim)
        tail = lax.slice_in_dim(cells, cells.shape[dim] - width, cells.shape[dim], axis=dim)
        cells = jnp.concatenate(
            [
                lax.ppermute(tail, axis, [(i, (i + 1) % count) for i in range(ends)]),
                cells,
                lax.ppermute(head, axis, [((i + 1) % count, i) for i in range(ends)]),
            ],
            axis=dim,
        )
    return cells


def interp_matrix(fine_count, coarse_count):
    position = (jnp.arange(fine_count, dtype=jnp.float32) + 0.5) / FACTOR - 0.5
    position = jnp.clip(position, 0.0, coarse_count - 1.0)
    centers = jnp.arange(coarse_count, dtype=jnp.float32)
    return jnp.maximum(0.0, 1.0 - jnp.abs(position[:, None] - centers[None, :]))


def upsample_blocks(mixed_blocks):
    batch_count = mixed_blocks.shape[0]
    cell_grid = mixed_blocks.reshape(batch_count, BR, BW, CCH)
    row_map = interp_matrix(P_SIZE, BR)
    col_map = interp_matrix(W, BW)
    tall_rows = jnp.einsum("pa,sabk->spbk", row_map, cell_grid, precision=lax.Precision.HIGHEST)
    return jnp.einsum("cb,spbk->spck", col_map, tall_rows, precision=lax.Precision.HIGHEST)


def shift_columns(piece, col_tap):
    zero_col = jnp.zeros_like(piece[:, :1])
    if col_tap == 0:
        return jnp.concatenate([zero_col, piece[:, :-1]], axis=1)
    if col_tap == 2:
        return jnp.concatenate([piece[:, 1:], zero_col], axis=1)
    return piece


def stem_conv(extended, noise_shift, w_stem):
    row_count = extended.shape[0] - 2
    cell_rows = extended.reshape((row_count + 2) * W, CIN)
    tap_weights = w_stem.reshape(9, CIN, CH).transpose(1, 0, 2).reshape(CIN, 9 * CH)
    tap_terms = jnp.dot(cell_rows, tap_weights, preferred_element_type=jnp.float32).reshape(
        row_count + 2, W, 9 * CH
    )
    summed = jnp.zeros((row_count, W, CH), jnp.float32)
    for col_tap in range(3):
        column_sum = jnp.zeros((row_count, W, CH), jnp.float32)
        for row_tap in range(3):
            lane_start = (3 * row_tap + col_tap) * CH
            column_sum = (
                column_sum
                + tap_terms[row_tap : row_tap + row_count, :, lane_start : lane_start + CH]
            )
        summed = summed + shift_columns(column_sum, col_tap)
    return (
        jax.nn.silu(summed + noise_shift[None, None, :])
        .astype(jnp.bfloat16)
        .reshape(row_count, W * CH)
    )


def stem_all(inputs_bf, row_above, row_below, held_count, noise_shift, w_stem):
    slot_ids = jnp.arange(SLOTS, dtype=jnp.int32)
    uppers = jnp.concatenate([row_above[None], inputs_bf[:-1, P_SIZE - 1]], axis=0)
    lowers = jnp.concatenate([inputs_bf[1:, 0], row_below[None]], axis=0)
    lowers = jnp.where((slot_ids == held_count - 1)[:, None], row_below[None], lowers)
    extended = jnp.concatenate([uppers[:, None], inputs_bf, lowers[:, None]], axis=1)
    return lax.map(lambda piece_rows: stem_conv(piece_rows, noise_shift, w_stem), extended)


def pool_domain(domain):
    cell_grid = domain.astype(jnp.float32).reshape(DOM // POOL, POOL, W // POOL, POOL, CH)
    return jnp.mean(cell_grid, axis=(1, 3)).reshape(TOKENS, CH).astype(jnp.bfloat16)


def bottleneck(pooled, w_down, w_query, w_key, w_value, w_attn_out, w_up):
    batch_count = pooled.shape[0]
    heads_count = CH2 // HEAD_DIM
    flat_rows = pooled.reshape(batch_count * TOKENS, CH)
    zeta = jax.nn.silu(jnp.dot(flat_rows, w_down, preferred_element_type=jnp.float32))
    inv_scale = lax.rsqrt(jnp.mean(zeta * zeta, axis=-1, keepdims=True) + NORM_EPS)
    normed = (zeta * inv_scale).astype(jnp.bfloat16)
    query_rows = jnp.dot(normed, w_query, preferred_element_type=jnp.float32).astype(jnp.bfloat16)
    key_rows = jnp.dot(normed, w_key, preferred_element_type=jnp.float32).astype(jnp.bfloat16)
    value_rows = jnp.dot(normed, w_value, preferred_element_type=jnp.float32).astype(jnp.bfloat16)
    query_rows = query_rows.reshape(batch_count, TOKENS, heads_count, HEAD_DIM)
    key_rows = key_rows.reshape(batch_count, TOKENS, heads_count, HEAD_DIM)
    value_rows = value_rows.reshape(batch_count, TOKENS, heads_count, HEAD_DIM)
    scores = jnp.einsum(
        "sthd,suhd->shtu", query_rows, key_rows, preferred_element_type=jnp.float32
    ) / math.sqrt(HEAD_DIM)
    scores = scores - jnp.max(scores, axis=-1, keepdims=True)
    expsum = jnp.exp(scores)
    weights_att = (expsum / jnp.sum(expsum, axis=-1, keepdims=True)).astype(jnp.bfloat16)
    attended = jnp.einsum(
        "shtu,suhd->sthd", weights_att, value_rows, preferred_element_type=jnp.float32
    )
    attended = attended.astype(jnp.bfloat16).reshape(batch_count * TOKENS, CH2)
    resid = (zeta + jnp.dot(attended, w_attn_out, preferred_element_type=jnp.float32)).astype(
        jnp.bfloat16
    )
    lifted = jnp.dot(resid, w_up, preferred_element_type=jnp.float32)
    return lifted.reshape(batch_count, TOKENS, CH)


def shift_rows(piece, row_tap):
    zero_row = jnp.zeros_like(piece[:1])
    if row_tap == 0:
        return jnp.concatenate([zero_row, piece[:-1]], axis=0)
    if row_tap == 2:
        return jnp.concatenate([piece[1:], zero_row], axis=0)
    return piece


def shift_lanes(piece, col_tap):
    zero_lanes = jnp.zeros_like(piece[:, :VARS])
    if col_tap == 0:
        return jnp.concatenate([zero_lanes, piece[:, :-VARS]], axis=1)
    if col_tap == 2:
        return jnp.concatenate([piece[:, VARS:], zero_lanes], axis=1)
    return piece


def output_conv(domain, lifted, w_out):
    cell_grid = domain.reshape(DOM, W, CH).astype(jnp.float32)
    token_grid = lifted.reshape(DOM // POOL, 1, W // POOL, 1, CH)
    raised = jnp.broadcast_to(token_grid, (DOM // POOL, POOL, W // POOL, POOL, CH)).reshape(
        DOM, W, CH
    )
    active = jax.nn.silu(cell_grid + raised).astype(jnp.bfloat16)
    kernel = w_out.reshape(CH, 3, 3, VARS)
    tap_terms = jnp.einsum("rwc,cabv->abrwv", active, kernel, preferred_element_type=jnp.float32)
    tap_terms = tap_terms.reshape(3, 3, DOM, W * VARS)
    summed = jnp.zeros((DOM, W * VARS), jnp.float32)
    for col_tap in range(3):
        column_sum = jnp.zeros((DOM, W * VARS), jnp.float32)
        for row_tap in range(3):
            column_sum = column_sum + shift_rows(tap_terms[row_tap, col_tap], row_tap)
        summed = summed + shift_lanes(column_sum, col_tap)
    return summed


def ramp_weight(position):
    return jnp.minimum(position + 1, DOM - position).astype(jnp.float32)


def shards(
    noisy,
    mean_field,
    coarse,
    counts,
    src,
    widx,
    table,
    sigma,
    sigma_next,
    w_stem,
    noise_embed,
    w_down,
    w_query,
    w_key,
    w_value,
    w_attn_out,
    w_up,
    w_out,
):
    held_count = counts[0]
    position = lax.axis_index("space")
    owners = lax.axis_size("space")
    has_left = position > 0
    has_right = position < owners - 1
    slot_ids = jnp.arange(SLOTS, dtype=jnp.int32)
    blocks = lax.all_gather(coarse, "member", axis=1, tiled=True)
    block_pick = (src[:, :, None] == jnp.arange(BLK_DEV, dtype=jnp.int32)[None, None, :]).astype(
        jnp.float32
    )
    table_pick = (widx[:, :, None] == jnp.arange(NW, dtype=jnp.int32)[None, None, :]).astype(
        jnp.float32
    )
    mix_weights = jnp.sum(table_pick * table[None, None, :], axis=-1)
    combine = jnp.sum(mix_weights[:, :, None] * block_pick, axis=1)
    mixed_blocks = jnp.dot(combine, blocks, precision=lax.Precision.HIGHEST)
    condition = upsample_blocks(mixed_blocks)
    state_now = noisy[0]
    noise_level = sigma[0]
    level_next = sigma_next[0]
    spread = noise_level * noise_level + SIGMA_DATA * SIGMA_DATA
    c_in = lax.rsqrt(spread)
    c_skip = SIGMA_DATA * SIGMA_DATA / spread
    c_out = noise_level * SIGMA_DATA * lax.rsqrt(spread)
    noise_shift = jnp.log(noise_level) / 4.0 * noise_embed
    inputs_bf = jnp.concatenate(
        [
            (c_in * state_now).reshape(SLOTS, P_SIZE, W, VARS),
            mean_field.reshape(SLOTS, P_SIZE, W, VARS),
            condition,
        ],
        axis=-1,
    )
    inputs_bf = inputs_bf.astype(jnp.bfloat16).reshape(SLOTS, P_SIZE, W * CIN)
    last_inputs = lax.dynamic_index_in_dim(inputs_bf, held_count - 1, 0, keepdims=False)
    edge_rows = jnp.stack([inputs_bf[0, :1], last_inputs[P_SIZE - 1 :]])
    rim_rows = extended_2(edge_rows, (("space", 0),), 1)
    features = stem_all(inputs_bf, rim_rows[0, 0], rim_rows[3, 0], held_count, noise_shift, w_stem)
    last_features = lax.dynamic_index_in_dim(features, held_count - 1, 0, keepdims=False)
    feature_edges = jnp.stack([features[0, :M], last_features[P_SIZE - M :]])
    outer_rows = extended_2(feature_edges, (("space", 0),), 1)
    prev_tail = outer_rows[0]
    next_head = outer_rows[3]

    def domain_of(slot_index):
        own_rows = lax.dynamic_index_in_dim(features, slot_index, 0, keepdims=False)
        before = lax.dynamic_index_in_dim(
            features, jnp.maximum(slot_index - 1, 0), 0, keepdims=False
        )[P_SIZE - M :]
        after_rows = lax.dynamic_index_in_dim(
            features, jnp.minimum(slot_index + 1, SLOTS - 1), 0, keepdims=False
        )[:M]
        before = jnp.where(slot_index == 0, prev_tail, before)
        after_rows = jnp.where(slot_index == held_count - 1, next_head, after_rows)
        return jnp.concatenate([before, own_rows, after_rows], axis=0)

    pooled = lax.map(lambda slot_index: pool_domain(domain_of(slot_index)), slot_ids)
    lifted = bottleneck(pooled, w_down, w_query, w_key, w_value, w_attn_out, w_up)
    field_out = lax.map(
        lambda item_pair: output_conv(domain_of(item_pair[0]), item_pair[1], w_out),
        (slot_ids, lifted),
    )
    last_field = lax.dynamic_index_in_dim(field_out, held_count - 1, 0, keepdims=False)
    strip_rows = jnp.stack([field_out[0, :M], last_field[P_SIZE + M :]])
    outer_strips = extended_2(strip_rows, (("space", 0),), 1)
    from_prev = jnp.concatenate([outer_strips[0][None], field_out[:-1, P_SIZE + M :]], axis=0)
    from_next = jnp.concatenate([field_out[1:, :M], outer_strips[3][None]], axis=0)
    from_next = jnp.where(
        (slot_ids == held_count - 1)[:, None, None], outer_strips[3][None], from_next
    )
    prev_live = (slot_ids > 0) | has_left
    next_live = (slot_ids < held_count - 1) | has_right
    row_ids = jnp.arange(P_SIZE, dtype=jnp.int32)
    margin_ids = jnp.arange(M, dtype=jnp.int32)
    own_weight = ramp_weight(M + row_ids)
    prev_weight = jnp.where(prev_live[:, None], ramp_weight(P_SIZE + M + margin_ids)[None, :], 0.0)
    next_weight = jnp.where(next_live[:, None], ramp_weight(margin_ids)[None, :], 0.0)
    denominator = jnp.broadcast_to(own_weight[None, :], (SLOTS, P_SIZE))
    denominator = denominator.at[:, :M].add(prev_weight)
    denominator = denominator.at[:, P_SIZE - M :].add(next_weight)
    numerator = own_weight[None, :, None] * field_out[:, M : M + P_SIZE]
    numerator = numerator.at[:, :M].add(prev_weight[:, :, None] * from_prev)
    numerator = numerator.at[:, P_SIZE - M :].add(next_weight[:, :, None] * from_next)
    blended = numerator / denominator[:, :, None]
    denoised = c_skip * state_now + c_out * blended
    stepped = state_now + (level_next / noise_level - 1.0) * (state_now - denoised)
    live_mask = (slot_ids < held_count)[:, None, None]
    denoised = jnp.where(live_mask, denoised, 0.0)
    stepped = jnp.where(live_mask, stepped, 0.0)
    return (denoised[None], stepped[None])


def solution(mesh):
    placed = (
        P("member", "space", None, None),
        P("space", None, None),
        P("space", "member"),
        P("space"),
        P("space", None),
        P("space", None),
        P(),
        P("member"),
        P("member"),
        P(),
        P(),
        P(),
        P(),
        P(),
        P(),
        P(),
        P(),
        P(),
    )
    return jax.shard_map(
        shards,
        mesh=mesh,
        in_specs=placed,
        out_specs=(P("member", "space", None, None), P("member", "space", None, None)),
        check_vma=False,
    )
```

profile of v0, /device:TPU:120, one launch (start us, length us, event | category | flops | bytes accessed | tf_op | source)
XLA Modules:
  0.0 184.7 jit_solution(17819968531911747519)
XLA Ops:
  2.1 0.9 multiply_convert_fusion.3
  3.3 13.3 %all-gather = f32[8,24,8]{1,2,0:T(8,128)S(1)} all-gather(f32[1,24,8]{1,2,0:T(8,128)} %bitcast.261), channel_id=1, replica_groups=mesh['member'=8,'space'=32] {'member'}, dimensions={0}, use_global_device_ids=true | all-gather | bytes 6912 | tf_op jit(solution)/shard_map/all_gather | solution.py:209
  16.7 0.8 copy.130
  17.5 0.8 copy.129
  18.3 0.8 select_reduce_fusion.1
  19.9 2.0 %fusion.17 = bf16[6,32,32,12]{2,1,3,0:T(8,128)(2,1)S(1)} fusion(f32[6,32,4,12]{1,3,2,0:T(8,128)S(1)} %convolution_bitcast_fusion.1, f32[32]{0:T(128)S(1)} %add_clamp_fusion), kind=kOutput, calls=%fused_computation.58 | convolution fusion | flops 3613184 | bytes 184448 | tf_op jit(solution)/shard_map/cb,spbk->spck/dot_general | solution.py:62
  22.5 1.6 copy.137
  24.1 3.8 %convert_element_type.131 = bf16[6,32,640]{2,1,0:T(8,128)(2,1)} reshape(bf16[6,32,32,20]{3,2,1,0:T(8,128)(2,1)S(1)} %copy.137) | data formatting | bytes 491520 | tf_op jit(solution)/shard_map/convert_element_type | solution.py:236
  27.9 0.7 constant_dynamic-slice_fusion.4
  28.6 2.6 %collective-permute-start.1 = (bf16[1,1,640]{2,1,0:T(2,128)(2,1)S(1)}, bf16[1,1,640]{2,1,0:T(2,128)(2,1)S(1)}, u32[]{:S(2)}, u32[]{:S(2)}) collective-permute-start(bf16[1,1,640]{2,1,0:T(2,128)(2,1)S(1)} %get-tuple-element.401), channel_id=1, source_target_pairs={{1,0},{2,1},{3,2},{4,3},{5,4},{6,5},{7,6},{8,7},{9,8},{10,9},{11,1... | collective-permute-start | bytes 3848 | tf_op jit(solution)/shard_map/ppermute | solution.py:42
  31.3 6.5 %collective-permute-start = (bf16[1,1,640]{2,1,0:T(2,128)(2,1)S(1)}, bf16[1,1,640]{2,1,0:T(2,128)(2,1)S(1)}, u32[]{:S(2)}, u32[]{:S(2)}) collective-permute-start(bf16[1,1,640]{2,1,0:T(2,128)(2,1)S(1)} %get-tuple-element.400), channel_id=1, source_target_pairs={{0,1},{1,2},{2,3},{3,4},{4,5},{5,6},{6,7},{7,8},{8,9},{9,10},{10,1... | collective-permute-start | bytes 3848 | tf_op jit(solution)/shard_map/ppermute | solution.py:40
  37.8 0.9 fusion.70
  39.5 0.8 add_select_fusion
  40.7 1.1 pad_maximum_fusion.3
  41.8 17.0 %while.41 = (s32[]{:T(128)}, bf16[6,32,4096]{2,1,0:T(8,128)(2,1)S(1)}, bf16[6,34,640]{2,1,0:T(8,128)(2,1)S(1)}, bf16[180,128]{1,0:T(8,128)(2,1)S(1)}, f32[128]{0:T(128)S(1)}, /*index=5*/s32[]{:T(128)}) while((s32[]{:T(128)}, bf16[6,32,4096]{2,1,0:T(8,128)(2,1)S(1)}, bf16[6,34,640]{2,1,0:T(8,128)(2,1)S(1)}, bf16[180,128]{1,0:T(8,128)(2,1)S(1)}, ...), condition=%wide.region_3.4_spmd, body=%wide.region_2.3_spmd.sunk | while | flops 51953664 | bytes 19808332 | solution.py:104
  42.6 0.8 fusion.110
  45.4 0.8 fusion.110
  48.3 0.8 fusion.110
  51.1 0.8 fusion.110
  54.0 0.8 fusion.110
  56.8 0.8 fusion.110
  58.9 6.1 %collective-permute-start.2 = (bf16[1,16,4096]{2,1,0:T(8,128)(2,1)S(1)}, bf16[1,16,4096]{2,1,0:T(8,128)(2,1)S(1)}, u32[]{:S(2)}, u32[]{:S(2)}) collective-permute-start(bf16[1,16,4096]{2,1,0:T(8,128)(2,1)S(1)} %get-tuple-element.399), channel_id=1, source_target_pairs={{0,1},{1,2},{2,3},{3,4},{4,5},{5,6},{6,7},{7,8},{8,9},{9,10},{10,1... | collective-permute-start | bytes 393224 | tf_op jit(solution)/shard_map/ppermute | solution.py:40
  64.9 2.1 %collective-permute-start.3 = (bf16[1,16,4096]{2,1,0:T(8,128)(2,1)S(1)}, bf16[1,16,4096]{2,1,0:T(8,128)(2,1)S(1)}, u32[]{:S(2)}, u32[]{:S(2)}) collective-permute-start(bf16[1,16,4096]{2,1,0:T(8,128)(2,1)S(1)} %get-tuple-element.398), channel_id=1, source_target_pairs={{1,0},{2,1},{3,2},{4,3},{5,4},{6,5},{7,6},{8,7},{9,8},{10,9},{11,1... | collective-permute-start | bytes 393224 | tf_op jit(solution)/shard_map/ppermute | solution.py:42
  68.2 6.9 %collective-permute-done.3 = bf16[1,16,4096]{2,1,0:T(8,128)(2,1)S(1)} collective-permute-done((bf16[1,16,4096]{2,1,0:T(8,128)(2,1)S(1)}, bf16[1,16,4096]{2,1,0:T(8,128)(2,1)S(1)}, u32[]{:S(2)}, u32[]{:S(2)}) %collective-permute-start.3) | collective-permute-done | bytes 131104 | tf_op jit(solution)/shard_map/ppermute | solution.py:42
  75.1 32.6 %while.42 = (s32[]{:T(128)}, bf16[6,32,128]{2,1,0:T(8,128)(2,1)S(1)}, s32[6]{0:T(128)S(1)}, bf16[6,32,4096]{2,1,0:T(8,128)(2,1)S(1)}, bf16[16,4096]{1,0:T(8,128)...) while((s32[]{:T(128)}, ...), condition=%wide.region_6.7_spmd, body=%wide.region_4.6_spmd.sunk | while | flops 2232335 | bytes 2941233 | solution.py:259
  110.5 1.0 fusion.22
  111.4 58.2 %while.43 = (s32[]{:T(128)}, f32[6,64,128]{2,1,0:T(8,128)}, s32[6]{0:T(128)S(1)}, bf16[16,4096]{1,0:T(8,128)(2,1)S(1)}, bf16[6,32,4096]{2,1,0:T(8,128)(2,1)S(1)}...) while((s32[]{:T(128)}, f32[6,64,128]{2,1,0:T(8,128)}, ...), condition=%wide.wide.region_11.12_spmd, body=%wide.wide.region_10.11_spmd.sunk | while | flops 21429264 | bytes 10169273 | solution.py:261
  116.9 0.7 constant_dynamic-slice_fusion.9
  117.9 1.0 convolution_bitcast_fusion.4
  118.9 1.1 copy.211
  126.6 0.7 constant_dynamic-slice_fusion.9
  127.6 1.0 convolution_bitcast_fusion.4
  128.6 1.1 copy.211
  136.3 0.7 constant_dynamic-slice_fusion.9
  137.3 1.0 convolution_bitcast_fusion.4
  138.3 1.1 copy.211
  147.0 1.0 convolution_bitcast_fusion.4
  148.0 1.1 copy.211
  156.8 1.0 convolution_bitcast_fusion.4
  157.7 1.1 copy.211
  166.5 1.0 convolution_bitcast_fusion.4
  167.4 1.1 copy.211
  169.7 1.0 slice_multiply_fusion
  171.4 1.9 %collective-permute-start.4 = (f32[1,16,128]{2,1,0:T(8,128)S(1)}, f32[1,16,128]{2,1,0:T(8,128)S(1)}, u32[]{:S(2)}, u32[]{:S(2)}) collective-permute-start(f32[1,16,128]{2,1,0:T(8,128)S(1)} %get-tuple-element.409), channel_id=1, source_target_pairs={{0,1},{1,2},{2,3},{3,4},{4,5},{5,6},{6,7},{7,8},{8,9},{9,10},{10,1... | collective-permute-start | bytes 24584 | tf_op jit(solution)/shard_map/ppermute | solution.py:40
  173.3 0.8 fusion.71
  174.1 3.9 %collective-permute-start.5 = (f32[1,16,128]{2,1,0:T(8,128)S(1)}, f32[1,16,128]{2,1,0:T(8,128)S(1)}, u32[]{:S(2)}, u32[]{:S(2)}) collective-permute-start(f32[1,16,128]{2,1,0:T(8,128)S(1)} %get-tuple-element.408), channel_id=1, source_target_pairs={{1,0},{2,1},{3,2},{4,3},{5,4},{6,5},{7,6},{8,7},{9,8},{10,9},{11,1... | collective-permute-start | bytes 24584 | tf_op jit(solution)/shard_map/ppermute | solution.py:42
  178.1 4.8 %collective-permute-done.5 = f32[1,16,128]{2,1,0:T(8,128)S(1)} collective-permute-done((f32[1,16,128]{2,1,0:T(8,128)S(1)}, f32[1,16,128]{2,1,0:T(8,128)S(1)}, u32[]{:S(2)}, u32[]{:S(2)}) %collective-permute-start.5) | collective-permute-done | bytes 8224 | tf_op jit(solution)/shard_map/ppermute | solution.py:42
  183.0 1.7 fusion.31
  (340 shorter events, 39.9 us)
Async XLA Ops:
  0.6 107.5 %copy-start = (bf16[256,256]{1,0:T(8,128)(2,1)S(1)}, bf16[256,256]{1,0:T(8,128)(2,1)}, u32[]{:S(2)}) copy-start(bf16[256,256]{1,0:T(8,128)(2,1)} %param.44) | copy-start | bytes 393220
  0.6 21.3 %copy-start.8 = (f32[6,32,128]{2,1,0:T(8,128)S(1)}, f32[6,32,128]{2,1,0:T(8,128)}, u32[]{:S(2)}) copy-start(f32[6,32,128]{2,1,0:T(8,128)} %param.33) | copy-start | bytes 294916
  24.1 15.4 %copy-start.13 = (f32[128]{0:T(128)S(1)}, f32[128]{0:T(128)}, u32[]{:S(2)}) copy-start(f32[128]{0:T(128)} %param.42) | copy-start | bytes 1540
  24.1 17.7 %copy-start.5 = (bf16[180,128]{1,0:T(8,128)(2,1)S(1)}, bf16[180,128]{1,0:T(8,128)(2,1)}, u32[]{:S(2)}) copy-start(bf16[180,128]{1,0:T(8,128)(2,1)} %param.41) | copy-start | bytes 138244
  28.6 11.9 %collective-permute-start.1 = (bf16[1,1,640]{2,1,0:T(2,128)(2,1)S(1)}, bf16[1,1,640]{2,1,0:T(2,128)(2,1)S(1)}, u32[]{:S(2)}, u32[]{:S(2)}) collective-permute-start(bf16[1,1,640]{2,1,0:T(2,128)(2,1)S(1)} %get-tuple-element.401), channel_id=1, source_target_pairs={{1,0},{2,1},{3,2},{4,3},{5,4},{6,5},{7,6},{8,7},{9,8},{10,9},{11,1... | collective-permute-start | bytes 3848 | tf_op jit(solution)/shard_map/ppermute | solution.py:42
  31.3 9.2 %collective-permute-start = (bf16[1,1,640]{2,1,0:T(2,128)(2,1)S(1)}, bf16[1,1,640]{2,1,0:T(2,128)(2,1)S(1)}, u32[]{:S(2)}, u32[]{:S(2)}) collective-permute-start(bf16[1,1,640]{2,1,0:T(2,128)(2,1)S(1)} %get-tuple-element.400), channel_id=1, source_target_pairs={{0,1},{1,2},{2,3},{3,4},{4,5},{5,6},{6,7},{7,8},{8,9},{9,10},{10,1... | collective-permute-start | bytes 3848 | tf_op jit(solution)/shard_map/ppermute | solution.py:40
  41.8 25.4 %copy-start.9 = (bf16[128,36]{0,1:T(8,128)(2,1)S(1)}, bf16[128,36]{0,1:T(8,128)(2,1)}, u32[]{:S(2)}) copy-start(bf16[128,36]{0,1:T(8,128)(2,1)} %param.49) | copy-start | bytes 27652
  58.9 9.3 %collective-permute-start.2 = (bf16[1,16,4096]{2,1,0:T(8,128)(2,1)S(1)}, bf16[1,16,4096]{2,1,0:T(8,128)(2,1)S(1)}, u32[]{:S(2)}, u32[]{:S(2)}) collective-permute-start(bf16[1,16,4096]{2,1,0:T(8,128)(2,1)S(1)} %get-tuple-element.399), channel_id=1, source_target_pairs={{0,1},{1,2},{2,3},{3,4},{4,5},{5,6},{6,7},{7,8},{8,9},{9,10},{10,1... | collective-permute-start | bytes 393224 | tf_op jit(solution)/shard_map/ppermute | solution.py:40
  64.9 10.2 %collective-permute-start.3 = (bf16[1,16,4096]{2,1,0:T(8,128)(2,1)S(1)}, bf16[1,16,4096]{2,1,0:T(8,128)(2,1)S(1)}, u32[]{:S(2)}, u32[]{:S(2)}) collective-permute-start(bf16[1,16,4096]{2,1,0:T(8,128)(2,1)S(1)} %get-tuple-element.398), channel_id=1, source_target_pairs={{1,0},{2,1},{3,2},{4,3},{5,4},{6,5},{7,6},{8,7},{9,8},{10,9},{11,1... | collective-permute-start | bytes 393224 | tf_op jit(solution)/shard_map/ppermute | solution.py:42
  75.1 32.6 %copy-start.11 = (bf16[128,256]{1,0:T(8,128)(2,1)S(1)}, bf16[128,256]{1,0:T(8,128)(2,1)}, u32[]{:S(2)}) copy-start(bf16[128,256]{1,0:T(8,128)(2,1)} %param.43) | copy-start | bytes 196612
  107.7 0.9 copy-start.6
  108.2 1.3 copy-start.7
  109.5 1.0 copy-start.10
  109.5 0.9 copy-start.12
  111.4 5.4 %copy-start.1 = (bf16[16,4096]{1,0:T(8,128)(2,1)}, bf16[16,4096]{1,0:T(8,128)(2,1)S(1)}, u32[]{:S(2)}) copy-start(bf16[16,4096]{1,0:T(8,128)(2,1)S(1)} %get-tuple-element.735) | copy-start | bytes 393220 | tf_op jit(solution)/shard_map/while
  111.4 5.4 %copy-start.3 = (bf16[16,4096]{1,0:T(8,128)(2,1)}, bf16[16,4096]{1,0:T(8,128)(2,1)S(1)}, u32[]{:S(2)}) copy-start(bf16[16,4096]{1,0:T(8,128)(2,1)S(1)} %get-tuple-element.738) | copy-start | bytes 393220 | tf_op jit(solution)/shard_map/while
  120.0 1.1 copy-start.2
  120.0 1.1 copy-start.4
  121.2 5.4 %copy-start.1 = (bf16[16,4096]{1,0:T(8,128)(2,1)}, bf16[16,4096]{1,0:T(8,128)(2,1)S(1)}, u32[]{:S(2)}) copy-start(bf16[16,4096]{1,0:T(8,128)(2,1)S(1)} %get-tuple-element.735) | copy-start | bytes 393220 | tf_op jit(solution)/shard_map/while
  121.2 5.4 %copy-start.3 = (bf16[16,4096]{1,0:T(8,128)(2,1)}, bf16[16,4096]{1,0:T(8,128)(2,1)S(1)}, u32[]{:S(2)}) copy-start(bf16[16,4096]{1,0:T(8,128)(2,1)S(1)} %get-tuple-element.738) | copy-start | bytes 393220 | tf_op jit(solution)/shard_map/while
  129.7 1.1 copy-start.2
  129.7 1.1 copy-start.4
  130.9 5.4 %copy-start.1 = (bf16[16,4096]{1,0:T(8,128)(2,1)}, bf16[16,4096]{1,0:T(8,128)(2,1)S(1)}, u32[]{:S(2)}) copy-start(bf16[16,4096]{1,0:T(8,128)(2,1)S(1)} %get-tuple-element.735) | copy-start | bytes 393220 | tf_op jit(solution)/shard_map/while
  130.9 5.4 %copy-start.3 = (bf16[16,4096]{1,0:T(8,128)(2,1)}, bf16[16,4096]{1,0:T(8,128)(2,1)S(1)}, u32[]{:S(2)}) copy-start(bf16[16,4096]{1,0:T(8,128)(2,1)S(1)} %get-tuple-element.738) | copy-start | bytes 393220 | tf_op jit(solution)/shard_map/while
  139.4 1.1 copy-start.2
  139.4 1.1 copy-start.4
  140.6 5.4 %copy-start.1 = (bf16[16,4096]{1,0:T(8,128)(2,1)}, bf16[16,4096]{1,0:T(8,128)(2,1)S(1)}, u32[]{:S(2)}) copy-start(bf16[16,4096]{1,0:T(8,128)(2,1)S(1)} %get-tuple-element.735) | copy-start | bytes 393220 | tf_op jit(solution)/shard_map/while
  140.6 5.4 %copy-start.3 = (bf16[16,4096]{1,0:T(8,128)(2,1)}, bf16[16,4096]{1,0:T(8,128)(2,1)S(1)}, u32[]{:S(2)}) copy-start(bf16[16,4096]{1,0:T(8,128)(2,1)S(1)} %get-tuple-element.738) | copy-start | bytes 393220 | tf_op jit(solution)/shard_map/while
  149.1 1.1 copy-start.2
  149.1 1.1 copy-start.4
  150.3 5.4 %copy-start.1 = (bf16[16,4096]{1,0:T(8,128)(2,1)}, bf16[16,4096]{1,0:T(8,128)(2,1)S(1)}, u32[]{:S(2)}) copy-start(bf16[16,4096]{1,0:T(8,128)(2,1)S(1)} %get-tuple-element.735) | copy-start | bytes 393220 | tf_op jit(solution)/shard_map/while
  150.3 5.4 %copy-start.3 = (bf16[16,4096]{1,0:T(8,128)(2,1)}, bf16[16,4096]{1,0:T(8,128)(2,1)S(1)}, u32[]{:S(2)}) copy-start(bf16[16,4096]{1,0:T(8,128)(2,1)S(1)} %get-tuple-element.738) | copy-start | bytes 393220 | tf_op jit(solution)/shard_map/while
  158.8 1.1 copy-start.2
  158.9 1.1 copy-start.4
  160.0 5.4 %copy-start.1 = (bf16[16,4096]{1,0:T(8,128)(2,1)}, bf16[16,4096]{1,0:T(8,128)(2,1)S(1)}, u32[]{:S(2)}) copy-start(bf16[16,4096]{1,0:T(8,128)(2,1)S(1)} %get-tuple-element.735) | copy-start | bytes 393220 | tf_op jit(solution)/shard_map/while
  160.0 5.4 %copy-start.3 = (bf16[16,4096]{1,0:T(8,128)(2,1)}, bf16[16,4096]{1,0:T(8,128)(2,1)S(1)}, u32[]{:S(2)}) copy-start(bf16[16,4096]{1,0:T(8,128)(2,1)S(1)} %get-tuple-element.738) | copy-start | bytes 393220 | tf_op jit(solution)/shard_map/while
  168.5 1.1 copy-start.2
  168.6 1.1 copy-start.4
  171.4 6.6 %collective-permute-start.4 = (f32[1,16,128]{2,1,0:T(8,128)S(1)}, f32[1,16,128]{2,1,0:T(8,128)S(1)}, u32[]{:S(2)}, u32[]{:S(2)}) collective-permute-start(f32[1,16,128]{2,1,0:T(8,128)S(1)} %get-tuple-element.409), channel_id=1, source_target_pairs={{0,1},{1,2},{2,3},{3,4},{4,5},{5,6},{6,7},{7,8},{8,9},{9,10},{10,1... | collective-permute-start | bytes 24584 | tf_op jit(solution)/shard_map/ppermute | solution.py:40
  174.1 8.9 %collective-permute-start.5 = (f32[1,16,128]{2,1,0:T(8,128)S(1)}, f32[1,16,128]{2,1,0:T(8,128)S(1)}, u32[]{:S(2)}, u32[]{:S(2)}) collective-permute-start(f32[1,16,128]{2,1,0:T(8,128)S(1)} %get-tuple-element.408), channel_id=1, source_target_pairs={{1,0},{2,1},{3,2},{4,3},{5,4},{6,5},{7,6},{8,7},{9,8},{10,9},{11,1... | collective-permute-start | bytes 24584 | tf_op jit(solution)/shard_map/ppermute | solution.py:42
where the time goes:
time: 187 us; the launch traced here: 185 us
  loops' own time  55.4 us (30%)
  local copies, waits for them, and re-layouts  44.6 us (24%)
  starting transfers between devices  23.1 us (12%)
  other arithmetic  17.3 us (9%)
  matrix products  15.9 us (9%)
  blocking collectives  13.3 us (7%)
  waiting for transfers between devices  11.8 us (6%)
  between operations  3.33 us (2%)
    another operation x1, loops' own time, shards(): lax.map(lambda slot_index: pool_domain(domain_of(slot_index)), slot_ids)  27.5 us
    another operation x1, loops' own time, shards(): lax.map(lambda item_pair: output_conv(domain_of(item_pair[0]), item_pair[...  27.4 us
    ppermute x3, starting transfers between devices, extended_2(): lax.ppermute(tail, axis, [(i, (i + 1) % count) for i in range(ends)])  14.5 us
    all_gather x1, blocking collectives, shards(): blocks = lax.all_gather(coarse, 'member', axis=1, tiled=True)  13.3 us
    ppermute x3, waiting for transfers between devices, extended_2(): lax.ppermute(head, axis, [((i + 1) % count, i) for i in range(ends)])  11.8 us
    ppermute x3, starting transfers between devices, extended_2(): lax.ppermute(head, axis, [((i + 1) % count, i) for i in range(ends)])  8.65 us
    dynamic_slice x12, local copies, waits for them, and re-layouts, shards(): lax.map(lambda slot_index: pool_domain(domain_of(slot_index)), slot_ids)  7.33 us
    transpose x6, local copies, waits for them, and re-layouts, output_conv(): jnp.einsum('rwc,cabv->abrwv', active, kernel, preferred_element_type=jnp....  6.67 us
  transfers between devices with their start and end apart: 6, of which 2 were waited for; matrix products, arithmetic and copies ran while one was open for 2% of the time, Pallas kernels for 0%

commit v1 on v0

v1 whole, which is shorter than its diff:
```python
import functools

import jax
import jax.numpy as jnp
import numpy as np
from jax import lax
from jax.experimental import pallas as pl
from jax.experimental.pallas import tpu as pltpu
from jax.sharding import PartitionSpec as P

VARS = 4
CCH = 12
CIN = 20
CH = 128
CH2 = 256
HEADS = 4
HEAD_DIM = 64
P_SIZE = 32
M = 16
W = 32
SLOTS = 6
FACTOR = 8
BLK_DEV = 8
MIX = 4
DOM = 64
TOKENS = 32
BR = 4
BW = 4
MEMBERS = 8

SIGMA_DATA = 0.5
NORM_EPS = 1e-06

F32 = jnp.float32
BF16 = jnp.bfloat16

IN_LANES = 2 * W * VARS
CELL = 64
STEM_LANES = (W + 2) * CELL
OWN_ROWS = SLOTS * P_SIZE
SIDE_ROWS = 64
OWN_TOKENS = OWN_ROWS // 8 * 4
SIDE_PATCHES = 4
PIECE = 160
CHUNKS = 9
HALF = W // 2
HALF_LANES = HALF * CH
TAP_LANES = (HALF + 2) * VARS
VMEM_LIMIT = 60 * 1024 * 1024


def interp_matrix(fine_count, coarse_count):
    position = (np.arange(fine_count) + 0.5) / FACTOR - 0.5
    position = np.clip(position, 0.0, coarse_count - 1.0)
    return np.maximum(0.0, 1.0 - np.abs(position[:, None] - np.arange(coarse_count)[None, :]))


def along_rows(rows, first, patches):
    row_map = interp_matrix(P_SIZE, BR)
    along = np.zeros((rows, 3, 2, patches, BR), np.float32)
    for row in range(rows):
        for tap in range(3):
            source = row + first + tap - 1
            if 0 <= source < patches * P_SIZE:
                along[row, tap, :, source // P_SIZE] = row_map[source % P_SIZE][None]
    return along.reshape(rows, 6 * patches * BR).astype(jnp.bfloat16)


@functools.cache
def tables():
    spread = np.zeros((3, 2, W, VARS, W + 2, CELL), np.float32)
    for tap in range(3):
        for array in range(2):
            for col in range(W):
                for var in range(VARS):
                    spread[tap, array, col, var, col + 1, tap * CIN + array * VARS + var] = 1.0
    spread = spread.reshape(3 * IN_LANES, STEM_LANES)
    spread = np.pad(spread, ((0, 0), (0, CHUNKS * 256 - STEM_LANES)))
    spread = spread.reshape(3 * IN_LANES, CHUNKS, 256).transpose(1, 0, 2)
    col_map = interp_matrix(W, BW)
    across = np.zeros((2, BW, CCH, W + 2, CELL), np.float32)
    taps = np.zeros((8, W + 2, CELL), np.float32)
    for tap in range(3):
        taps[tap, :, tap * CIN : (tap + 1) * CIN] = 1.0
        for channel in range(CCH):
            across[:, :, channel, 1 : W + 1, tap * CIN + 2 * VARS + channel] = col_map.T[None]
    across = np.concatenate([across.reshape(2 * BW * CCH, STEM_LANES), np.zeros((32, STEM_LANES))])
    place = np.zeros((3, 3, VARS, HALF, 256), np.float32)
    for cell in range(HALF):
        for row_tap in range(3):
            for col_tap in range(3):
                for var in range(VARS):
                    lane = row_tap * TAP_LANES + (cell + 2 - col_tap) * VARS + var
                    place[row_tap, col_tap, var, cell, lane] = 1.0
    place = place.reshape(36, HALF * 256)
    return (
        spread.astype(jnp.bfloat16),
        across.astype(jnp.bfloat16),
        taps.reshape(8, STEM_LANES).astype(np.float32),
        along_rows(OWN_ROWS, 0, SLOTS),
        along_rows(SIDE_ROWS, M, SIDE_PATCHES),
        place.astype(jnp.bfloat16),
    )


def silu(value):
    half = 0.5 * value
    return half + half * jnp.tanh(half)


def dot(left, right):
    return jnp.dot(left, right, preferred_element_type=F32)


def fetch(sems, pairs):
    copies = [pltpu.make_async_copy(a, b, sems.at[i]) for i, (a, b) in enumerate(pairs)]
    for copy in copies:
        copy.start()
    return copies


def mix_kernel(src, widx, table, coarse, copies_out, src_s, widx_s, table_s, blocks, sems):
    for copy in fetch(sems, [(src, src_s), (widx, widx_s), (table, table_s), (coarse, blocks)]):
        copy.wait()
    copies_out[...] = jnp.zeros_like(copies_out)
    for slot in range(SLOTS):
        total = jnp.zeros((1, 24), F32)
        for k in range(MIX):
            total = total + table_s[widx_s[k, slot]] * blocks[pl.ds(src_s[k, slot], 1)]
        for member in range(MEMBERS):
            copies_out[member, slot : slot + 1, 0:24] = total


def prepare_kernel(
    scalars, noisy, mean_field, w_stem, noise_embed, w_out, spread, place,
    held_out, first_out, second_out, own_out, levels_out, stem_out, right_out,
    scalars_s, noisy_v, mean_v, w_stem_v, embed_v, w_out_v, spread_v, place_v,
    state_rows, mean_rows, stem_left, stem_f32, sems,
):
    copies = fetch(
        sems,
        [
            (scalars, scalars_s),
            (noise_embed, embed_v),
            (noisy, noisy_v),
            (mean_field, mean_v),
            (w_stem, w_stem_v),
            (w_out, w_out_v),
            (place, place_v),
        ]
        + [(spread.at[chunk], spread_v.at[chunk]) for chunk in range(CHUNKS)],
    )
    for copy in copies[0:4]:
        copy.wait()
    held = scalars_s[2].astype(jnp.int32)
    held_out[0] = held
    level = jnp.full((1, 128), scalars_s[0], F32)
    variance = level * level + SIGMA_DATA * SIGMA_DATA
    c_in = lax.rsqrt(variance)
    levels_out[0:1] = jnp.log(level) * 0.25 * embed_v[...]
    levels_out[1:2] = SIGMA_DATA * SIGMA_DATA / variance
    levels_out[2:3] = level * SIGMA_DATA * lax.rsqrt(variance)
    levels_out[3:4] = jnp.full((1, 128), scalars_s[1], F32) / level - 1.0
    levels_out[4:5] = c_in
    even = lax.rem(lax.axis_index("space"), 2) == 0
    c_in = c_in.reshape(1, 1, 128)
    for out, to_right in ((first_out, even), (second_out, jnp.logical_not(even))):
        start = jnp.where(to_right, held - 2, 0)
        out[0:64] = (c_in * noisy_v[pl.ds(start, 2)]).astype(BF16).reshape(64, 128)
        out[64:128] = mean_v[pl.ds(start, 2)].astype(BF16).reshape(64, 128)
    for rows, value in (
        (state_rows, (c_in * noisy_v[...]).reshape(OWN_ROWS, 128)),
        (mean_rows, mean_v[...].reshape(OWN_ROWS, 128)),
    ):
        rows[0:8] = jnp.zeros((8, 128), F32)
        rows[8 : 8 + OWN_ROWS] = value
        rows[8 + OWN_ROWS :] = jnp.zeros((8, 128), F32)
    for tap in range(3):
        for array, rows in enumerate((state_rows, mean_rows)):
            lane = tap * IN_LANES + array * 128
            stem_left[:, lane : lane + 128] = rows[7 + tap : 7 + tap + OWN_ROWS].astype(BF16)

    for copy in copies[4:7]:
        copy.wait()
    stem_f32[...] = jnp.zeros_like(stem_f32)
    stem_taps = w_stem_v[...].astype(F32)
    for cell in range(4):
        for target in range(2):
            col_tap = cell - target
            if 0 <= col_tap < 3:
                for row_tap in range(3):
                    at = (3 * row_tap + col_tap) * CIN
                    to = cell * CELL + row_tap * CIN
                    stem_f32[to : to + CIN, target * CH : (target + 1) * CH] = stem_taps[at : at + CIN]
    stem_out[...] = stem_f32[...].astype(BF16)
    for cell in range(HALF):
        right_out[cell * CH : (cell + 1) * CH] = dot(
            w_out_v[...], place_v[:, cell * 256 : (cell + 1) * 256]
        ).astype(BF16)
    for chunk in range(CHUNKS):
        copies[7 + chunk].wait()
        lanes = min(256, STEM_LANES - chunk * 256)
        own_out[:, chunk * 256 : chunk * 256 + lanes] = dot(
            stem_left[...], spread_v[chunk, :, 0:lanes]
        ).astype(BF16)


def pack_kernel(held_in, cells, first_in, second_in, first_out, second_out, mix_out):
    held = held_in[0]
    for member in range(MEMBERS):
        mix_out[pl.ds(member, SLOTS, stride=MEMBERS)] = cells[member, 0:SLOTS]
    even = lax.rem(lax.axis_index("space"), 2) == 0
    for out, given, to_right in (
        (first_out, first_in, even),
        (second_out, second_in, jnp.logical_not(even)),
    ):
        start = pl.multiple_of(jnp.where(to_right, held - 2, 0) * MEMBERS, MEMBERS)
        out[0:128] = given[0:128]
        mixed = mix_out[pl.ds(start, 16)]
        high = mixed.astype(BF16)
        out[128:144] = high
        out[144:160] = (mixed - high.astype(F32)).astype(BF16)


def conditioning(mixes, count, across, taps):
    pair = mixes[pl.ds(0, count, stride=2)] + pltpu.roll(mixes[pl.ds(1, count, stride=2)], 24, 1)
    pair_high = pair.astype(BF16).astype(F32)
    both = pair_high + pltpu.roll(pair - pair_high, 48, 1)
    wide = dot(both.astype(BF16), across[...])
    wide_high = wide.astype(BF16).astype(F32)
    return wide_high, wide - wide_high


def by_tap(wide_high, wide_low, taps):
    parts = []
    for tap in range(3):
        parts += [wide_high * taps[tap : tap + 1], wide_low * taps[tap : tap + 1]]
    return jnp.concatenate(parts, axis=0).astype(BF16)


def stem(stem_in, stem_right, shift, features, store_pooled):
    rows = features.shape[0]
    for block_col in range(4):
        summed = jnp.zeros((rows, CH), F32)
        for cell_pair in range(4):
            number = block_col * 4 + cell_pair
            raw = dot(stem_in[:, number * 128 : number * 128 + 256], stem_right[...])
            for half in range(2):
                feature = silu(raw[:, half * CH : (half + 1) * CH] + shift).astype(BF16)
                lane = number * 256 + half * CH
                features[:, lane : lane + CH] = feature
                summed = summed + feature.astype(F32)
        store_pooled(block_col, jnp.sum(summed.reshape(rows // 8, 8, CH), axis=1) * (1.0 / 64.0))


def bottleneck(pooled, starts, weights, copies):
    w_down, w_query, w_key, w_value, w_attn_out, w_up = weights
    for copy in copies:
        copy.wait()
    zeta = silu(dot(pooled.astype(BF16), w_down[...]))
    scale = lax.rsqrt(jnp.mean(zeta * zeta, axis=-1, keepdims=True) + NORM_EPS)
    normed = (zeta * scale).astype(BF16)
    query = dot(normed, w_query[...]).astype(BF16)
    keyed = dot(normed, w_key[...]).astype(BF16)
    valued = dot(normed, w_value[...]).astype(BF16)
    head_of_row = lax.broadcasted_iota(jnp.int32, (HEADS * TOKENS, CH2), 0) // TOKENS
    head_of_channel = lax.broadcasted_iota(jnp.int32, (HEADS * TOKENS, CH2), 1) // HEAD_DIM
    own_head = (head_of_row == head_of_channel).astype(F32).astype(BF16)
    head_of_lane = lax.broadcasted_iota(jnp.int32, (TOKENS, HEADS * TOKENS), 1) // TOKENS
    mixed_heads = []
    residual = []
    for start in starts:
        rows = slice(start, start + TOKENS)
        keys = jnp.concatenate([keyed[rows]] * HEADS, axis=0) * own_head
        values = jnp.concatenate([valued[rows]] * HEADS, axis=0) * own_head
        scores = lax.dot_general(
            query[rows], keys, (((1,), (1,)), ((), ())), preferred_element_type=F32
        ) * (HEAD_DIM**-0.5)
        top = jnp.zeros_like(scores)
        for head in range(HEADS):
            inside = head_of_lane == head
            largest = jnp.max(jnp.where(inside, scores, -jnp.inf), axis=1, keepdims=True)
            top = jnp.where(inside, largest, top)
        weight = jnp.exp(scores - top).astype(BF16)
        mixed_heads.append((dot(weight, values) / dot(weight, own_head)).astype(BF16))
        residual.append(zeta[rows])
    attended = jnp.concatenate(mixed_heads, axis=0)
    resid = (jnp.concatenate(residual, axis=0) + dot(attended, w_attn_out[...])).astype(BF16)
    return dot(resid, w_up[...])


def activate(number, sources, first, lifted, active, base):
    half_rows = active.shape[0] // 2
    count = sum(rows for _, _, rows in sources) // 8
    for block_col in range(4):
        raised = lifted[pl.ds(number * TOKENS + first * 4 + block_col, count, stride=4)].reshape(
            count, 1, CH
        )
        done = 0
        for ref, start, rows in sources:
            part = raised[done // 8 : (done + rows) // 8]
            for cell in range(block_col * 8, block_col * 8 + 8):
                given = ref[pl.ds(start, rows), cell * CH : (cell + 1) * CH]
                value = silu(given.astype(F32).reshape(rows // 8, 8, CH) + part)
                to = base + done + cell // HALF * half_rows
                lane = cell % HALF * CH
                active[to : to + rows, lane : lane + CH] = value.reshape(rows, CH).astype(BF16)
            done += rows


def predict(halves, base, first, last, padded):
    rows = (last - first) * 8
    half_rows = halves.shape[0] // 2
    left = halves[base : base + rows]
    right = halves[half_rows + base : half_rows + base + rows]
    lane = lax.broadcasted_iota(jnp.int32, (rows, 128), 1)
    for tap in range(3):
        from_left = pltpu.roll(left, (-4 - TAP_LANES * tap) % 256, 1)[:, 0:128]
        from_right = pltpu.roll(right, (60 - TAP_LANES * tap) % 256, 1)[:, 0:128]
        padded[8 : 8 + rows, tap * 128 : (tap + 1) * 128] = jnp.where(
            lane < 68, from_left, 0.0
        ) + jnp.where(lane >= 60, from_right, 0.0)
    zero = jnp.zeros((8, 384), F32)
    padded[0:8] = zero
    padded[8 + rows : 16 + rows] = zero
    field = (
        padded[7 : 7 + rows, 0:128] + padded[8 : 8 + rows, 128:256] + padded[9 : 9 + rows, 256:384]
    )
    row = lax.broadcasted_iota(jnp.int32, (rows, 128), 0) + first * 8
    return field * jnp.minimum(row + 1, DOM - row).astype(F32)


def inner_kernel(
    held_in, *refs,
):
    inputs, (features_out, pooled_out, total), scratch = refs[:14], refs[14:17], refs[17:]
    locals_, (cond_right, stem_in, features, pooled, lifted, active, halves, padded, sems) = (
        scratch[:14],
        scratch[14:],
    )
    mixes, across, taps, along, own_in, stem_right, levels = locals_[:7]
    weights, out_right = locals_[7:13], locals_[13]
    copies = fetch(sems, list(zip(inputs, locals_)))
    held = held_in[0]
    for copy in copies[0:3]:
        copy.wait()
    wide_high, wide_low = conditioning(mixes, 24, across, taps)
    cond_right[...] = by_tap(wide_high, wide_low, taps)
    for copy in copies[3:7]:
        copy.wait()
    for start in range(0, STEM_LANES, 256):
        stop = min(start + 256, STEM_LANES)
        stem_in[:, start:stop] = own_in[:, start:stop] + dot(
            along[...], cond_right[:, start:stop]
        ).astype(BF16)
    pooled[0:8] = jnp.zeros((8, CH), F32)
    pooled[8 + OWN_TOKENS :] = jnp.zeros((8, CH), F32)

    def store_pooled(block_col, value):
        pooled[pl.ds(8 + block_col, OWN_ROWS // 8, stride=4)] = value

    stem(stem_in, stem_right, levels[0:1], features, store_pooled)
    out_copy = pltpu.make_async_copy(features, features_out, sems.at[14])
    out_copy.start()
    pooled_out[...] = pooled[8 : 8 + OWN_TOKENS]
    lifted[...] = bottleneck(
        pooled[...], [16 * patch for patch in range(1, SLOTS - 1)], weights, copies[7:13]
    )
    for patch in range(1, SLOTS - 1):
        activate(
            patch - 1, [(features, P_SIZE * patch - M, DOM)], 0, lifted, active, DOM * (patch - 1)
        )
    copies[13].wait()
    halves[...] = dot(active[...], out_right[...])
    total[...] = jnp.zeros_like(total)
    for patch in range(1, SLOTS - 1):
        span = slice(P_SIZE * patch - M, P_SIZE * patch - M + DOM)
        field = predict(halves, DOM * (patch - 1), 0, 8, padded.at[patch % 2])
        total[span] = total[span] + jnp.where(patch <= held - 2, field, 0.0)
    out_copy.wait()


def edge_kernel(
    held_in, *refs,
):
    inputs, (denoised_out, next_out), scratch = refs[:21], refs[21:23], refs[23:]
    locals_, rest = scratch[:21], scratch[21:]
    noisy, mean_field, first_in, second_in, mix_own, levels, across, taps, along = locals_[:9]
    spread, stem_right, pooled_own, features = locals_[9:13]
    weights, out_right, total = locals_[13:19], locals_[19], locals_[20]
    (
        state_rows, mean_rows, mixes, cond_right, stem_left, stem_in, ends, pooled, lifted, active,
        halves, padded, sems,
    ) = rest
    pairs = []
    for number, (given, held_here) in enumerate(zip(inputs, locals_)):
        if number == 9:
            pairs += [(given.at[chunk], held_here.at[chunk]) for chunk in range(CHUNKS)]
        else:
            pairs.append((given, held_here))
    copies = fetch(sems, pairs)
    chunk_copies = copies[9 : 9 + CHUNKS]
    copies = copies[:9] + [None] + copies[9 + CHUNKS :]
    held = held_in[0]
    position = lax.axis_index("space")
    even = lax.rem(position, 2) == 0
    has_left = position > 0
    has_right = position < lax.axis_size("space") - 1
    for copy in copies[0:9]:
        copy.wait()
    c_in = levels[4:5].reshape(1, 1, 128)

    state_rows[0, 64:96] = (c_in * noisy[0:1]).reshape(P_SIZE, 128)
    mean_rows[0, 64:96] = mean_field[0]
    state_rows[1, 0:32] = (c_in * noisy[pl.ds(held - 1, 1)]).reshape(P_SIZE, 128)
    mean_rows[1, 0:32] = mean_field[pl.ds(held - 1, 1)].reshape(P_SIZE, 128)
    mixes[16:24] = mix_own[0:8]
    mixes[24:32] = jnp.zeros((8, 128), F32)
    mixes[32:40] = mix_own[pl.ds(pl.multiple_of(8 * held - 8, 8), 8)]
    mixes[56:64] = jnp.zeros((8, 128), F32)

    def take(piece, side, rows_at, mixes_at):
        state_rows[side, rows_at : rows_at + 64] = piece[0:64].astype(F32)
        mean_rows[side, rows_at : rows_at + 64] = piece[64:128].astype(F32)
        mixes[mixes_at : mixes_at + 16] = piece[128:144].astype(F32) + piece[144:160].astype(F32)

    @pl.when(even)
    def _():
        take(second_in, 0, 0, 0)
        take(first_in, 1, 32, 40)

    @pl.when(jnp.logical_not(even))
    def _():
        take(first_in, 0, 0, 0)
        take(second_in, 1, 32, 40)

    wide_high, wide_low = conditioning(mixes, 32, across, taps)
    for side in range(2):
        span = slice(16 * side, 16 * side + 16)
        cond_right[side] = by_tap(wide_high[span], wide_low[span], taps)
        for tap in range(3):
            for array, rows in enumerate((state_rows, mean_rows)):
                lane = tap * IN_LANES + array * 128
                stem_left[SIDE_ROWS * side : SIDE_ROWS * (side + 1), lane : lane + 128] = rows[
                    side, 15 + tap : 15 + tap + SIDE_ROWS
                ].astype(BF16)
    for chunk in range(CHUNKS):
        start = chunk * 256
        stop = min(start + 256, STEM_LANES)
        chunk_copies[chunk].wait()
        given = dot(stem_left[...], spread[chunk, :, 0 : stop - start])
        for side in range(2):
            span = slice(SIDE_ROWS * side, SIDE_ROWS * (side + 1))
            stem_in[span, start:stop] = (
                given[span] + dot(along[...], cond_right[side, :, start:stop])
            ).astype(BF16)

    def store_pooled(block_col, value):
        pooled[pl.ds(block_col, 8, stride=4)] = value[0:8]
        pooled[pl.ds(64 + block_col, 8, stride=4)] = value[8:16]

    for copy in copies[10:13]:
        copy.wait()
    stem(stem_in, stem_right, levels[0:1], ends, store_pooled)
    pooled[32:48] = pooled_own[8:24]
    pooled[48:64] = pooled_own[pl.ds(pl.multiple_of(16 * held - 24, 8), 16)]

    @pl.when(jnp.logical_not(has_left))
    def _():
        ends[0:48] = jnp.zeros((48, W * CH), BF16)
        pooled[0:24] = jnp.zeros((24, CH), F32)

    @pl.when(jnp.logical_not(has_right))
    def _():
        ends[80:128] = jnp.zeros((48, W * CH), BF16)
        pooled[72:96] = jnp.zeros((24, CH), F32)

    lifted[...] = bottleneck(pooled[...], [0, 16, 48, 64], weights, copies[13:19])
    near = pl.multiple_of(P_SIZE * held - 48, 16)
    activate(0, [(ends, 32, 32)], 4, lifted, active, 0)
    activate(1, [(ends, 32, 32), (features, 16, 32)], 0, lifted, active, 32)
    activate(2, [(features, near, 32), (ends, 64, 32)], 0, lifted, active, 96)
    activate(3, [(ends, 64, 32)], 0, lifted, active, 160)
    copies[19].wait()
    halves[...] = dot(active[...], out_right[...])
    copies[20].wait()
    field = predict(halves, 0, 4, 8, padded.at[0])
    total[0:M] = total[0:M] + jnp.where(has_left, field[16:32], 0.0)
    field = predict(halves, 32, 0, 8, padded.at[1])
    total[0:48] = total[0:48] + field[16:64]
    field = predict(halves, 96, 0, 8, padded.at[0])
    total[pl.ds(near, 48)] = total[pl.ds(near, 48)] + field[0:48]
    field = predict(halves, 160, 0, 4, padded.at[1])
    last = pl.multiple_of(P_SIZE * held - M, 16)
    total[pl.ds(last, M)] = total[pl.ds(last, M)] + jnp.where(has_right, field[0:16], 0.0)

    slot = lax.broadcasted_iota(jnp.int32, (SLOTS, P_SIZE, 128), 0)
    row = lax.broadcasted_iota(jnp.int32, (SLOTS, P_SIZE, 128), 1)
    norm = jnp.full((SLOTS, P_SIZE, 128), 33, jnp.int32)
    no_left = jnp.logical_and(jnp.logical_not(has_left), jnp.logical_and(slot == 0, row < M))
    no_right = jnp.logical_and(
        jnp.logical_not(has_right), jnp.logical_and(slot == held - 1, row >= M)
    )
    norm = jnp.where(no_left, 17 + row, norm)
    norm = jnp.where(no_right, 48 - row, norm)
    blended = total[...].reshape(SLOTS, P_SIZE, 128) / norm.astype(F32)
    state = noisy[...]
    denoised = levels[1:2].reshape(1, 1, 128) * state + levels[2:3].reshape(1, 1, 128) * blended
    stepped = state + levels[3:4].reshape(1, 1, 128) * (state - denoised)
    live = slot < held
    denoised_out[...] = jnp.where(live, denoised, 0.0)
    next_out[...] = jnp.where(live, stepped, 0.0)


def shards(
    noisy,
    mean_field,
    coarse,
    counts,
    src,
    widx,
    table,
    sigma,
    sigma_next,
    w_stem,
    noise_embed,
    w_down,
    w_query,
    w_key,
    w_value,
    w_attn_out,
    w_up,
    w_out,
):
    owners = lax.axis_size("space")
    smem = pl.BlockSpec(memory_space=pltpu.SMEM)
    vmem = pl.BlockSpec(memory_space=pltpu.VMEM)
    hbm = pl.BlockSpec(memory_space=pltpu.HBM)
    limit = pltpu.CompilerParams(vmem_limit_bytes=24 * 1024 * 1024)
    limit = pltpu.CompilerParams(vmem_limit_bytes=VMEM_LIMIT)
    state = noisy[0]
    copies = pl.pallas_call(
        mix_kernel,
        out_shape=jax.ShapeDtypeStruct((MEMBERS, 8, 128), F32),
        in_specs=[hbm] * 4,
        out_specs=vmem,
        scratch_shapes=[
            pltpu.SMEM((MIX, SLOTS), jnp.int32),
            pltpu.SMEM((MIX, SLOTS), jnp.int32),
            pltpu.SMEM((16,), F32),
            pltpu.VMEM((BLK_DEV, 24), F32),
            pltpu.SemaphoreType.DMA((4,)),
        ],
        compiler_params=limit,
        name="mix",
    )(src.T, widx.T, table, coarse)
    cells = lax.all_to_all(copies, "member", 0, 0, tiled=True)

    spread, across, taps, along, along_side, place = (jnp.asarray(array) for array in tables())
    scalars = jnp.concatenate([sigma, sigma_next, counts.astype(F32)])
    embed = noise_embed.reshape(1, CH)
    held, first, second, own_in, levels, stem_right, out_right = pl.pallas_call(
        prepare_kernel,
        out_shape=(
            jax.ShapeDtypeStruct((8,), jnp.int32),
            jax.ShapeDtypeStruct((PIECE, 128), BF16),
            jax.ShapeDtypeStruct((PIECE, 128), BF16),
            jax.ShapeDtypeStruct((OWN_ROWS, STEM_LANES), BF16),
            jax.ShapeDtypeStruct((8, 128), F32),
            jax.ShapeDtypeStruct((CH2, CH2), BF16),
            jax.ShapeDtypeStruct((HALF_LANES, 256), BF16),
        ),
        in_specs=[hbm] * 8,
        out_specs=[smem] + [vmem] * 6,
        scratch_shapes=[
            pltpu.SMEM((3,), F32),
            pltpu.VMEM((SLOTS, P_SIZE, 128), F32),
            pltpu.VMEM((SLOTS, P_SIZE, 128), F32),
            pltpu.VMEM(w_stem.shape, BF16),
            pltpu.VMEM((1, CH), F32),
            pltpu.VMEM(w_out.shape, BF16),
            pltpu.VMEM(spread.shape, BF16),
            pltpu.VMEM(place.shape, BF16),
            pltpu.VMEM((OWN_ROWS + 16, 128), F32),
            pltpu.VMEM((OWN_ROWS + 16, 128), F32),
            pltpu.VMEM((OWN_ROWS, 3 * IN_LANES), BF16),
            pltpu.VMEM((256, 256), F32),
            pltpu.SemaphoreType.DMA((7 + CHUNKS,)),
        ],
        compiler_params=limit,
        cost_estimate=pl.CostEstimate(flops=10**9, bytes_accessed=8 * 10**6, transcendentals=0),
        name="prepare",
    )(scalars, state, mean_field, w_stem, embed, w_out, spread, place)

    first, second, mix_own = pl.pallas_call(
        pack_kernel,
        out_shape=(
            jax.ShapeDtypeStruct((PIECE, 128), BF16),
            jax.ShapeDtypeStruct((PIECE, 128), BF16),
            jax.ShapeDtypeStruct((SLOTS * MEMBERS, 128), F32),
        ),
        in_specs=[smem] + [vmem] * 3,
        out_specs=(vmem, vmem, vmem),
        compiler_params=limit,
        name="pack",
    )(held, cells, first, second)
    pairs = [(i, i ^ 1) for i in range(owners)]
    others = []
    for i in range(1, owners - 1, 2):
        others += [(i, i + 1), (i + 1, i)]
    first = lax.ppermute(first, "space", pairs)
    second = lax.ppermute(second, "space", others)

    weights = [w_down, w_query, w_key, w_value, w_attn_out, w_up]
    given = [mix_own, across, taps, along, own_in, stem_right, levels, *weights, out_right]
    features, pooled, total = pl.pallas_call(
        inner_kernel,
        out_shape=(
            jax.ShapeDtypeStruct((OWN_ROWS, W * CH), BF16),
            jax.ShapeDtypeStruct((OWN_TOKENS, CH), F32),
            jax.ShapeDtypeStruct((OWN_ROWS, 128), F32),
        ),
        in_specs=[smem] + [hbm] * len(given),
        out_specs=(hbm, vmem, vmem),
        scratch_shapes=[pltpu.VMEM(array.shape, array.dtype) for array in given]
        + [
            pltpu.VMEM((144, STEM_LANES), BF16),
            pltpu.VMEM((OWN_ROWS, STEM_LANES), BF16),
            pltpu.VMEM((OWN_ROWS, W * CH), BF16),
            pltpu.VMEM((OWN_TOKENS + 16, CH), F32),
            pltpu.VMEM((4 * TOKENS, CH), F32),
            pltpu.VMEM((2 * 4 * DOM, HALF_LANES), BF16),
            pltpu.VMEM((2 * 4 * DOM, 256), F32),
            pltpu.VMEM((2, 80, 384), F32),
            pltpu.SemaphoreType.DMA((15,)),
        ],
        compiler_params=limit,
        cost_estimate=pl.CostEstimate(flops=10**9, bytes_accessed=10**7, transcendentals=2 * 10**6),
        name="inner",
    )(held, *given)

    given = [state, mean_field, first, second, mix_own, levels, across, taps, along_side, spread]
    given += [stem_right, pooled, features, *weights, out_right, total]
    denoised, stepped = pl.pallas_call(
        edge_kernel,
        out_shape=(
            jax.ShapeDtypeStruct((SLOTS, P_SIZE, 128), F32),
            jax.ShapeDtypeStruct((SLOTS, P_SIZE, 128), F32),
        ),
        in_specs=[smem] + [hbm] * len(given),
        out_specs=(vmem, vmem),
        scratch_shapes=[pltpu.VMEM(array.shape, array.dtype) for array in given]
        + [
            pltpu.VMEM((2, 96, 128), F32),
            pltpu.VMEM((2, 96, 128), F32),
            pltpu.VMEM((64, 128), F32),
            pltpu.VMEM((2, 96, STEM_LANES), BF16),
            pltpu.VMEM((2 * SIDE_ROWS, 3 * IN_LANES), BF16),
            pltpu.VMEM((2 * SIDE_ROWS, STEM_LANES), BF16),
            pltpu.VMEM((2 * SIDE_ROWS, W * CH), BF16),
            pltpu.VMEM((96, CH), F32),
            pltpu.VMEM((4 * TOKENS, CH), F32),
            pltpu.VMEM((2 * 192, HALF_LANES), BF16),
            pltpu.VMEM((2 * 192, 256), F32),
            pltpu.VMEM((2, 80, 384), F32),
            pltpu.SemaphoreType.DMA((len(given) + CHUNKS,)),
        ],
        compiler_params=limit,
        cost_estimate=pl.CostEstimate(flops=10**9, bytes_accessed=10**7, transcendentals=2 * 10**6),
        name="edge",
    )(held, *given)
    return denoised[None], stepped[None]


def solution(mesh):
    placed = (
        P("member", "space", None, None),
        P("space", None, None),
        P("space", "member"),
        P("space"),
        P("space", None),
        P("space", None),
        P(),
        P("member"),
        P("member"),
        P(),
        P(),
        P(),
        P(),
        P(),
        P(),
        P(),
        P(),
        P(),
    )
    return jax.shard_map(
        shards,
        mesh=mesh,
        in_specs=placed,
        out_specs=(P("member", "space", None, None), P("member", "space", None, None)),
        check_vma=False,
    )
```

time: 187 us -> 43.2 us (0.23)
  the two profiles are of different devices: /device:TPU:120 before, /device:TPU:122 now
where the time goes in v1:
time: 43.2 us; the launch traced here: 42.9 us
  Pallas kernels  25.9 us (60%)
  starting transfers between devices  11.1 us (26%)
  between operations  2.66 us (6%)
  local copies, waits for them, and re-layouts  2.62 us (6%)
  other arithmetic  0.55 us (1%)
    pallas_call x1, Pallas kernels, shards(): pl.pallas_call(edge_kernel, out_shape=(jax.ShapeDtypeStruct((SLOTS, P_SIZ...  9.67 us
    pallas_call x1, Pallas kernels, shards(): pl.pallas_call(inner_kernel, out_shape=(jax.ShapeDtypeStruct((OWN_ROWS, W...  7.87 us
    ppermute x1, starting transfers between devices, shards(): second = lax.ppermute(second, 'space', others)  5.52 us
    pallas_call x1, Pallas kernels, shards(): pl.pallas_call(prepare_kernel, out_shape=(jax.ShapeDtypeStruct((8,), jnp....  5.49 us
    all_to_all x1, starting transfers between devices, shards(): cells = lax.all_to_all(copies, 'member', 0, 0, tiled=True)  4.84 us
    unnamed x7, local copies, waits for them, and re-layouts  2.62 us
    pallas_call x1, Pallas kernels, shards(): pl.pallas_call(pack_kernel, out_shape=(jax.ShapeDtypeStruct((PIECE, 128),...  1.49 us
    pallas_call x1, Pallas kernels, shards(): pl.pallas_call(mix_kernel, out_shape=jax.ShapeDtypeStruct((MEMBERS, 8, 12...  1.42 us
  transfers between devices with their start and end apart: 3, of which 0 were waited for; matrix products, arithmetic and copies ran while one was open for 5% of the time, Pallas kernels for 31%

profile of v1, /device:TPU:122, one launch (start us, length us, event | category | flops | bytes accessed | tf_op | source)
XLA Modules:
  0.0 42.9 jit_solution(18262697369947551270)
XLA Ops:
  0.6 1.4 %mix.1 = f32[8,8,128]{2,1,0:T(8,128)} custom-call(s32[4,6]{1,0:T(4,128)} %bitcast.8, s32[4,6]{1,0:T(4,128)} %bitcast.9, f32[16]{0:T(128)} %table.1, f32[8,24]{1,0:T(8,128)} %coarse.1), custom_call_target="tpu_custom_call" | custom-call | tf_op jit(solution)/shard_map/mix/pallas_call | solution.py:542
  2.1 4.8 %all-to-all-start = ((f32[8,8,128]{2,1,0:T(8,128)}), f32[8,8,128]{2,1,0:T(8,128)S(1)}, u32[]{:S(2)}, u32[]{:S(2)}) async-start(f32[8,8,128]{2,1,0:T(8,128)} %mix.1), calls=%async_computation | async-start | bytes 65536 | tf_op jit(solution)/shard_map/all_to_all | solution.py:557
  8.8 1.4 %copy.26.w_out = bf16[128,36]{1,0:T(8,128)(2,1)} copy(bf16[128,36]{0,1:T(8,128)(2,1)} %param.41) | data formatting | bytes 18432 | tf_op args[17]
  10.3 0.6 %pad_maximum_fusion.scalars = f32[3]{0:T(128)} fusion(f32[1]{0:T(128)S(6)} %convert_element_type.3, f32[1]{0:T(128)S(6)} %copy.29, f32[1]{0:T(128)S(6)} %copy.28), kind=kLoop, calls=%fused_computation | loop fusion | flops 6 | bytes 24 | tf_op jit(solution)/shard_map/concatenate | solution.py:560
  10.8 5.5 %prepare.1 = (s32[8]{0:T(128)}, bf16[160,128]{1,0:T(8,128)(2,1)}, bf16[160,128]{1,0:T(8,128)(2,1)}, bf16[192,2176]{1,0:T(8,128)(2,1)}, f32[8,128]{1,0:T(8,128)},...) custom-call(f32[3]{0:T(128)} %pad_maximum_fusion.scalars, f32[6,32,128]{2,1,0:T(8,128)} %bitcast.6, ...), custom_call_target="tpu_custom_call" | custom-call | flops 1000000000 | bytes 8000000 | tf_op jit(solution)/shard_map/prepare/pallas_call | solution.py:562
  16.3 0.0 all-to-all-done.cells
  16.3 0.0 copy-start
  16.3 0.6 %copy-done = f32[8,8,128]{2,1,0:T(8,128)} copy-done((f32[8,8,128]{2,1,0:T(8,128)}, f32[8,8,128]{2,1,0:T(8,128)S(1)}, u32[]{:S(2)}) %copy-start) | copy-done | bytes 32792
  16.9 1.5 %pack.1 = (bf16[160,128]{1,0:T(8,128)(2,1)}, bf16[160,128]{1,0:T(8,128)(2,1)}, f32[48,128]{1,0:T(8,128)}) custom-call(s32[8]{0:T(128)} %get-tuple-element.17.held_in, f32[8,8,128]{2,1,0:T(8,128)} %copy-done, bf16[160,128]{1,0:T(8,128)(2,1)} %get-tuple-element.18.first_in, bf16[160,128]{1,0:T(8,128)(2,1)} %get-tuple-element.19.second_in), custom_call_target="tpu_custom_call" | custom-call | tf_op jit(solution)/shard_map/pack/pallas_call | solution.py:595
  18.4 0.7 %collective-permute-start = (bf16[160,128]{1,0:T(8,128)(2,1)}, bf16[160,128]{1,0:T(8,128)(2,1)S(1)}, u32[]{:S(2)}, u32[]{:S(2)}) collective-permute-start(bf16[160,128]{1,0:T(8,128)(2,1)} %get-tuple-element.20), channel_id=1, source_target_pairs={{0,1},{1,0},{2,3},{3,2},{4,5},{5,4},{6,7},{7,6},{8,9},{9,8},{10,11... | collective-permute-start | bytes 122888 | tf_op jit(solution)/shard_map/ppermute | solution.py:611
  19.2 5.5 %collective-permute-start.1 = (bf16[160,128]{1,0:T(8,128)(2,1)}, bf16[160,128]{1,0:T(8,128)(2,1)S(1)}, u32[]{:S(2)}, u32[]{:S(2)}) collective-permute-start(bf16[160,128]{1,0:T(8,128)(2,1)} %get-tuple-element.21), channel_id=1, source_target_pairs={{1,2},{2,1},{3,4},{4,3},{5,6},{6,5},{7,8},{8,7},{9,10},{10,9},{11,... | collective-permute-start | bytes 122888 | tf_op jit(solution)/shard_map/ppermute | solution.py:612
  24.7 7.9 %inner.1 = (bf16[192,4096]{1,0:T(8,128)(2,1)}, f32[96,128]{1,0:T(8,128)}, f32[192,128]{1,0:T(8,128)}) custom-call(s32[8]{0:T(128)} %get-tuple-element.17.held_in, f32[48,128]{1,0:T(8,128)} %get-tuple-element.22.refs_0_.refs_4_, bf16[128,2176]{1,0:T(8,128)(2,1)} %constant.13.clone.refs_1_.refs_6_, f32[8,2176]{1,0:T(8,128)} %constant.14.clone.refs_2_.refs_7_, ...), custom_call_target="tpu_custom_call" | custom-call | flops 1000000000 | bytes 10000000 | tf_op jit(solution)/shard_map/inner/pallas_call | solution.py:616
  32.6 0.0 collective-permute-done.refs_2_
  32.6 0.0 copy-start.1
  32.6 0.0 collective-permute-done.1.refs_3_
  32.6 0.0 copy-start.2
  32.6 0.6 %copy-done.1 = bf16[160,128]{1,0:T(8,128)(2,1)} copy-done((bf16[160,128]{1,0:T(8,128)(2,1)}, bf16[160,128]{1,0:T(8,128)(2,1)S(1)}, u32[]{:S(2)}) %copy-start.1) | copy-done | bytes 40984
  33.2 0.0 copy-done.2
  33.2 9.7 %edge.1 = (f32[6,32,128]{2,1,0:T(8,128)}, f32[6,32,128]{2,1,0:T(8,128)}) custom-call(s32[8]{0:T(128)} %get-tuple-element.17.held_in, f32[6,32,128]{2,1,0:T(8,128)} %bitcast.7, f32[6,32,128]{2,1,0:T(8,128)} %refs_1_.2, bf16[160,128]{1,0:T(8,128)(2,1)} %copy-done.1, bf16[160,128]{1,0:T(8,128)(2,1)} %copy-done.2, f32[48,128]{1,0:T(8,128)} %get-tuple-element.22.refs_0_.refs_4_, ...), custom_call_target="tpu_custom_call" | custom-call | flops 1000000000 | bytes 10000000 | tf_op jit(solution)/shard_map/edge/pallas_call | solution.py:644
Async XLA Ops:
  2.1 14.3 %all-to-all-start = ((f32[8,8,128]{2,1,0:T(8,128)}), f32[8,8,128]{2,1,0:T(8,128)S(1)}, u32[]{:S(2)}, u32[]{:S(2)}) async-start(f32[8,8,128]{2,1,0:T(8,128)} %mix.1), calls=%async_computation | async-start | bytes 65536 | tf_op jit(solution)/shard_map/all_to_all | solution.py:557
  16.3 0.6 %copy-start = (f32[8,8,128]{2,1,0:T(8,128)}, f32[8,8,128]{2,1,0:T(8,128)S(1)}, u32[]{:S(2)}) copy-start(f32[8,8,128]{2,1,0:T(8,128)S(1)} %all-to-all-done.cells) | copy-start | bytes 98308
  18.4 14.2 %collective-permute-start = (bf16[160,128]{1,0:T(8,128)(2,1)}, bf16[160,128]{1,0:T(8,128)(2,1)S(1)}, u32[]{:S(2)}, u32[]{:S(2)}) collective-permute-start(bf16[160,128]{1,0:T(8,128)(2,1)} %get-tuple-element.20), channel_id=1, source_target_pairs={{0,1},{1,0},{2,3},{3,2},{4,5},{5,4},{6,7},{7,6},{8,9},{9,8},{10,11... | collective-permute-start | bytes 122888 | tf_op jit(solution)/shard_map/ppermute | solution.py:611
  19.2 13.4 %collective-permute-start.1 = (bf16[160,128]{1,0:T(8,128)(2,1)}, bf16[160,128]{1,0:T(8,128)(2,1)S(1)}, u32[]{:S(2)}, u32[]{:S(2)}) collective-permute-start(bf16[160,128]{1,0:T(8,128)(2,1)} %get-tuple-element.21), channel_id=1, source_target_pairs={{1,2},{2,1},{3,4},{4,3},{5,6},{6,5},{7,8},{8,7},{9,10},{10,9},{11,... | collective-permute-start | bytes 122888 | tf_op jit(solution)/shard_map/ppermute | solution.py:612
  32.6 0.6 %copy-start.1 = (bf16[160,128]{1,0:T(8,128)(2,1)}, bf16[160,128]{1,0:T(8,128)(2,1)S(1)}, u32[]{:S(2)}) copy-start(bf16[160,128]{1,0:T(8,128)(2,1)S(1)} %collective-permute-done.refs_2_) | copy-start | bytes 122884
  32.6 0.6 %copy-start.2 = (bf16[160,128]{1,0:T(8,128)(2,1)}, bf16[160,128]{1,0:T(8,128)(2,1)S(1)}, u32[]{:S(2)}) copy-start(bf16[160,128]{1,0:T(8,128)(2,1)S(1)} %collective-permute-done.1.refs_3_) | copy-start | bytes 122884

commit v2 on v1

v2 whole, which is shorter than its diff:
```python
import functools

import jax
import jax.numpy as jnp
import numpy as np
from jax import lax
from jax.experimental import pallas as pl
from jax.experimental.pallas import tpu as pltpu
from jax.sharding import PartitionSpec as P

VARS = 4
CCH = 12
CIN = 20
CH = 128
CH2 = 256
HEADS = 4
HEAD_DIM = 64
P_SIZE = 32
M = 16
W = 32
SLOTS = 6
FACTOR = 8
BLK_DEV = 8
MIX = 4
DOM = 64
TOKENS = 32
BR = 4
BW = 4
MEMBERS = 8

SIGMA_DATA = 0.5
NORM_EPS = 1e-06

F32 = jnp.float32
BF16 = jnp.bfloat16

IN_LANES = 2 * W * VARS
CELL = 64
STEM_LANES = (W + 2) * CELL
OWN_ROWS = SLOTS * P_SIZE
DOMAINS = SLOTS + 2
SIDE_ROWS = 64
OWN_TOKENS = OWN_ROWS // 8 * 4
SIDE_PATCHES = 4
PIECE = 160
BASIS = IN_LANES + 2 * BW * CCH
SIDE_SPAN = 80
CHUNKS = 9
HALF = W // 2
HALF_LANES = HALF * CH
TAP_LANES = (HALF + 2) * VARS
GROUP_ROWS = 224
VMEM_LIMIT = 24 * 1024 * 1024


def interp_matrix(fine_count, coarse_count):
    position = (np.arange(fine_count) + 0.5) / FACTOR - 0.5
    position = np.clip(position, 0.0, coarse_count - 1.0)
    return np.maximum(0.0, 1.0 - np.abs(position[:, None] - np.arange(coarse_count)[None, :]))


def along_rows(sources, patches):
    row_map = interp_matrix(P_SIZE, BR)
    along = np.zeros((len(sources), 2, patches, BR), np.float32)
    for row, source in enumerate(sources):
        along[row, :, source // P_SIZE] = row_map[source % P_SIZE][None]
    return along


@functools.cache
def tables():
    col_map = interp_matrix(W, BW)
    noisy, mean = (np.zeros((W, VARS, W + 2, CELL), np.float32) for _ in range(2))
    across = np.zeros((2, BW, CCH, W + 2, CELL), np.float32)
    for tap in range(3):
        at = tap * CIN
        for col in range(W):
            for var in range(VARS):
                noisy[col, var, col + 1, at + var] = 1.0
                mean[col, var, col + 1, at + VARS + var] = 1.0
        for channel in range(CCH):
            across[:, :, channel, 1 : W + 1, at + 2 * VARS + channel] = col_map.T[None]
    basis = np.concatenate([part.reshape(-1, STEM_LANES) for part in (noisy, mean, across)])
    basis = np.pad(basis, ((0, 0), (0, CHUNKS * 256 - STEM_LANES)))
    basis = basis.reshape(BASIS, CHUNKS, 256).transpose(1, 0, 2)
    along = along_rows(range(OWN_ROWS), SLOTS).reshape(OWN_ROWS, 2 * SLOTS * BR)
    side = along_rows(range(8, 8 + SIDE_SPAN), SIDE_PATCHES)
    along_side = np.zeros((2, SIDE_SPAN, 2, 2, SIDE_PATCHES, BR), np.float32)
    for number in range(2):
        along_side[number, :, :, number] = side
    along_side = along_side.reshape(2 * SIDE_SPAN, 4 * SIDE_PATCHES * BR)
    place = np.zeros((3, 3, VARS, HALF, 256), np.float32)
    for cell in range(HALF):
        for row_tap in range(3):
            for col_tap in range(3):
                for var in range(VARS):
                    lane = row_tap * TAP_LANES + (cell + 2 - col_tap) * VARS + var
                    place[row_tap, col_tap, var, cell, lane] = 1.0
    place = place.reshape(36, HALF * 256)
    return tuple(array.astype(jnp.bfloat16) for array in (basis, along, along_side, place))


def silu(value):
    half = 0.5 * value
    return half + half * jnp.tanh(half)


def dot(left, right):
    return jnp.dot(left, right, preferred_element_type=F32)


def fetch(sems, pairs):
    copies = [pltpu.make_async_copy(a, b, sems.at[i]) for i, (a, b) in enumerate(pairs)]
    for copy in copies:
        copy.start()
    return copies


def mix_kernel(src, widx, table, coarse, copies_out, src_s, widx_s, table_s, blocks, sems):
    for copy in fetch(sems, [(src, src_s), (widx, widx_s), (table, table_s), (coarse, blocks)]):
        copy.wait()
    copies_out[...] = jnp.zeros_like(copies_out)
    for slot in range(SLOTS):
        total = jnp.zeros((1, 24), F32)
        for k in range(MIX):
            total = total + table_s[widx_s[k, slot]] * blocks[pl.ds(src_s[k, slot], 1)]
        for member in range(MEMBERS):
            copies_out[member, slot : slot + 1, 0:24] = total


def prepare_kernel(
    counts, sigma, sigma_next, noise_embed, w_stem, noisy, mean_field, basis, along,
    noisy_v, mean_v, basis_v, along_v, held_out, first_out, second_out, levels_out, stem_out,
    embed_v, w_stem_v, stem_f32, sems,
):
    copies = fetch(
        sems,
        [
            (noise_embed, embed_v),
            (noisy, noisy_v),
            (mean_field, mean_v),
            (w_stem, w_stem_v),
            (basis, basis_v),
            (along, along_v),
        ],
    )
    stem_f32[...] = jnp.zeros_like(stem_f32)
    for copy in copies[0:3]:
        copy.wait()
    held = counts[0]
    held_out[0] = held
    level = jnp.full((1, 128), sigma[0], F32)
    variance = level * level + SIGMA_DATA * SIGMA_DATA
    c_in = lax.rsqrt(variance)
    levels_out[0:1] = jnp.log(level) * 0.125 * embed_v[...].reshape(1, CH)
    levels_out[1:2] = SIGMA_DATA * SIGMA_DATA / variance
    levels_out[2:3] = level * SIGMA_DATA * lax.rsqrt(variance)
    levels_out[3:4] = jnp.full((1, 128), sigma_next[0], F32) / level - 1.0
    levels_out[4:5] = c_in
    even = lax.rem(lax.axis_index("space"), 2) == 0
    c_in = c_in.reshape(1, 1, 128)
    for out, to_right in ((first_out, even), (second_out, jnp.logical_not(even))):
        start = jnp.where(to_right, held - 2, 0)
        out[0:64] = (c_in * noisy_v[pl.ds(start, 2)]).astype(BF16).reshape(64, 128)
        out[64:128] = mean_v[pl.ds(start, 2)].astype(BF16).reshape(64, 128)

    copies[3].wait()
    stem_taps = w_stem_v[...].astype(F32) * 0.5
    for cell in range(4):
        for target in range(2):
            col_tap = cell - target
            if 0 <= col_tap < 3:
                for row_tap in range(3):
                    at = (3 * row_tap + col_tap) * CIN
                    to = cell * CELL + row_tap * CIN
                    stem_f32[to : to + CIN, target * CH : (target + 1) * CH] = stem_taps[at : at + CIN]
    stem_out[...] = stem_f32[...].astype(BF16)
    for copy in copies[4:]:
        copy.wait()


def pack_kernel(held_in, cells, first_in, second_in, first_out, second_out, mix_out):
    held = held_in[0]
    for member in range(MEMBERS):
        mix_out[pl.ds(member, SLOTS, stride=MEMBERS)] = cells[member, 0:SLOTS]
    even = lax.rem(lax.axis_index("space"), 2) == 0
    for out, given, to_right in (
        (first_out, first_in, even),
        (second_out, second_in, jnp.logical_not(even)),
    ):
        start = pl.multiple_of(jnp.where(to_right, held - 2, 0) * MEMBERS, MEMBERS)
        out[0:128] = given[0:128]
        mixed = mix_out[pl.ds(start, 16)]
        high = mixed.astype(BF16)
        out[128:144] = high
        out[144:160] = (mixed - high.astype(F32)).astype(BF16)


def interpolate(mixes, count, along):
    pair = mixes[pl.ds(0, count, stride=2)] + pltpu.roll(mixes[pl.ds(1, count, stride=2)], 24, 1)
    high = pair.astype(BF16).astype(F32)
    rows = dot(along[...], jnp.concatenate([high, pair - high], axis=0).astype(BF16))
    high = rows.astype(BF16).astype(F32)
    return (high + pltpu.roll(rows - high, 48, 1)).astype(BF16)


def widen(operand, basis, blocks, wide, stem_in):
    rows = operand.shape[0]
    lane = lax.rem(lax.broadcasted_iota(jnp.int32, (1, 128), 1), CELL)
    above, here = lane < CIN, lane < 2 * CIN
    zero = jnp.zeros((8, 128), F32)
    for number in range(4):
        wide[number, 0:8] = zero
        wide[number, 8 + rows :] = zero
    given = operand[:, 0:BASIS]
    for chunk in range(CHUNKS):
        lanes = min(256, STEM_LANES - chunk * 256)
        product = dot(given, basis[chunk, :, 0:lanes])
        for half in range(lanes // 128):
            number = chunk % 2 * 2 + half
            wide[number, 8 : 8 + rows] = product[:, half * 128 : (half + 1) * 128]
            start = chunk * 256 + half * 128
            for first, to, count in blocks:
                at = 8 + first
                stem_in[to : to + count, start : start + 128] = jnp.where(
                    above,
                    wide[number, at - 1 : at - 1 + count],
                    jnp.where(
                        here, wide[number, at : at + count], wide[number, at + 1 : at + 1 + count]
                    ),
                ).astype(BF16)


def stem(stem_in, stem_right, shift, features, store_pooled):
    rows = features.shape[0]
    for block_col in range(4):
        summed = jnp.zeros((rows, CH), F32)
        for cell_pair in range(4):
            number = block_col * 4 + cell_pair
            raw = dot(stem_in[:, number * 128 : number * 128 + 256], stem_right[...])
            for part in range(2):
                half = raw[:, part * CH : (part + 1) * CH] + shift
                feature = (0.5 * half) * (1.0 + jnp.tanh(half))
                lane = number * 256 + part * CH
                features[:, lane : lane + CH] = feature.astype(BF16)
                summed = summed + feature
        store_pooled(block_col, jnp.sum(summed.reshape(rows // 8, 8, CH), axis=1) * (1.0 / 32.0))


def bottleneck(pooled, starts, weights):
    w_down, w_query, w_key, w_value, w_attn_out, w_up = weights
    zeta = silu(dot(pooled.astype(BF16), w_down[...]))
    scale = lax.rsqrt(jnp.mean(zeta * zeta, axis=-1, keepdims=True) + NORM_EPS)
    normed = (zeta * scale).astype(BF16)
    query = dot(normed, w_query[...]).astype(BF16)
    keyed = dot(normed, w_key[...]).astype(BF16)
    valued = dot(normed, w_value[...]).astype(BF16)
    head_of_row = lax.broadcasted_iota(jnp.int32, (HEADS * TOKENS, CH2), 0) // TOKENS
    head_of_channel = lax.broadcasted_iota(jnp.int32, (HEADS * TOKENS, CH2), 1) // HEAD_DIM
    own_head = (head_of_row == head_of_channel).astype(F32).astype(BF16)
    head_of_lane = lax.broadcasted_iota(jnp.int32, (TOKENS, HEADS * TOKENS), 1) // TOKENS
    mixed_heads = []
    residual = []
    for start in starts:
        rows = slice(start, start + TOKENS)
        keys = jnp.concatenate([keyed[rows]] * HEADS, axis=0) * own_head
        values = jnp.concatenate([valued[rows]] * HEADS, axis=0) * own_head
        scores = lax.dot_general(
            query[rows], keys, (((1,), (1,)), ((), ())), preferred_element_type=F32
        ) * (HEAD_DIM**-0.5)
        top = jnp.zeros_like(scores)
        for head in range(HEADS):
            inside = head_of_lane == head
            largest = jnp.max(jnp.where(inside, scores, -jnp.inf), axis=1, keepdims=True)
            top = jnp.where(inside, largest, top)
        weight = jnp.exp(scores - top).astype(BF16)
        mixed_heads.append((dot(weight, values) / dot(weight, own_head)).astype(BF16))
        residual.append(zeta[rows])
    attended = jnp.concatenate(mixed_heads, axis=0)
    resid = (jnp.concatenate(residual, axis=0) + dot(attended, w_attn_out[...])).astype(BF16)
    return 0.5 * dot(resid, w_up[...])


def activate(number, sources, first, lifted, active, base):
    half_rows = active.shape[0] // 2
    count = sum(rows for _, _, rows in sources) // 8
    for block_col in range(4):
        raised = lifted[pl.ds(number * TOKENS + first * 4 + block_col, count, stride=4)].reshape(
            count, 1, CH
        )
        done = 0
        for ref, start, rows in sources:
            part = raised[done // 8 : (done + rows) // 8]
            for cell in range(block_col * 8, block_col * 8 + 8):
                given = ref[pl.ds(start, rows), cell * CH : (cell + 1) * CH]
                half = given.astype(F32).reshape(rows // 8, 8, CH) + part
                value = half + half * jnp.tanh(half)
                to = base + done + cell // HALF * half_rows
                lane = cell % HALF * CH
                active[to : to + rows, lane : lane + CH] = value.reshape(rows, CH).astype(BF16)
            done += rows


def predict(left, right, first, last, padded):
    rows = (last - first) * 8
    lane = lax.broadcasted_iota(jnp.int32, (rows, 128), 1)
    for tap in range(3):
        from_left = pltpu.roll(left, (-4 - TAP_LANES * tap) % 256, 1)[:, 0:128]
        from_right = pltpu.roll(right, (60 - TAP_LANES * tap) % 256, 1)[:, 0:128]
        padded[8 : 8 + rows, tap * 128 : (tap + 1) * 128] = jnp.where(
            lane < 68, from_left, 0.0
        ) + jnp.where(lane >= 60, from_right, 0.0)
    zero = jnp.zeros((8, 384), F32)
    padded[0:8] = zero
    padded[8 + rows : 16 + rows] = zero
    field = (
        padded[7 : 7 + rows, 0:128] + padded[8 : 8 + rows, 128:256] + padded[9 : 9 + rows, 256:384]
    )
    row = lax.broadcasted_iota(jnp.int32, (rows, 128), 0) + first * 8
    return field * jnp.minimum(row + 1, DOM - row).astype(F32)


def own_kernel(
    noisy, mean_field, mixes, along, levels, basis, stem_right, w_out, place, *refs
):
    loaded, kept = refs[:7], refs[7:14]
    features, pooled, right_out = refs[14:17]
    w_out_v, place_v, operand, wide, stem_in, sems = refs[17:]
    copies = fetch(sems, [(w_out, w_out_v), (place, place_v)] + list(zip(loaded, kept)))
    c_in = levels[4:5].reshape(1, 1, 128)
    operand[:, 0:128] = (c_in * noisy[...]).astype(BF16).reshape(OWN_ROWS, 128)
    operand[:, 128:256] = mean_field[...].astype(BF16).reshape(OWN_ROWS, 128)
    operand[:, 256:384] = interpolate(mixes, SLOTS * BR, along)
    widen(operand, basis, [(0, 0, OWN_ROWS)], wide, stem_in)

    def store_pooled(block_col, value):
        pooled[pl.ds(block_col, OWN_ROWS // 8, stride=4)] = value

    stem(stem_in, stem_right, levels[0:1], features, store_pooled)
    for copy in copies[0:2]:
        copy.wait()
    weights = w_out_v[...]
    for cell in range(HALF):
        right_out[cell * CH : (cell + 1) * CH] = lax.dot_general(
            weights,
            place_v[:, cell * 256 : (cell + 1) * 256],
            (((0,), (0,)), ((), ())),
            preferred_element_type=F32,
        ).astype(BF16)
    for copy in copies[2:]:
        copy.wait()


def main_kernel(
    held_in, noisy, mean_field, first_in, second_in, mix_own, levels, along, basis, stem_right,
    pooled_own, features, w_down, w_query, w_key, w_value, w_attn_out, w_up, out_right,
    denoised_out, next_out,
    state_rows, mean_rows, mixes, operand, wide, stem_in, ends, pooled, lifted, active, halves,
    padded, total,
):
    held = held_in[0]
    position = lax.axis_index("space")
    even = lax.rem(position, 2) == 0
    has_left = position > 0
    has_right = position < lax.axis_size("space") - 1
    c_in = levels[4:5].reshape(1, 1, 128)

    state_rows[0, 64:96] = (c_in * noisy[0:1]).reshape(P_SIZE, 128)
    mean_rows[0, 64:96] = mean_field[0]
    state_rows[1, 0:32] = (c_in * noisy[pl.ds(held - 1, 1)]).reshape(P_SIZE, 128)
    mean_rows[1, 0:32] = mean_field[pl.ds(held - 1, 1)].reshape(P_SIZE, 128)
    mixes[16:24] = mix_own[0:8]
    mixes[24:32] = jnp.zeros((8, 128), F32)
    mixes[32:40] = mix_own[pl.ds(pl.multiple_of(8 * held - 8, 8), 8)]
    mixes[56:64] = jnp.zeros((8, 128), F32)

    def take(piece, side, rows_at, mixes_at):
        state_rows[side, rows_at : rows_at + 64] = piece[0:64].astype(F32)
        mean_rows[side, rows_at : rows_at + 64] = piece[64:128].astype(F32)
        mixes[mixes_at : mixes_at + 16] = piece[128:144].astype(F32) + piece[144:160].astype(F32)

    @pl.when(even)
    def _():
        take(second_in, 0, 0, 0)
        take(first_in, 1, 32, 40)

    @pl.when(jnp.logical_not(even))
    def _():
        take(first_in, 0, 0, 0)
        take(second_in, 1, 32, 40)

    for side in range(2):
        span = slice(SIDE_SPAN * side, SIDE_SPAN * (side + 1))
        operand[span, 0:128] = state_rows[side, 8 : 8 + SIDE_SPAN].astype(BF16)
        operand[span, 128:256] = mean_rows[side, 8 : 8 + SIDE_SPAN].astype(BF16)
    operand[:, 256:384] = interpolate(mixes, 2 * SIDE_PATCHES * BR, along)
    widen(
        operand, basis, [(8, 0, SIDE_ROWS), (SIDE_SPAN + 8, SIDE_ROWS, SIDE_ROWS)], wide, stem_in
    )

    def store_pooled(block_col, value):
        pooled[pl.ds(block_col, 8, stride=4)] = value[0:8]
        pooled[pl.ds(64 + block_col, 8, stride=4)] = value[8:16]

    stem(stem_in, stem_right, levels[0:1], ends, store_pooled)
    pooled[32:48] = pooled_own[8:24]
    pooled[48:64] = pooled_own[pl.ds(pl.multiple_of(16 * held - 24, 8), 16)]
    pooled[96:104] = jnp.zeros((8, CH), F32)
    pooled[104:200] = pooled_own[...]
    pooled[200:208] = jnp.zeros((8, CH), F32)

    @pl.when(jnp.logical_not(has_left))
    def _():
        ends[0:48] = jnp.zeros((48, W * CH), BF16)
        pooled[0:24] = jnp.zeros((24, CH), F32)

    @pl.when(jnp.logical_not(has_right))
    def _():
        ends[80:128] = jnp.zeros((48, W * CH), BF16)
        pooled[72:96] = jnp.zeros((24, CH), F32)

    lifted[...] = bottleneck(
        pooled[...],
        [0, 16, 112, 128, 144, 160, 48, 64],
        (w_down, w_query, w_key, w_value, w_attn_out, w_up),
    )
    near = pl.multiple_of(P_SIZE * held - 48, 16)
    last = pl.multiple_of(P_SIZE * held - M, 16)
    plans = [
        (4, 8, [(ends, 32, 32)], 0, 16, 32, has_left),
        (0, 8, [(ends, 32, 32), (features, 16, 32)], 0, 16, 64, True),
    ]
    for patch in range(1, SLOTS - 1):
        start = P_SIZE * patch - M
        plans.append((0, 8, [(features, start, DOM)], start, 0, 64, patch <= held - 2))
    plans += [
        (0, 8, [(features, near, 32), (ends, 64, 32)], near, 0, 48, True),
        (0, 4, [(ends, 64, 32)], last, 0, 16, has_right),
    ]
    total[...] = jnp.zeros_like(total)
    for group in range(2):
        base = 0
        for number in range(4 * group, 4 * group + 4):
            first, stop, sources = plans[number][:3]
            activate(number, sources, first, lifted, active.at[group], base)
            base += (stop - first) * 8
        halves[group] = dot(active[group], out_right[...])
    for group in range(2):
        base = 0
        for number in range(4 * group, 4 * group + 4):
            first, stop, _, to, start, end, counted = plans[number]
            rows = (stop - first) * 8
            field = predict(
                halves[group, base : base + rows],
                halves[group, GROUP_ROWS + base : GROUP_ROWS + base + rows],
                first,
                stop,
                padded.at[number % 2],
            )[start:end]
            if counted is not True:
                field = jnp.where(counted, field, 0.0)
            span = pl.ds(to, end - start)
            total[span] = total[span] + field
            base += rows

    slot = lax.broadcasted_iota(jnp.int32, (SLOTS, P_SIZE, 128), 0)
    row = lax.broadcasted_iota(jnp.int32, (SLOTS, P_SIZE, 128), 1)
    norm = jnp.full((SLOTS, P_SIZE, 128), 33, jnp.int32)
    no_left = jnp.logical_and(jnp.logical_not(has_left), jnp.logical_and(slot == 0, row < M))
    no_right = jnp.logical_and(
        jnp.logical_not(has_right), jnp.logical_and(slot == held - 1, row >= M)
    )
    norm = jnp.where(no_left, 17 + row, norm)
    norm = jnp.where(no_right, 48 - row, norm)
    blended = total[...].reshape(SLOTS, P_SIZE, 128) / norm.astype(F32)
    state = noisy[...]
    denoised = levels[1:2].reshape(1, 1, 128) * state + levels[2:3].reshape(1, 1, 128) * blended
    stepped = state + levels[3:4].reshape(1, 1, 128) * (state - denoised)
    live = slot < held
    denoised_out[...] = jnp.where(live, denoised, 0.0)
    next_out[...] = jnp.where(live, stepped, 0.0)


def shards(
    noisy,
    mean_field,
    coarse,
    counts,
    src,
    widx,
    table,
    sigma,
    sigma_next,
    w_stem,
    noise_embed,
    w_down,
    w_query,
    w_key,
    w_value,
    w_attn_out,
    w_up,
    w_out,
):
    owners = lax.axis_size("space")
    smem = pl.BlockSpec(memory_space=pltpu.SMEM)
    vmem = pl.BlockSpec(memory_space=pltpu.VMEM)
    hbm = pl.BlockSpec(memory_space=pltpu.HBM)
    limit = pltpu.CompilerParams(vmem_limit_bytes=VMEM_LIMIT)

    def in_hbm(*arrays):
        return [pltpu.with_memory_space_constraint(array, pltpu.HBM) for array in arrays]

    def in_vmem(*shapes):
        return [pltpu.VMEM(shape, dtype) for shape, dtype in shapes]

    state = noisy[0]
    copies = pl.pallas_call(
        mix_kernel,
        out_shape=pltpu.VMEM((MEMBERS, 8, 128), F32),
        in_specs=[hbm] * 4,
        out_specs=vmem,
        scratch_shapes=[
            pltpu.SMEM((MIX, SLOTS), jnp.int32),
            pltpu.SMEM((MIX, SLOTS), jnp.int32),
            pltpu.SMEM((16,), F32),
            pltpu.VMEM((BLK_DEV, 24), F32),
            pltpu.SemaphoreType.DMA((4,)),
        ],
        compiler_params=limit,
        name="mix",
    )(*in_hbm(src.T, widx.T, table, coarse))
    cells = lax.all_to_all(copies, "member", 0, 0, tiled=True)

    basis, along, along_side, place = (jnp.asarray(array) for array in tables())
    loaded = [state, mean_field, basis, along]
    prepared = pl.pallas_call(
        prepare_kernel,
        out_shape=in_vmem(*((array.shape, array.dtype) for array in loaded))
        + [jax.ShapeDtypeStruct((8,), jnp.int32)]
        + in_vmem(
            ((PIECE, 128), BF16), ((PIECE, 128), BF16), ((8, 128), F32), ((CH2, CH2), BF16)
        ),
        in_specs=[smem] * 3 + [hbm] * 6,
        out_specs=[vmem] * 4 + [smem] + [vmem] * 4,
        scratch_shapes=[
            pltpu.VMEM(noise_embed.shape, F32),
            pltpu.VMEM(w_stem.shape, BF16),
            pltpu.VMEM((256, 256), F32),
            pltpu.SemaphoreType.DMA((6,)),
        ],
        compiler_params=limit,
        cost_estimate=pl.CostEstimate(flops=10**9, bytes_accessed=8 * 10**6, transcendentals=0),
        name="prepare",
    )(counts, sigma, sigma_next, *in_hbm(noise_embed, w_stem, *loaded))
    state, mean_field, basis, along, held, first, second, levels, stem_right = prepared

    first, second, mix_own = pl.pallas_call(
        pack_kernel,
        out_shape=in_vmem(
            ((PIECE, 128), BF16), ((PIECE, 128), BF16), ((SLOTS * MEMBERS, 128), F32)
        ),
        in_specs=[smem] + [vmem] * 3,
        out_specs=[vmem] * 3,
        compiler_params=limit,
        name="pack",
    )(held, cells, first, second)
    pairs = [(i, i ^ 1) for i in range(owners)]
    others = []
    for i in range(1, owners - 1, 2):
        others += [(i, i + 1), (i + 1, i)]
    first = lax.ppermute(first, "space", pairs)
    second = lax.ppermute(second, "space", others)

    loaded = [along_side, w_down, w_query, w_key, w_value, w_attn_out, w_up]
    *loaded, features, pooled, out_right = pl.pallas_call(
        own_kernel,
        out_shape=in_vmem(*((array.shape, array.dtype) for array in loaded))
        + in_vmem(
            ((OWN_ROWS, W * CH), BF16), ((OWN_TOKENS, CH), F32), ((HALF_LANES, 256), BF16)
        ),
        in_specs=[vmem] * 7 + [hbm] * 9,
        out_specs=[vmem] * 10,
        scratch_shapes=[
            pltpu.VMEM(w_out.T.shape, BF16),
            pltpu.VMEM(place.shape, BF16),
            pltpu.VMEM((OWN_ROWS, 384), BF16),
            pltpu.VMEM((4, OWN_ROWS + 16, 128), F32),
            pltpu.VMEM((OWN_ROWS, STEM_LANES), BF16),
            pltpu.SemaphoreType.DMA((9,)),
        ],
        compiler_params=limit,
        cost_estimate=pl.CostEstimate(flops=10**9, bytes_accessed=10**7, transcendentals=2 * 10**6),
        name="own",
    )(
        state, mean_field, mix_own, along, levels, basis, stem_right,
        *in_hbm(w_out.T, place, *loaded),
    )
    along_side, *weights = loaded

    denoised, stepped = pl.pallas_call(
        main_kernel,
        out_shape=(
            jax.ShapeDtypeStruct((SLOTS, P_SIZE, 128), F32),
            jax.ShapeDtypeStruct((SLOTS, P_SIZE, 128), F32),
        ),
        in_specs=[smem] + [vmem] * 18,
        out_specs=(vmem, vmem),
        scratch_shapes=[
            pltpu.VMEM((2, 96, 128), F32),
            pltpu.VMEM((2, 96, 128), F32),
            pltpu.VMEM((64, 128), F32),
            pltpu.VMEM((2 * SIDE_SPAN, 384), BF16),
            pltpu.VMEM((4, 2 * SIDE_SPAN + 16, 128), F32),
            pltpu.VMEM((2 * SIDE_ROWS, STEM_LANES), BF16),
            pltpu.VMEM((2 * SIDE_ROWS, W * CH), BF16),
            pltpu.VMEM((208, CH), F32),
            pltpu.VMEM((DOMAINS * TOKENS, CH), F32),
            pltpu.VMEM((2, 2 * GROUP_ROWS, HALF_LANES), BF16),
            pltpu.VMEM((2, 2 * GROUP_ROWS, 256), F32),
            pltpu.VMEM((2, 80, 384), F32),
            pltpu.VMEM((OWN_ROWS, 128), F32),
        ],
        compiler_params=limit,
        cost_estimate=pl.CostEstimate(flops=10**9, bytes_accessed=10**7, transcendentals=2 * 10**6),
        name="main",
    )(
        held, state, mean_field, first, second, mix_own, levels, along_side, basis, stem_right,
        pooled, features, *weights, out_right,
    )
    return denoised[None], stepped[None]


def solution(mesh):
    placed = (
        P("member", "space", None, None),
        P("space", None, None),
        P("space", "member"),
        P("space"),
        P("space", None),
        P("space", None),
        P(),
        P("member"),
        P("member"),
        P(),
        P(),
        P(),
        P(),
        P(),
        P(),
        P(),
        P(),
        P(),
    )
    return jax.shard_map(
        shards,
        mesh=mesh,
        in_specs=placed,
        out_specs=(P("member", "space", None, None), P("member", "space", None, None)),
        check_vma=False,
    )
```

time: 43.2 us -> 30.3 us (0.70)
  the two profiles are of different devices: /device:TPU:122 before, /device:TPU:128 now
where the time goes in v2:
time: 30.3 us; the launch traced here: 30 us
  Pallas kernels  13.8 us (46%)
  starting transfers between devices  9.6 us (32%)
  waiting for transfers between devices  3.89 us (13%)
  between operations  2.63 us (9%)
    pallas_call x1, Pallas kernels, shards(): pl.pallas_call(main_kernel, out_shape=(jax.ShapeDtypeStruct((SLOTS, P_SIZ...  6.7 us
    all_to_all x1, starting transfers between devices, shards(): cells = lax.all_to_all(copies, 'member', 0, 0, tiled=True)  4.31 us
    ppermute x1, starting transfers between devices, shards(): second = lax.ppermute(second, 'space', others)  3.62 us
    pallas_call x1, Pallas kernels, shards(): pl.pallas_call(own_kernel, out_shape=in_vmem(*((array.shape, array.dtype)...  2.93 us
    ppermute x1, waiting for transfers between devices, shards(): second = lax.ppermute(second, 'space', others)  2.63 us
    pallas_call x1, Pallas kernels, shards(): pl.pallas_call(prepare_kernel, out_shape=in_vmem(*((array.shape, array.dt...  2.23 us
    ppermute x1, starting transfers between devices, shards(): first = lax.ppermute(first, 'space', pairs)  1.66 us
    pallas_call x1, Pallas kernels, shards(): pl.pallas_call(mix_kernel, out_shape=pltpu.VMEM((MEMBERS, 8, 128), F32),...  1.42 us
  transfers between devices with their start and end apart: 3, of which 2 were waited for; matrix products, arithmetic and copies ran while one was open for 0% of the time, Pallas kernels for 17%

profile of v2, /device:TPU:128, one launch (start us, length us, event | category | flops | bytes accessed | tf_op | source)
XLA Modules:
  0.0 30.0 jit_solution(18158670428151196919)
XLA Ops:
  0.6 1.4 %mix.1 = f32[8,8,128]{2,1,0:T(8,128)} custom-call(s32[4,6]{1,0:T(4,128)} %bitcast.6, s32[4,6]{1,0:T(4,128)} %bitcast.7, f32[16]{0:T(128)} %table.1, f32[8,24]{1,0:T(8,128)} %coarse.1), custom_call_target="tpu_custom_call" | custom-call | tf_op jit(solution)/shard_map/mix/pallas_call | solution.py:517
  2.1 4.3 %all-to-all-start = ((f32[8,8,128]{2,1,0:T(8,128)}), f32[8,8,128]{2,1,0:T(8,128)S(1)}, u32[]{:S(2)}, u32[]{:S(2)}) async-start(f32[8,8,128]{2,1,0:T(8,128)} %mix.1), calls=%async_computation | async-start | bytes 65536 | tf_op jit(solution)/shard_map/all_to_all | solution.py:532
  8.3 2.2 %prepare.1 = (f32[6,32,128]{2,1,0:T(8,128)S(1)}, f32[6,32,128]{2,1,0:T(8,128)S(1)}, bf16[9,352,256]{2,1,0:T(8,128)(2,1)S(1)}, bf16[192,48]{1,0:T(8,128)(2,1)S(1)...) custom-call(s32[1]{0:T(128)S(6)} %copy.24.counts, ...), custom_call_target="tpu_custom_call" | custom-call | flops 1000000000 | bytes 8000000 | tf_op jit(solution)/shard_map/prepare/pallas_call | solution.py:536
  10.6 1.3 %all-to-all-done.cells = f32[8,8,128]{2,1,0:T(8,128)S(1)} async-done(((f32[8,8,128]{2,1,0:T(8,128)}), f32[8,8,128]{2,1,0:T(8,128)S(1)}, u32[]{:S(2)}, u32[]{:S(2)}) %all-to-all-start) | async-done | bytes 32800 | tf_op jit(solution)/shard_map/all_to_all | solution.py:532
  11.8 0.6 %pack.1 = (bf16[160,128]{1,0:T(8,128)(2,1)S(1)}, bf16[160,128]{1,0:T(8,128)(2,1)S(1)}, f32[48,128]{1,0:T(8,128)S(1)}) custom-call(s32[8]{0:T(128)S(1)} %get-tuple-element.26.held_in, f32[8,8,128]{2,1,0:T(8,128)S(1)} %all-to-all-done.cells, bf16[160,128]{1,0:T(8,128)(2,1)S(1)} %get-tuple-element.29.first_in, bf16[160,128]{1,0:T(8,128)(2,1)S(1)} %get-tuple-element.30.second_in), custom_call_target="tpu_custom_call" | custom-call | tf_op jit(solution)/shard_map/pack/pallas_call | solution.py:557
  12.4 1.7 %collective-permute-start = (bf16[160,128]{1,0:T(8,128)(2,1)S(1)}, bf16[160,128]{1,0:T(8,128)(2,1)S(1)}, u32[]{:S(2)}, u32[]{:S(2)}) collective-permute-start(bf16[160,128]{1,0:T(8,128)(2,1)S(1)} %get-tuple-element.31), channel_id=1, source_target_pairs={{0,1},{1,0},{2,3},{3,2},{4,5},{5,4},{6,7},{7,6},{8,9},{9,8},{10,11... | collective-permute-start | bytes 122888 | tf_op jit(solution)/shard_map/ppermute | solution.py:571
  14.1 3.6 %collective-permute-start.1 = (bf16[160,128]{1,0:T(8,128)(2,1)S(1)}, bf16[160,128]{1,0:T(8,128)(2,1)S(1)}, u32[]{:S(2)}, u32[]{:S(2)}) collective-permute-start(bf16[160,128]{1,0:T(8,128)(2,1)S(1)} %get-tuple-element.32), channel_id=1, source_target_pairs={{1,2},{2,1},{3,4},{4,3},{5,6},{6,5},{7,8},{8,7},{9,10},{10,9},{11,... | collective-permute-start | bytes 122888 | tf_op jit(solution)/shard_map/ppermute | solution.py:572
  17.7 2.9 %own.1 = (bf16[160,64]{1,0:T(8,128)(2,1)S(1)}, bf16[128,256]{1,0:T(8,128)(2,1)S(1)}, bf16[256,256]{1,0:T(8,128)(2,1)S(1)}, bf16[256,256]{1,0:T(8,128)(2,1)S(1)},...) custom-call(f32[6,32,128]{2,1,0:T(8,128)S(1)} %get-tuple-element.27., ...), custom_call_target="tpu_custom_call" | custom-call | flops 1000000000 | bytes 10000000 | tf_op jit(solution)/shard_map/own/pallas_call | solution.py:575
  20.6 0.0 collective-permute-done.first_in
  20.6 2.6 %collective-permute-done.1.second_in = bf16[160,128]{1,0:T(8,128)(2,1)S(1)} collective-permute-done((bf16[160,128]{1,0:T(8,128)(2,1)S(1)}, bf16[160,128]{1,0:T(8,128)(2,1)S(1)}, u32[]{:S(2)}, u32[]{:S(2)}) %collective-permute-start.1) | collective-permute-done | bytes 40992 | tf_op jit(solution)/shard_map/ppermute | solution.py:572
  23.3 6.7 %main.1 = (f32[6,32,128]{2,1,0:T(8,128)}, f32[6,32,128]{2,1,0:T(8,128)}) custom-call(s32[8]{0:T(128)S(1)} %get-tuple-element.26.held_in, f32[6,32,128]{2,1,0:T(8,128)S(1)} %get-tuple-element.27.noisy, f32[6,32,128]{2,1,0:T(8,128)S(1)} %get-tuple-element.28.mean_field, bf16[160,128]{1,0:T(8,128)(2,1)S(1)} %collective-permute-done.first_in, ...), custom_call_target="tpu_custom_call" | custom-call | flops 1000000000 | bytes 10000000 | tf_op jit(solution)/shard_map/main/pallas_call | solution.py:600
Async XLA Ops:
  2.1 9.8 %all-to-all-start = ((f32[8,8,128]{2,1,0:T(8,128)}), f32[8,8,128]{2,1,0:T(8,128)S(1)}, u32[]{:S(2)}, u32[]{:S(2)}) async-start(f32[8,8,128]{2,1,0:T(8,128)} %mix.1), calls=%async_computation | async-start | bytes 65536 | tf_op jit(solution)/shard_map/all_to_all | solution.py:532
  12.4 8.2 %collective-permute-start = (bf16[160,128]{1,0:T(8,128)(2,1)S(1)}, bf16[160,128]{1,0:T(8,128)(2,1)S(1)}, u32[]{:S(2)}, u32[]{:S(2)}) collective-permute-start(bf16[160,128]{1,0:T(8,128)(2,1)S(1)} %get-tuple-element.31), channel_id=1, source_target_pairs={{0,1},{1,0},{2,3},{3,2},{4,5},{5,4},{6,7},{7,6},{8,9},{9,8},{10,11... | collective-permute-start | bytes 122888 | tf_op jit(solution)/shard_map/ppermute | solution.py:571
  14.1 9.2 %collective-permute-start.1 = (bf16[160,128]{1,0:T(8,128)(2,1)S(1)}, bf16[160,128]{1,0:T(8,128)(2,1)S(1)}, u32[]{:S(2)}, u32[]{:S(2)}) collective-permute-start(bf16[160,128]{1,0:T(8,128)(2,1)S(1)} %get-tuple-element.32), channel_id=1, source_target_pairs={{1,2},{2,1},{3,4},{4,3},{5,6},{6,5},{7,8},{8,7},{9,10},{10,9},{11,... | collective-permute-start | bytes 122888 | tf_op jit(solution)/shard_map/ppermute | solution.py:572

commit v3 on v2

--- a/solution.py
+++ b/solution.py
@@ -27,6 +27,7 @@
 BR = 4
 BW = 4
 MEMBERS = 8
+DISTANCES = (1, 3, 2)
 
 SIGMA_DATA = 0.5
 NORM_EPS = 1e-06
@@ -34,22 +35,18 @@
 F32 = jnp.float32
 BF16 = jnp.bfloat16
 
-IN_LANES = 2 * W * VARS
 CELL = 64
 STEM_LANES = (W + 2) * CELL
 OWN_ROWS = SLOTS * P_SIZE
-DOMAINS = SLOTS + 2
 SIDE_ROWS = 64
 OWN_TOKENS = OWN_ROWS // 8 * 4
 SIDE_PATCHES = 4
 PIECE = 160
-BASIS = IN_LANES + 2 * BW * CCH
+LEFT_LANES = 1152
 SIDE_SPAN = 80
-CHUNKS = 9
 HALF = W // 2
 HALF_LANES = HALF * CH
 TAP_LANES = (HALF + 2) * VARS
-GROUP_ROWS = 224
 VMEM_LIMIT = 24 * 1024 * 1024
 
 
@@ -80,9 +77,15 @@
                 mean[col, var, col + 1, at + VARS + var] = 1.0
         for channel in range(CCH):
             across[:, :, channel, 1 : W + 1, at + 2 * VARS + channel] = col_map.T[None]
-    basis = np.concatenate([part.reshape(-1, STEM_LANES) for part in (noisy, mean, across)])
-    basis = np.pad(basis, ((0, 0), (0, CHUNKS * 256 - STEM_LANES)))
-    basis = basis.reshape(BASIS, CHUNKS, 256).transpose(1, 0, 2)
+    basis = np.zeros((2, 256, LEFT_LANES), np.float32)
+    for half, lanes in enumerate((slice(0, LEFT_LANES), slice(LEFT_LANES, STEM_LANES))):
+        count = lanes.stop - lanes.start
+        cells = slice(HALF * half, HALF * half + HALF)
+        basis[half, 0:64, :count] = noisy[cells].reshape(64, STEM_LANES)[:, lanes]
+        basis[half, 64:128, :count] = mean[cells].reshape(64, STEM_LANES)[:, lanes]
+        basis[half, 128:224, :count] = across.reshape(96, STEM_LANES)[:, lanes]
+    basis[0, 224:228] = noisy[HALF].reshape(4, STEM_LANES)[:, :LEFT_LANES]
+    basis[0, 228:232] = mean[HALF].reshape(4, STEM_LANES)[:, :LEFT_LANES]
     along = along_rows(range(OWN_ROWS), SLOTS).reshape(OWN_ROWS, 2 * SLOTS * BR)
     side = along_rows(range(8, 8 + SIDE_SPAN), SIDE_PATCHES)
     along_side = np.zeros((2, SIDE_SPAN, 2, 2, SIDE_PATCHES, BR), np.float32)
@@ -116,33 +119,41 @@
     return copies
 
 
-def mix_kernel(src, widx, table, coarse, copies_out, src_s, widx_s, table_s, blocks, sems):
+def mix_kernel(src, widx, table, coarse, mixed_out, src_s, widx_s, table_s, blocks, sems):
     for copy in fetch(sems, [(src, src_s), (widx, widx_s), (table, table_s), (coarse, blocks)]):
         copy.wait()
-    copies_out[...] = jnp.zeros_like(copies_out)
+    mixed_out[...] = jnp.zeros_like(mixed_out)
     for slot in range(SLOTS):
         total = jnp.zeros((1, 24), F32)
         for k in range(MIX):
             total = total + table_s[widx_s[k, slot]] * blocks[pl.ds(src_s[k, slot], 1)]
-        for member in range(MEMBERS):
-            copies_out[member, slot : slot + 1, 0:24] = total
-
-
-def prepare_kernel(
-    counts, sigma, sigma_next, noise_embed, w_stem, noisy, mean_field, basis, along,
-    noisy_v, mean_v, basis_v, along_v, held_out, first_out, second_out, levels_out, stem_out,
-    embed_v, w_stem_v, stem_f32, sems,
-):
+        mixed_out[slot : slot + 1, 0:24] = total
+
+
+def merge_kernel(mixed, partners, merged_out):
+    core = lax.rem(lax.axis_index("member"), 2)
+    merged_out[pl.ds(pl.multiple_of(8 * core, 8), 8)] = mixed[...]
+    merged_out[pl.ds(pl.multiple_of(8 - 8 * core, 8), 8)] = partners[...]
+
+
+def prepare_kernel(counts, sigma, noise_embed, w_stem, w_out, place, *refs):
+    loaded, kept, rest = refs[:11], refs[11:22], refs[22:]
+    (
+        held_out, first_out, second_out, levels_out, stem_out, right_out,
+        embed_v, w_stem_v, w_out_v, place_v, stem_f32, sems,
+    ) = rest
+    noisy_v, mean_v = kept[:2]
     copies = fetch(
         sems,
         [
             (noise_embed, embed_v),
-            (noisy, noisy_v),
-            (mean_field, mean_v),
+            (loaded[0], noisy_v),
+            (loaded[1], mean_v),
             (w_stem, w_stem_v),
-            (basis, basis_v),
-            (along, along_v),
-        ],
+            (w_out, w_out_v),
+            (place, place_v),
+        ]
+        + list(zip(loaded[2:], kept[2:])),
     )
     stem_f32[...] = jnp.zeros_like(stem_f32)
     for copy in copies[0:3]:
@@ -155,7 +166,7 @@
     levels_out[0:1] = jnp.log(level) * 0.125 * embed_v[...].reshape(1, CH)
     levels_out[1:2] = SIGMA_DATA * SIGMA_DATA / variance
     levels_out[2:3] = level * SIGMA_DATA * lax.rsqrt(variance)
-    levels_out[3:4] = jnp.full((1, 128), sigma_next[0], F32) / level - 1.0
+    levels_out[3:4] = 1.0 / level
     levels_out[4:5] = c_in
     even = lax.rem(lax.axis_index("space"), 2) == 0
     c_in = c_in.reshape(1, 1, 128)
@@ -175,12 +186,24 @@
                     to = cell * CELL + row_tap * CIN
                     stem_f32[to : to + CIN, target * CH : (target + 1) * CH] = stem_taps[at : at + CIN]
     stem_out[...] = stem_f32[...].astype(BF16)
-    for copy in copies[4:]:
+    for copy in copies[4:6]:
         copy.wait()
-
-
-def pack_kernel(held_in, cells, first_in, second_in, first_out, second_out, mix_out):
+    weights = jnp.transpose(w_out_v[...].astype(F32)).astype(BF16)
+    for cell in range(HALF):
+        right_out[cell * CH : (cell + 1) * CH] = dot(
+            weights, place_v[:, cell * 256 : (cell + 1) * 256]
+        ).astype(BF16)
+    for copy in copies[6:]:
+        copy.wait()
+
+
+def pack_kernel(held_in, chip0, chip1, chip2, chip3, first_in, second_in, second_out, first_out, mix_out, cells):
     held = held_in[0]
+    chip = lax.axis_index("member") // 2
+    for distance, given in zip((0, *DISTANCES), (chip0, chip1, chip2, chip3)):
+        member = 2 * jnp.bitwise_xor(chip, distance)
+        cells[member] = given[0:8]
+        cells[member + 1] = given[8:16]
     for member in range(MEMBERS):
         mix_out[pl.ds(member, SLOTS, stride=MEMBERS)] = cells[member, 0:SLOTS]
     even = lax.rem(lax.axis_index("space"), 2) == 0
@@ -201,34 +224,50 @@
     high = pair.astype(BF16).astype(F32)
     rows = dot(along[...], jnp.concatenate([high, pair - high], axis=0).astype(BF16))
     high = rows.astype(BF16).astype(F32)
-    return (high + pltpu.roll(rows - high, 48, 1)).astype(BF16)
+    return high + pltpu.roll(rows - high, 48, 1)
+
+
+def assemble(operand, state, mean, cond):
+    lane = lax.broadcasted_iota(jnp.int32, state.shape, 1)
+    left = lane < 64
+    operand[0, :, 0:128] = jnp.where(left, state, pltpu.roll(mean, 64, 1)).astype(BF16)
+    operand[1, :, 0:128] = jnp.where(left, pltpu.roll(state, 64, 1), mean).astype(BF16)
+    operand[1, :, 128:256] = cond.astype(BF16)
+    more = jnp.where(lane < 100, pltpu.roll(state, 32, 1), pltpu.roll(mean, 36, 1))
+    operand[0, :, 128:256] = jnp.where(lane < 96, cond, jnp.where(lane < 104, more, 0.0)).astype(BF16)
 
 
 def widen(operand, basis, blocks, wide, stem_in):
-    rows = operand.shape[0]
+    rows = operand.shape[1]
     lane = lax.rem(lax.broadcasted_iota(jnp.int32, (1, 128), 1), CELL)
     above, here = lane < CIN, lane < 2 * CIN
     zero = jnp.zeros((8, 128), F32)
     for number in range(4):
         wide[number, 0:8] = zero
         wide[number, 8 + rows :] = zero
-    given = operand[:, 0:BASIS]
-    for chunk in range(CHUNKS):
-        lanes = min(256, STEM_LANES - chunk * 256)
-        product = dot(given, basis[chunk, :, 0:lanes])
-        for half in range(lanes // 128):
-            number = chunk % 2 * 2 + half
-            wide[number, 8 : 8 + rows] = product[:, half * 128 : (half + 1) * 128]
-            start = chunk * 256 + half * 128
-            for first, to, count in blocks:
-                at = 8 + first
-                stem_in[to : to + count, start : start + 128] = jnp.where(
-                    above,
-                    wide[number, at - 1 : at - 1 + count],
-                    jnp.where(
-                        here, wide[number, at : at + count], wide[number, at + 1 : at + 1 + count]
-                    ),
-                ).astype(BF16)
+    turn = 0
+    for half, (start, stop) in enumerate(((0, LEFT_LANES), (LEFT_LANES, STEM_LANES))):
+        given = operand[half]
+        for chunk in range(start, stop, 256):
+            lanes = min(256, stop - chunk)
+            at = chunk - start
+            product = dot(given, basis[half, :, at : at + lanes])
+            for part in range(0, lanes, 128):
+                number = turn % 4
+                turn += 1
+                wide[number, 8 : 8 + rows] = product[:, part : part + 128]
+                to_lane = chunk + part
+                for first, to, count in blocks:
+                    at_row = 8 + first
+                    stem_in[to : to + count, to_lane : to_lane + 128] = jnp.where(
+                        above,
+                        wide[number, at_row - 1 : at_row - 1 + count],
+                        jnp.where(
+                            here,
+                            wide[number, at_row : at_row + count],
+                            wide[number, at_row + 1 : at_row + 1 + count],
+                        ),
+                    ).astype(BF16)
 
 
 def stem(stem_in, stem_right, shift, features, store_pooled):
@@ -251,10 +290,10 @@
     w_down, w_query, w_key, w_value, w_attn_out, w_up = weights
     zeta = silu(dot(pooled.astype(BF16), w_down[...]))
     scale = lax.rsqrt(jnp.mean(zeta * zeta, axis=-1, keepdims=True) + NORM_EPS)
-    normed = (zeta * scale).astype(BF16)
-    query = dot(normed, w_query[...]).astype(BF16)
-    keyed = dot(normed, w_key[...]).astype(BF16)
-    valued = dot(normed, w_value[...]).astype(BF16)
+    given = zeta.astype(BF16)
+    query = (scale * HEAD_DIM**-0.5 * dot(given, w_query[...])).astype(BF16)
+    keyed = (scale * dot(given, w_key[...])).astype(BF16)
+    valued = (scale * dot(given, w_value[...])).astype(BF16)
     head_of_row = lax.broadcasted_iota(jnp.int32, (HEADS * TOKENS, CH2), 0) // TOKENS
     head_of_channel = lax.broadcasted_iota(jnp.int32, (HEADS * TOKENS, CH2), 1) // HEAD_DIM
     own_head = (head_of_row == head_of_channel).astype(F32).astype(BF16)
@@ -267,7 +306,7 @@
         values = jnp.concatenate([valued[rows]] * HEADS, axis=0) * own_head
         scores = lax.dot_general(
             query[rows], keys, (((1,), (1,)), ((), ())), preferred_element_type=F32
-        ) * (HEAD_DIM**-0.5)
+        )
         top = jnp.zeros_like(scores)
         for head in range(HEADS):
             inside = head_of_lane == head
@@ -320,40 +359,70 @@
     return field * jnp.minimum(row + 1, DOM - row).astype(F32)
 
 
+def convolve(plans, group_rows, lifted, active, halves, padded, out_right, total):
+    groups = active.shape[0]
+    each = len(plans) // groups
+    for group in range(groups):
+        base = 0
+        for number in range(each * group, each * group + each):
+            first, stop, sources = plans[number][:3]
+            activate(number, sources, first, lifted, active.at[group], base)
+            base += (stop - first) * 8
+        halves[group] = dot(active[group], out_right[...])
+    for group in range(groups):
+        base = 0
+        for number in range(each * group, each * group + each):
+            first, stop, _, to, start, end, counted = plans[number]
+            rows = (stop - first) * 8
+            field = predict(
+                halves[group, base : base + rows],
+                halves[group, group_rows + base : group_rows + base + rows],
+                first,
+                stop,
+                padded.at[number % 2],
+            )[start:end]
+            if counted is not True:
+                field = jnp.where(counted, field, 0.0)
+            span = pl.ds(to, end - start)
+            total[span] = total[span] + field
+            base += rows
+
+
 def own_kernel(
-    noisy, mean_field, mixes, along, levels, basis, stem_right, w_out, place, *refs
+    held_in, noisy, mean_field, mixes, along, levels, basis, stem_right, out_right, *refs
 ):
-    loaded, kept = refs[:7], refs[7:14]
-    features, pooled, right_out = refs[14:17]
-    w_out_v, place_v, operand, wide, stem_in, sems = refs[17:]
-    copies = fetch(sems, [(w_out, w_out_v), (place, place_v)] + list(zip(loaded, kept)))
-    c_in = levels[4:5].reshape(1, 1, 128)
-    operand[:, 0:128] = (c_in * noisy[...]).astype(BF16).reshape(OWN_ROWS, 128)
-    operand[:, 128:256] = mean_field[...].astype(BF16).reshape(OWN_ROWS, 128)
-    operand[:, 256:384] = interpolate(mixes, SLOTS * BR, along)
+    weights = refs[:6]
+    features, pooled_out, total = refs[6:9]
+    operand, wide, stem_in, pooled, lifted, active, halves, padded = refs[9:]
+    held = held_in[0]
+    assemble(
+        operand,
+        levels[4:5] * noisy[...].reshape(OWN_ROWS, 128),
+        mean_field[...].reshape(OWN_ROWS, 128),
+        interpolate(mixes, SLOTS * BR, along),
+    )
     widen(operand, basis, [(0, 0, OWN_ROWS)], wide, stem_in)
+    pooled[0:8] = jnp.zeros((8, CH), F32)
+    pooled[8 + OWN_TOKENS :] = jnp.zeros((8, CH), F32)
+    total[...] = jnp.zeros_like(total)
 
     def store_pooled(block_col, value):
-        pooled[pl.ds(block_col, OWN_ROWS // 8, stride=4)] = value
+        pooled[pl.ds(8 + block_col, OWN_ROWS // 8, stride=4)] = value
 
     stem(stem_in, stem_right, levels[0:1], features, store_pooled)
-    for copy in copies[0:2]:
-        copy.wait()
-    weights = w_out_v[...]
-    for cell in range(HALF):
-        right_out[cell * CH : (cell + 1) * CH] = lax.dot_general(
-            weights,
-            place_v[:, cell * 256 : (cell + 1) * 256],
-            (((0,), (0,)), ((), ())),
-            preferred_element_type=F32,
-        ).astype(BF16)
-    for copy in copies[2:]:
-        copy.wait()
+    pooled_out[...] = pooled[8 : 8 + OWN_TOKENS]
+    inner = range(1, SLOTS - 1)
+    lifted[...] = bottleneck(pooled[...], [16 * patch for patch in inner], weights)
+    plans = []
+    for patch in inner:
+        start = P_SIZE * patch - M
+        plans.append((0, 8, [(features, start, DOM)], start, 0, 64, patch <= held - 2))
+    convolve(plans, 2 * DOM, lifted, active, halves, padded, out_right, total)
 
 
 def main_kernel(
-    held_in, noisy, mean_field, first_in, second_in, mix_own, levels, along, basis, stem_right,
-    pooled_own, features, w_down, w_query, w_key, w_value, w_attn_out, w_up, out_right,
+    held_in, sigma_next, noisy, mean_field, second_in, first_in, mix_own, levels, along, basis, stem_right,
+    pooled_own, features, total_own, w_down, w_query, w_key, w_value, w_attn_out, w_up, out_right,
     denoised_out, next_out,
     state_rows, mean_rows, mixes, operand, wide, stem_in, ends, pooled, lifted, active, halves,
     padded, total,
@@ -389,11 +458,12 @@
         take(first_in, 0, 0, 0)
         take(second_in, 1, 32, 40)
 
-    for side in range(2):
-        span = slice(SIDE_SPAN * side, SIDE_SPAN * (side + 1))
-        operand[span, 0:128] = state_rows[side, 8 : 8 + SIDE_SPAN].astype(BF16)
-        operand[span, 128:256] = mean_rows[side, 8 : 8 + SIDE_SPAN].astype(BF16)
-    operand[:, 256:384] = interpolate(mixes, 2 * SIDE_PATCHES * BR, along)
+    assemble(
+        operand,
+        state_rows[:, 8 : 8 + SIDE_SPAN].reshape(2 * SIDE_SPAN, 128),
+        mean_rows[:, 8 : 8 + SIDE_SPAN].reshape(2 * SIDE_SPAN, 128),
+        interpolate(mixes, 2 * SIDE_PATCHES * BR, along),
+    )
     widen(
         operand, basis, [(8, 0, SIDE_ROWS), (SIDE_SPAN + 8, SIDE_ROWS, SIDE_ROWS)], wide, stem_in
     )
@@ -405,9 +475,6 @@
     stem(stem_in, stem_right, levels[0:1], ends, store_pooled)
     pooled[32:48] = pooled_own[8:24]
     pooled[48:64] = pooled_own[pl.ds(pl.multiple_of(16 * held - 24, 8), 16)]
-    pooled[96:104] = jnp.zeros((8, CH), F32)
-    pooled[104:200] = pooled_own[...]
-    pooled[200:208] = jnp.zeros((8, CH), F32)
 
     @pl.when(jnp.logical_not(has_left))
     def _():
@@ -420,48 +487,18 @@
         pooled[72:96] = jnp.zeros((24, CH), F32)
 
     lifted[...] = bottleneck(
-        pooled[...],
-        [0, 16, 112, 128, 144, 160, 48, 64],
-        (w_down, w_query, w_key, w_value, w_attn_out, w_up),
+        pooled[...], [0, 16, 48, 64], (w_down, w_query, w_key, w_value, w_attn_out, w_up)
     )
     near = pl.multiple_of(P_SIZE * held - 48, 16)
     last = pl.multiple_of(P_SIZE * held - M, 16)
     plans = [
         (4, 8, [(ends, 32, 32)], 0, 16, 32, has_left),
         (0, 8, [(ends, 32, 32), (features, 16, 32)], 0, 16, 64, True),
-    ]
-    for patch in range(1, SLOTS - 1):
-        start = P_SIZE * patch - M
-        plans.append((0, 8, [(features, start, DOM)], start, 0, 64, patch <= held - 2))
-    plans += [
         (0, 8, [(features, near, 32), (ends, 64, 32)], near, 0, 48, True),
         (0, 4, [(ends, 64, 32)], last, 0, 16, has_right),
     ]
-    total[...] = jnp.zeros_like(total)
-    for group in range(2):
-        base = 0
-        for number in range(4 * group, 4 * group + 4):
-            first, stop, sources = plans[number][:3]
-            activate(number, sources, first, lifted, active.at[group], base)
-            base += (stop - first) * 8
-        halves[group] = dot(active[group], out_right[...])
-    for group in range(2):
-        base = 0
-        for number in range(4 * group, 4 * group + 4):
-            first, stop, _, to, start, end, counted = plans[number]
-            rows = (stop - first) * 8
-            field = predict(
-                halves[group, base : base + rows],
-                halves[group, GROUP_ROWS + base : GROUP_ROWS + base + rows],
-                first,
-                stop,
-                padded.at[number % 2],
-            )[start:end]
-            if counted is not True:
-                field = jnp.where(counted, field, 0.0)
-            span = pl.ds(to, end - start)
-            total[span] = total[span] + field
-            base += rows
+    total[...] = total_own[...]
+    convolve(plans, 96, lifted, active, halves, padded, out_right, total)
 
     slot = lax.broadcasted_iota(jnp.int32, (SLOTS, P_SIZE, 128), 0)
     row = lax.broadcasted_iota(jnp.int32, (SLOTS, P_SIZE, 128), 1)
@@ -475,7 +512,8 @@
     blended = total[...].reshape(SLOTS, P_SIZE, 128) / norm.astype(F32)
     state = noisy[...]
     denoised = levels[1:2].reshape(1, 1, 128) * state + levels[2:3].reshape(1, 1, 128) * blended
-    stepped = state + levels[3:4].reshape(1, 1, 128) * (state - denoised)
+    step = sigma_next[0] * levels[3:4].reshape(1, 1, 128) - 1.0
+    stepped = state + step * (state - denoised)
     live = slot < held
     denoised_out[...] = jnp.where(live, denoised, 0.0)
     next_out[...] = jnp.where(live, stepped, 0.0)
@@ -514,9 +552,9 @@
         return [pltpu.VMEM(shape, dtype) for shape, dtype in shapes]
 
     state = noisy[0]
-    copies = pl.pallas_call(
+    mixed = pl.pallas_call(
         mix_kernel,
-        out_shape=pltpu.VMEM((MEMBERS, 8, 128), F32),
+        out_shape=pltpu.VMEM((8, 128), F32),
         in_specs=[hbm] * 4,
         out_specs=vmem,
         scratch_shapes=[
@@ -529,73 +567,93 @@
         compiler_params=limit,
         name="mix",
     )(*in_hbm(src.T, widx.T, table, coarse))
-    cells = lax.all_to_all(copies, "member", 0, 0, tiled=True)
+    partners = lax.ppermute(mixed, "member", [(i, i ^ 1) for i in range(MEMBERS)])
+    merged = pl.pallas_call(
+        merge_kernel,
+        out_shape=pltpu.VMEM((16, 128), F32),
+        in_specs=[vmem] * 2,
+        out_specs=vmem,
+        compiler_params=limit,
+        name="merge",
+    )(mixed, partners)
+    chips = [merged] + [
+        lax.ppermute(merged, "member", [(i, i ^ (2 * distance)) for i in range(MEMBERS)])
+        for distance in DISTANCES
+    ]
 
     basis, along, along_side, place = (jnp.asarray(array) for array in tables())
-    loaded = [state, mean_field, basis, along]
+    loaded = [state, mean_field, basis, along, along_side]
+    loaded += [w_down, w_query, w_key, w_value, w_attn_out, w_up]
     prepared = pl.pallas_call(
         prepare_kernel,
         out_shape=in_vmem(*((array.shape, array.dtype) for array in loaded))
         + [jax.ShapeDtypeStruct((8,), jnp.int32)]
         + in_vmem(
-            ((PIECE, 128), BF16), ((PIECE, 128), BF16), ((8, 128), F32), ((CH2, CH2), BF16)
+            ((PIECE, 128), BF16),
+            ((PIECE, 128), BF16),
+            ((8, 128), F32),
+            ((CH2, CH2), BF16),
+            ((HALF_LANES, 256), BF16),
         ),
-        in_specs=[smem] * 3 + [hbm] * 6,
-        out_specs=[vmem] * 4 + [smem] + [vmem] * 4,
+        in_specs=[smem] * 2 + [hbm] * (4 + len(loaded)),
+        out_specs=[vmem] * len(loaded) + [smem] + [vmem] * 5,
         scratch_shapes=[
             pltpu.VMEM(noise_embed.shape, F32),
             pltpu.VMEM(w_stem.shape, BF16),
+            pltpu.VMEM(w_out.T.shape, BF16),
+            pltpu.VMEM(place.shape, BF16),
             pltpu.VMEM((256, 256), F32),
-            pltpu.SemaphoreType.DMA((6,)),
+            pltpu.SemaphoreType.DMA((4 + len(loaded),)),
         ],
         compiler_params=limit,
         cost_estimate=pl.CostEstimate(flops=10**9, bytes_accessed=8 * 10**6, transcendentals=0),
         name="prepare",
-    )(counts, sigma, sigma_next, *in_hbm(noise_embed, w_stem, *loaded))
-    state, mean_field, basis, along, held, first, second, levels, stem_right = prepared
-
-    first, second, mix_own = pl.pallas_call(
+    )(counts, sigma, *in_hbm(noise_embed, w_stem, w_out.T, place, *loaded))
+    state, mean_field, basis, along, along_side = prepared[:5]
+    weights = prepared[5:11]
+    held, first, second, levels, stem_right, out_right = prepared[11:]
+
+    second, first, mix_own = pl.pallas_call(
         pack_kernel,
         out_shape=in_vmem(
             ((PIECE, 128), BF16), ((PIECE, 128), BF16), ((SLOTS * MEMBERS, 128), F32)
         ),
-        in_specs=[smem] + [vmem] * 3,
+        in_specs=[smem] + [vmem] * 6,
         out_specs=[vmem] * 3,
+        scratch_shapes=[pltpu.VMEM((MEMBERS, 8, 128), F32)],
         compiler_params=limit,
         name="pack",
-    )(held, cells, first, second)
+    )(held, *chips, first, second)
     pairs = [(i, i ^ 1) for i in range(owners)]
     others = []
     for i in range(1, owners - 1, 2):
         others += [(i, i + 1), (i + 1, i)]
+    second = lax.ppermute(second, "space", others)
     first = lax.ppermute(first, "space", pairs)
-    second = lax.ppermute(second, "space", others)
-
-    loaded = [along_side, w_down, w_query, w_key, w_value, w_attn_out, w_up]
-    *loaded, features, pooled, out_right = pl.pallas_call(
+
+    features, pooled, total = pl.pallas_call(
         own_kernel,
-        out_shape=in_vmem(*((array.shape, array.dtype) for array in loaded))
-        + in_vmem(
-            ((OWN_ROWS, W * CH), BF16), ((OWN_TOKENS, CH), F32), ((HALF_LANES, 256), BF16)
+        out_shape=in_vmem(
+            ((OWN_ROWS, W * CH), BF16), ((OWN_TOKENS, CH), F32), ((OWN_ROWS, 128), F32)
         ),
-        in_specs=[vmem] * 7 + [hbm] * 9,
-        out_specs=[vmem] * 10,
+        in_specs=[smem] + [vmem] * 14,
+        out_specs=[vmem] * 3,
         scratch_shapes=[
-            pltpu.VMEM(w_out.T.shape, BF16),
-            pltpu.VMEM(place.shape, BF16),
-            pltpu.VMEM((OWN_ROWS, 384), BF16),
+            pltpu.VMEM((2, OWN_ROWS, 256), BF16),
             pltpu.VMEM((4, OWN_ROWS + 16, 128), F32),
             pltpu.VMEM((OWN_ROWS, STEM_LANES), BF16),
-            pltpu.SemaphoreType.DMA((9,)),
+            pltpu.VMEM((OWN_TOKENS + 16, CH), F32),
+            pltpu.VMEM((4 * TOKENS, CH), F32),
+            pltpu.VMEM((2, 4 * DOM, HALF_LANES), BF16),
+            pltpu.VMEM((2, 4 * DOM, 256), F32),
+            pltpu.VMEM((2, 80, 384), F32),
         ],
         compiler_params=limit,
         cost_estimate=pl.CostEstimate(flops=10**9, bytes_accessed=10**7, transcendentals=2 * 10**6),
         name="own",
     )(
-        state, mean_field, mix_own, along, levels, basis, stem_right,
-        *in_hbm(w_out.T, place, *loaded),
-    )
-    along_side, *weights = loaded
+        held, state, mean_field, mix_own, along, levels, basis, stem_right, out_right, *weights
+    )
 
     denoised, stepped = pl.pallas_call(
         main_kernel,
@@ -603,20 +661,20 @@
             jax.ShapeDtypeStruct((SLOTS, P_SIZE, 128), F32),
             jax.ShapeDtypeStruct((SLOTS, P_SIZE, 128), F32),
         ),
-        in_specs=[smem] + [vmem] * 18,
+        in_specs=[smem] * 2 + [vmem] * 19,
         out_specs=(vmem, vmem),
         scratch_shapes=[
             pltpu.VMEM((2, 96, 128), F32),
             pltpu.VMEM((2, 96, 128), F32),
             pltpu.VMEM((64, 128), F32),
-            pltpu.VMEM((2 * SIDE_SPAN, 384), BF16),
+            pltpu.VMEM((2, 2 * SIDE_SPAN, 256), BF16),
             pltpu.VMEM((4, 2 * SIDE_SPAN + 16, 128), F32),
             pltpu.VMEM((2 * SIDE_ROWS, STEM_LANES), BF16),
             pltpu.VMEM((2 * SIDE_ROWS, W * CH), BF16),
-            pltpu.VMEM((208, CH), F32),
-            pltpu.VMEM((DOMAINS * TOKENS, CH), F32),
-            pltpu.VMEM((2, 2 * GROUP_ROWS, HALF_LANES), BF16),
-            pltpu.VMEM((2, 2 * GROUP_ROWS, 256), F32),
+            pltpu.VMEM((96, CH), F32),
+            pltpu.VMEM((4 * TOKENS, CH), F32),
+            pltpu.VMEM((2, 2 * 96, HALF_LANES), BF16),
+            pltpu.VMEM((2, 2 * 96, 256), F32),
             pltpu.VMEM((2, 80, 384), F32),
             pltpu.VMEM((OWN_ROWS, 128), F32),
         ],
@@ -624,8 +682,8 @@
         cost_estimate=pl.CostEstimate(flops=10**9, bytes_accessed=10**7, transcendentals=2 * 10**6),
         name="main",
     )(
-        held, state, mean_field, first, second, mix_own, levels, along_side, basis, stem_right,
-        pooled, features, *weights, out_right,
+        held, sigma_next, state, mean_field, second, first, mix_own, levels, along_side, basis, stem_right,
+        pooled, features, total, *weights, out_right,
     )
     return denoised[None], stepped[None]
 

time: 30.3 us -> 27.8 us (0.917)
  the two profiles are of different devices: /device:TPU:128 before, /device:TPU:112 now
where the time goes in v3:
time: 27.8 us; the launch traced here: 27.6 us
  Pallas kernels  13.9 us (50%)
  starting transfers between devices  10.4 us (37%)
  between operations  2.65 us (10%)
  waiting for transfers between devices  0.66 us (2%)
    pallas_call x1, Pallas kernels, shards(): pl.pallas_call(own_kernel, out_shape=in_vmem(((OWN_ROWS, W * CH), BF16),...  5.08 us
    pallas_call x1, Pallas kernels, shards(): pl.pallas_call(main_kernel, out_shape=(jax.ShapeDtypeStruct((SLOTS, P_SIZ...  4.98 us
    ppermute x3, starting transfers between devices, shards(): lax.ppermute(merged, 'member', [(i, i ^ 2 * distance) for i in range(MEMB...  4.25 us
    ppermute x1, starting transfers between devices, shards(): first = lax.ppermute(first, 'space', pairs)  3.71 us
    pallas_call x1, Pallas kernels, shards(): pl.pallas_call(prepare_kernel, out_shape=in_vmem(*((array.shape, array.dt...  2.4 us
    ppermute x1, starting transfers between devices, shards(): second = lax.ppermute(second, 'space', others)  2.36 us
    pallas_call x1, Pallas kernels, shards(): pl.pallas_call(mix_kernel, out_shape=pltpu.VMEM((8, 128), F32), in_specs=...  0.8 us
    ppermute x3, waiting for transfers between devices, shards(): lax.ppermute(merged, 'member', [(i, i ^ 2 * distance) for i in range(MEMB...  0.66 us
  transfers between devices with their start and end apart: 6, of which 1 were waited for; matrix products, arithmetic and copies ran while one was open for 0% of the time, Pallas kernels for 27%

profile of v3, /device:TPU:112, one launch (start us, length us, event | category | flops | bytes accessed | tf_op | source)
XLA Modules:
  0.0 27.6 jit_solution(14914549655793827305)
XLA Ops:
  0.6 0.8 %mix.1.mixed = f32[8,128]{1,0:T(8,128)S(1)} custom-call(s32[4,6]{1,0:T(4,128)} %bitcast.6, s32[4,6]{1,0:T(4,128)} %bitcast.7, f32[16]{0:T(128)} %table.1, f32[8,24]{1,0:T(8,128)} %coarse.1), custom_call_target="tpu_custom_call" | custom-call | tf_op jit(solution)/shard_map/mix/pallas_call | solution.py:555
  1.4 0.1 collective-permute-start
  2.8 0.0 collective-permute-done.partners
  2.9 3.1 %collective-permute-start.3 = (f32[16,128]{1,0:T(8,128)S(1)}, f32[16,128]{1,0:T(8,128)S(1)}, u32[]{:S(2)}, u32[]{:S(2)}) collective-permute-start(f32[16,128]{1,0:T(8,128)S(1)} %merge.1.chip0), channel_id=1, source_target_pairs={{0,128},{32,160},{64,192},{96,224},{128,0},{160,32},{192,64},{224,... | collective-permute-start | bytes 24584 | tf_op jit(solution)/shard_map/ppermute | solution.py:580
  6.0 1.1 %collective-permute-start.2 = (f32[16,128]{1,0:T(8,128)S(1)}, f32[16,128]{1,0:T(8,128)S(1)}, u32[]{:S(2)}, u32[]{:S(2)}) collective-permute-start(f32[16,128]{1,0:T(8,128)S(1)} %merge.1.chip0), channel_id=1, source_target_pairs={{0,192},{32,224},{64,128},{96,160},{128,64},{160,96},{192,0},{224,... | collective-permute-start | bytes 24584 | tf_op jit(solution)/shard_map/ppermute | solution.py:580
  7.1 0.0 collective-permute-start.1
  7.1 2.4 %prepare.1 = (f32[6,32,128]{2,1,0:T(8,128)S(1)}, f32[6,32,128]{2,1,0:T(8,128)S(1)}, bf16[2,256,1152]{2,1,0:T(8,128)(2,1)S(1)}, bf16[192,48]{1,0:T(8,128)(2,1)S(1...) custom-call(s32[1]{0:T(128)S(6)} %copy.24.counts, ...), custom_call_target="tpu_custom_call" | custom-call | flops 1000000000 | bytes 8000000 | tf_op jit(solution)/shard_map/prepare/pallas_call | solution.py:587
  10.2 0.0 collective-permute-done.3.chip3
  10.2 0.7 %collective-permute-done.2.chip2 = f32[16,128]{1,0:T(8,128)S(1)} collective-permute-done((f32[16,128]{1,0:T(8,128)S(1)}, f32[16,128]{1,0:T(8,128)S(1)}, u32[]{:S(2)}, u32[]{:S(2)}) %collective-permute-start.2) | collective-permute-done | bytes 8224 | tf_op jit(solution)/shard_map/ppermute | solution.py:580
  10.8 0.0 collective-permute-done.1.chip1
  10.8 0.6 %pack.1 = (bf16[160,128]{1,0:T(8,128)(2,1)S(1)}, bf16[160,128]{1,0:T(8,128)(2,1)S(1)}, f32[48,128]{1,0:T(8,128)S(1)}) custom-call(s32[8]{0:T(128)S(1)} %get-tuple-element.27.held_in, f32[16,128]{1,0:T(8,128)S(1)} %merge.1.chip0, f32[16,128]{1,0:T(8,128)S(1)} %collective-permute-done.1.chip1, f32[16,128]{1,0:T(8,128)S(1)} %collective-permute-done.2.chip2, ...), custom_call_target="tpu_custom_call" | custom-call | tf_op jit(solution)/shard_map/pack/pallas_call | solution.py:616
  11.4 2.4 %collective-permute-start.4 = (bf16[160,128]{1,0:T(8,128)(2,1)S(1)}, bf16[160,128]{1,0:T(8,128)(2,1)S(1)}, u32[]{:S(2)}, u32[]{:S(2)}) collective-permute-start(bf16[160,128]{1,0:T(8,128)(2,1)S(1)} %get-tuple-element.32), channel_id=1, source_target_pairs={{1,2},{2,1},{3,4},{4,3},{5,6},{6,5},{7,8},{8,7},{9,10},{10,9},{11,... | collective-permute-start | bytes 122888 | tf_op jit(solution)/shard_map/ppermute | solution.py:631
  13.8 3.7 %collective-permute-start.5 = (bf16[160,128]{1,0:T(8,128)(2,1)S(1)}, bf16[160,128]{1,0:T(8,128)(2,1)S(1)}, u32[]{:S(2)}, u32[]{:S(2)}) collective-permute-start(bf16[160,128]{1,0:T(8,128)(2,1)S(1)} %get-tuple-element.33), channel_id=1, source_target_pairs={{0,1},{1,0},{2,3},{3,2},{4,5},{5,4},{6,7},{7,6},{8,9},{9,8},{10,11... | collective-permute-start | bytes 122888 | tf_op jit(solution)/shard_map/ppermute | solution.py:632
  17.5 5.1 %own.1 = (bf16[192,4096]{1,0:T(8,128)(2,1)S(1)}, f32[96,128]{1,0:T(8,128)S(1)}, f32[192,128]{1,0:T(8,128)S(1)}) custom-call(s32[8]{0:T(128)S(1)} %get-tuple-element.27.held_in, f32[6,32,128]{2,1,0:T(8,128)S(1)} %get-tuple-element.28.noisy, f32[6,32,128]{2,1,0:T(8,128)S(1)} %get-tuple-element.29.mean_field, f32[48,128]{1,0:T(8,128)S(1)} %get-tuple-element.34.mixes.mix_own, ...), custom_call_target="tpu_custom_call" | custom-call | flops 1000000000 | bytes 10000000 | tf_op jit(solution)/shard_map/own/pallas_call | solution.py:634
  22.6 0.0 collective-permute-done.4.second_in
  22.6 0.0 collective-permute-done.5.first_in
  22.6 5.0 %main.1 = (f32[6,32,128]{2,1,0:T(8,128)}, f32[6,32,128]{2,1,0:T(8,128)}) custom-call(s32[8]{0:T(128)S(1)} %get-tuple-element.27.held_in, f32[1]{0:T(128)S(6)} %copy.26.sigma_next, f32[6,32,128]{2,1,0:T(8,128)S(1)} %get-tuple-element.28.noisy, f32[6,32,128]{2,1,0:T(8,128)S(1)} %get-tuple-element.29.mean_field, ...), custom_call_target="tpu_custom_call" | custom-call | flops 1000000000 | bytes 10000000 | tf_op jit(solution)/shard_map/main/pallas_call | solution.py:658
  (1 shorter events, 0.0 us)
Async XLA Ops:
  1.4 1.4 %collective-permute-start = (f32[8,128]{1,0:T(8,128)S(1)}, f32[8,128]{1,0:T(8,128)S(1)}, u32[]{:S(2)}, u32[]{:S(2)}) collective-permute-start(f32[8,128]{1,0:T(8,128)S(1)} %mix.1.mixed), channel_id=1, source_target_pairs={{0,32},{32,0},{64,96},{96,64},{128,160},{160,128},{192,224},{224,1... | collective-permute-start | bytes 12296 | tf_op jit(solution)/shard_map/ppermute | solution.py:570
  2.9 7.3 %collective-permute-start.3 = (f32[16,128]{1,0:T(8,128)S(1)}, f32[16,128]{1,0:T(8,128)S(1)}, u32[]{:S(2)}, u32[]{:S(2)}) collective-permute-start(f32[16,128]{1,0:T(8,128)S(1)} %merge.1.chip0), channel_id=1, source_target_pairs={{0,128},{32,160},{64,192},{96,224},{128,0},{160,32},{192,64},{224,... | collective-permute-start | bytes 24584 | tf_op jit(solution)/shard_map/ppermute | solution.py:580
  6.0 4.9 %collective-permute-start.2 = (f32[16,128]{1,0:T(8,128)S(1)}, f32[16,128]{1,0:T(8,128)S(1)}, u32[]{:S(2)}, u32[]{:S(2)}) collective-permute-start(f32[16,128]{1,0:T(8,128)S(1)} %merge.1.chip0), channel_id=1, source_target_pairs={{0,192},{32,224},{64,128},{96,160},{128,64},{160,96},{192,0},{224,... | collective-permute-start | bytes 24584 | tf_op jit(solution)/shard_map/ppermute | solution.py:580
  7.1 3.7 %collective-permute-start.1 = (f32[16,128]{1,0:T(8,128)S(1)}, f32[16,128]{1,0:T(8,128)S(1)}, u32[]{:S(2)}, u32[]{:S(2)}) collective-permute-start(f32[16,128]{1,0:T(8,128)S(1)} %merge.1.chip0), channel_id=1, source_target_pairs={{0,64},{32,96},{64,0},{96,32},{128,192},{160,224},{192,128},{224,1... | collective-permute-start | bytes 24584 | tf_op jit(solution)/shard_map/ppermute | solution.py:580
  11.4 11.2 %collective-permute-start.4 = (bf16[160,128]{1,0:T(8,128)(2,1)S(1)}, bf16[160,128]{1,0:T(8,128)(2,1)S(1)}, u32[]{:S(2)}, u32[]{:S(2)}) collective-permute-start(bf16[160,128]{1,0:T(8,128)(2,1)S(1)} %get-tuple-element.32), channel_id=1, source_target_pairs={{1,2},{2,1},{3,4},{4,3},{5,6},{6,5},{7,8},{8,7},{9,10},{10,9},{11,... | collective-permute-start | bytes 122888 | tf_op jit(solution)/shard_map/ppermute | solution.py:631
  13.8 8.8 %collective-permute-start.5 = (bf16[160,128]{1,0:T(8,128)(2,1)S(1)}, bf16[160,128]{1,0:T(8,128)(2,1)S(1)}, u32[]{:S(2)}, u32[]{:S(2)}) collective-permute-start(bf16[160,128]{1,0:T(8,128)(2,1)S(1)} %get-tuple-element.33), channel_id=1, source_target_pairs={{0,1},{1,0},{2,3},{3,2},{4,5},{5,4},{6,7},{7,6},{8,9},{9,8},{10,11... | collective-permute-start | bytes 122888 | tf_op jit(solution)/shard_map/ppermute | solution.py:632

commit v4 on v3

--- a/solution.py
+++ b/solution.py
@@ -47,6 +47,8 @@
 HALF = W // 2
 HALF_LANES = HALF * CH
 TAP_LANES = (HALF + 2) * VARS
+EARLY = 3
+LATE = SLOTS - 2 - EARLY
 VMEM_LIMIT = 24 * 1024 * 1024
 
 
@@ -84,6 +86,7 @@
         basis[half, 0:64, :count] = noisy[cells].reshape(64, STEM_LANES)[:, lanes]
         basis[half, 64:128, :count] = mean[cells].reshape(64, STEM_LANES)[:, lanes]
         basis[half, 128:224, :count] = across.reshape(96, STEM_LANES)[:, lanes]
+        basis[half, 232, :count] = np.tile(np.arange(CELL) >= 3 * CIN, W + 2)[lanes]
     basis[0, 224:228] = noisy[HALF].reshape(4, STEM_LANES)[:, :LEFT_LANES]
     basis[0, 228:232] = mean[HALF].reshape(4, STEM_LANES)[:, :LEFT_LANES]
     along = along_rows(range(OWN_ROWS), SLOTS).reshape(OWN_ROWS, 2 * SLOTS * BR)
@@ -136,11 +139,11 @@
     merged_out[pl.ds(pl.multiple_of(8 - 8 * core, 8), 8)] = partners[...]
 
 
-def prepare_kernel(counts, sigma, noise_embed, w_stem, w_out, place, *refs):
-    loaded, kept, rest = refs[:11], refs[11:22], refs[22:]
+def prepare_kernel(counts, sigma, noise_embed, w_stem, w_out, place, w_value, w_attn_out, *refs):
+    loaded, kept, rest = refs[:9], refs[9:18], refs[18:]
     (
-        held_out, first_out, second_out, levels_out, stem_out, right_out,
-        embed_v, w_stem_v, w_out_v, place_v, stem_f32, sems,
+        first_out, second_out, levels_out, stem_out, right_out, joint_out,
+        value_v, attn_v, embed_v, w_stem_v, w_out_v, place_v, stem_f32, sems,
     ) = rest
     noisy_v, mean_v = kept[:2]
     copies = fetch(
@@ -152,6 +155,8 @@
             (w_stem, w_stem_v),
             (w_out, w_out_v),
             (place, place_v),
+            (w_value, value_v),
+            (w_attn_out, attn_v),
         ]
         + list(zip(loaded[2:], kept[2:])),
     )
@@ -159,7 +164,6 @@
     for copy in copies[0:3]:
         copy.wait()
     held = counts[0]
-    held_out[0] = held
     level = jnp.full((1, 128), sigma[0], F32)
     variance = level * level + SIGMA_DATA * SIGMA_DATA
     c_in = lax.rsqrt(variance)
@@ -185,6 +189,13 @@
                     at = (3 * row_tap + col_tap) * CIN
                     to = cell * CELL + row_tap * CIN
                     stem_f32[to : to + CIN, target * CH : (target + 1) * CH] = stem_taps[at : at + CIN]
+    part = levels_out[0:1]
+    for number in range(3):
+        high = part.astype(BF16).astype(F32)
+        for target in range(2):
+            to = (target + 1) * CELL + 3 * CIN + number
+            stem_f32[to : to + 1, target * CH : (target + 1) * CH] = high
+        part = part - high
     stem_out[...] = stem_f32[...].astype(BF16)
     for copy in copies[4:6]:
         copy.wait()
@@ -195,10 +206,14 @@
         ).astype(BF16)
     for copy in copies[6:]:
         copy.wait()
-
-
-def pack_kernel(held_in, chip0, chip1, chip2, chip3, first_in, second_in, second_out, first_out, mix_out, cells):
-    held = held_in[0]
+    after = dot(attn_v[...], kept[8][...]).astype(BF16)
+    for head in range(HEADS):
+        span = slice(head * HEAD_DIM, (head + 1) * HEAD_DIM)
+        joint_out[:, head * CH : (head + 1) * CH] = dot(value_v[:, span], after[span]).astype(BF16)
+
+
+def pack_kernel(counts, chip0, chip1, chip2, chip3, first_in, second_in, second_out, first_out, mix_out, cells):
+    held = counts[0]
     chip = lax.axis_index("member") // 2
     for distance, given in zip((0, *DISTANCES), (chip0, chip1, chip2, chip3)):
         member = 2 * jnp.bitwise_xor(chip, distance)
@@ -232,9 +247,12 @@
     left = lane < 64
     operand[0, :, 0:128] = jnp.where(left, state, pltpu.roll(mean, 64, 1)).astype(BF16)
     operand[1, :, 0:128] = jnp.where(left, pltpu.roll(state, 64, 1), mean).astype(BF16)
-    operand[1, :, 128:256] = cond.astype(BF16)
+    one = lane == 104
+    operand[1, :, 128:256] = jnp.where(one, 1.0, cond).astype(BF16)
     more = jnp.where(lane < 100, pltpu.roll(state, 32, 1), pltpu.roll(mean, 36, 1))
-    operand[0, :, 128:256] = jnp.where(lane < 96, cond, jnp.where(lane < 104, more, 0.0)).astype(BF16)
+    operand[0, :, 128:256] = jnp.where(
+        lane < 96, cond, jnp.where(lane < 104, more, one.astype(F32))
+    ).astype(BF16)
 
 
 def widen(operand, basis, blocks, wide, stem_in):
@@ -270,15 +288,15 @@
                     ).astype(BF16)
 
 
-def stem(stem_in, stem_right, shift, features, store_pooled):
+def stem(stem_in, stem_right, features, store_pooled):
     rows = features.shape[0]
     for block_col in range(4):
         summed = jnp.zeros((rows, CH), F32)
         for cell_pair in range(4):
             number = block_col * 4 + cell_pair
-            raw = dot(stem_in[:, number * 128 : number * 128 + 256], stem_right[...])
+            halves = dot(stem_in[:, number * 128 : number * 128 + 256], stem_right[...])
             for part in range(2):
-                half = raw[:, part * CH : (part + 1) * CH] + shift
+                half = halves[:, part * CH : (part + 1) * CH]
                 feature = (0.5 * half) * (1.0 + jnp.tanh(half))
                 lane = number * 256 + part * CH
                 features[:, lane : lane + CH] = feature.astype(BF16)
@@ -287,23 +305,28 @@
 
 
 def bottleneck(pooled, starts, weights):
-    w_down, w_query, w_key, w_value, w_attn_out, w_up = weights
+    w_down, w_query, w_key, w_joint, w_up = weights
     zeta = silu(dot(pooled.astype(BF16), w_down[...]))
     scale = lax.rsqrt(jnp.mean(zeta * zeta, axis=-1, keepdims=True) + NORM_EPS)
     given = zeta.astype(BF16)
     query = (scale * HEAD_DIM**-0.5 * dot(given, w_query[...])).astype(BF16)
     keyed = (scale * dot(given, w_key[...])).astype(BF16)
-    valued = (scale * dot(given, w_value[...])).astype(BF16)
+    valued = (scale * dot(given, w_joint[...])).astype(BF16)
+    raised = dot(given, w_up[...])
     head_of_row = lax.broadcasted_iota(jnp.int32, (HEADS * TOKENS, CH2), 0) // TOKENS
     head_of_channel = lax.broadcasted_iota(jnp.int32, (HEADS * TOKENS, CH2), 1) // HEAD_DIM
     own_head = (head_of_row == head_of_channel).astype(F32).astype(BF16)
+    row = lax.broadcasted_iota(jnp.int32, (HEADS * TOKENS, HEADS * TOKENS), 0) // TOKENS
+    lane = lax.broadcasted_iota(jnp.int32, (HEADS * TOKENS, HEADS * TOKENS), 1) // TOKENS
+    same_head = (row == lane).astype(F32).astype(BF16)
     head_of_lane = lax.broadcasted_iota(jnp.int32, (TOKENS, HEADS * TOKENS), 1) // TOKENS
-    mixed_heads = []
-    residual = []
+    lifted = []
     for start in starts:
         rows = slice(start, start + TOKENS)
         keys = jnp.concatenate([keyed[rows]] * HEADS, axis=0) * own_head
-        values = jnp.concatenate([valued[rows]] * HEADS, axis=0) * own_head
+        values = jnp.concatenate(
+            [valued[rows, head * CH : (head + 1) * CH] for head in range(HEADS)], axis=0
+        )
         scores = lax.dot_general(
             query[rows], keys, (((1,), (1,)), ((), ())), preferred_element_type=F32
         )
@@ -312,12 +335,10 @@
             inside = head_of_lane == head
             largest = jnp.max(jnp.where(inside, scores, -jnp.inf), axis=1, keepdims=True)
             top = jnp.where(inside, largest, top)
-        weight = jnp.exp(scores - top).astype(BF16)
-        mixed_heads.append((dot(weight, values) / dot(weight, own_head)).astype(BF16))
-        residual.append(zeta[rows])
-    attended = jnp.concatenate(mixed_heads, axis=0)
-    resid = (jnp.concatenate(residual, axis=0) + dot(attended, w_attn_out[...])).astype(BF16)
-    return 0.5 * dot(resid, w_up[...])
+        weight = jnp.exp(scores - top)
+        weight = (weight / dot(weight.astype(BF16), same_head)).astype(BF16)
+        lifted.append(0.5 * (raised[rows] + dot(weight, values)))
+    return jnp.concatenate(lifted, axis=0)
 
 
 def activate(number, sources, first, lifted, active, base):
@@ -388,13 +409,21 @@
             base += rows
 
 
+def inner_plans(numbers, held):
+    plans = []
+    for patch in (number + 1 for number in numbers):
+        start = P_SIZE * patch - M
+        plans.append((0, 8, start, start, 0, 64, patch <= held - 2))
+    return plans
+
+
 def own_kernel(
-    held_in, noisy, mean_field, mixes, along, levels, basis, stem_right, out_right, *refs
+    counts, noisy, mean_field, mixes, along, levels, basis, stem_right, out_right, *refs
 ):
-    weights = refs[:6]
-    features, pooled_out, total = refs[6:9]
-    operand, wide, stem_in, pooled, lifted, active, halves, padded = refs[9:]
-    held = held_in[0]
+    weights = refs[:5]
+    features, pooled_out, lifted, total = refs[5:9]
+    operand, wide, stem_in, pooled, active, halves, padded = refs[9:]
+    held = counts[0]
     assemble(
         operand,
         levels[4:5] * noisy[...].reshape(OWN_ROWS, 128),
@@ -402,32 +431,33 @@
         interpolate(mixes, SLOTS * BR, along),
     )
     widen(operand, basis, [(0, 0, OWN_ROWS)], wide, stem_in)
+
     pooled[0:8] = jnp.zeros((8, CH), F32)
     pooled[8 + OWN_TOKENS :] = jnp.zeros((8, CH), F32)
-    total[...] = jnp.zeros_like(total)
 
     def store_pooled(block_col, value):
         pooled[pl.ds(8 + block_col, OWN_ROWS // 8, stride=4)] = value
 
-    stem(stem_in, stem_right, levels[0:1], features, store_pooled)
+    stem(stem_in, stem_right, features, store_pooled)
     pooled_out[...] = pooled[8 : 8 + OWN_TOKENS]
-    inner = range(1, SLOTS - 1)
-    lifted[...] = bottleneck(pooled[...], [16 * patch for patch in inner], weights)
-    plans = []
-    for patch in inner:
-        start = P_SIZE * patch - M
-        plans.append((0, 8, [(features, start, DOM)], start, 0, 64, patch <= held - 2))
-    convolve(plans, 2 * DOM, lifted, active, halves, padded, out_right, total)
+    lifted[...] = bottleneck(pooled[...], [16 * patch for patch in range(1, SLOTS - 1)], weights)
+    total[...] = jnp.zeros_like(total)
+    plans = [
+        (first, stop, [(features, start, DOM)], *rest)
+        for first, stop, start, *rest in inner_plans(range(EARLY), held)
+    ]
+    convolve(plans, EARLY * DOM, lifted, active, halves, padded, out_right, total)
 
 
 def main_kernel(
-    held_in, sigma_next, noisy, mean_field, second_in, first_in, mix_own, levels, along, basis, stem_right,
-    pooled_own, features, total_own, w_down, w_query, w_key, w_value, w_attn_out, w_up, out_right,
+    counts, sigma_next, noisy, mean_field, second_in, first_in, mix_own, levels, along, basis, stem_right,
+    pooled_own, features, lifted_own, total_own, w_down, w_query, w_key, w_joint, w_up, out_right,
     denoised_out, next_out,
     state_rows, mean_rows, mixes, operand, wide, stem_in, ends, pooled, lifted, active, halves,
-    padded, total,
+    padded, total, active_inner, halves_inner,
 ):
-    held = held_in[0]
+    held = counts[0]
+    weights = (w_down, w_query, w_key, w_joint, w_up)
     position = lax.axis_index("space")
     even = lax.rem(position, 2) == 0
     has_left = position > 0
@@ -472,7 +502,7 @@
         pooled[pl.ds(block_col, 8, stride=4)] = value[0:8]
         pooled[pl.ds(64 + block_col, 8, stride=4)] = value[8:16]
 
-    stem(stem_in, stem_right, levels[0:1], ends, store_pooled)
+    stem(stem_in, stem_right, ends, store_pooled)
     pooled[32:48] = pooled_own[8:24]
     pooled[48:64] = pooled_own[pl.ds(pl.multiple_of(16 * held - 24, 8), 16)]
 
@@ -486,8 +516,15 @@
         ends[80:128] = jnp.zeros((48, W * CH), BF16)
         pooled[72:96] = jnp.zeros((24, CH), F32)
 
-    lifted[...] = bottleneck(
-        pooled[...], [0, 16, 48, 64], (w_down, w_query, w_key, w_value, w_attn_out, w_up)
+    lifted[...] = bottleneck(pooled[...], [0, 16, 48, 64], weights)
+    total[...] = total_own[...]
+    plans = [
+        (first, stop, [(features, start, DOM)], *rest)
+        for first, stop, start, *rest in inner_plans(range(EARLY, SLOTS - 2), held)
+    ]
+    late = lifted_own.at[EARLY * TOKENS :]
+    convolve(
+        plans, LATE * DOM, late, active_inner, halves_inner, padded.at[0:2], out_right, total
     )
     near = pl.multiple_of(P_SIZE * held - 48, 16)
     last = pl.multiple_of(P_SIZE * held - M, 16)
@@ -497,8 +534,7 @@
         (0, 8, [(features, near, 32), (ends, 64, 32)], near, 0, 48, True),
         (0, 4, [(ends, 64, 32)], last, 0, 16, has_right),
     ]
-    total[...] = total_own[...]
-    convolve(plans, 96, lifted, active, halves, padded, out_right, total)
+    convolve(plans, 96, lifted, active, halves, padded.at[2:4], out_right, total)
 
     slot = lax.broadcasted_iota(jnp.int32, (SLOTS, P_SIZE, 128), 0)
     row = lax.broadcasted_iota(jnp.int32, (SLOTS, P_SIZE, 128), 1)
@@ -583,35 +619,37 @@
 
     basis, along, along_side, place = (jnp.asarray(array) for array in tables())
     loaded = [state, mean_field, basis, along, along_side]
-    loaded += [w_down, w_query, w_key, w_value, w_attn_out, w_up]
+    loaded += [w_down, w_query, w_key, w_up]
     prepared = pl.pallas_call(
         prepare_kernel,
         out_shape=in_vmem(*((array.shape, array.dtype) for array in loaded))
-        + [jax.ShapeDtypeStruct((8,), jnp.int32)]
         + in_vmem(
             ((PIECE, 128), BF16),
             ((PIECE, 128), BF16),
             ((8, 128), F32),
             ((CH2, CH2), BF16),
             ((HALF_LANES, 256), BF16),
+            ((CH2, HEADS * CH), BF16),
         ),
-        in_specs=[smem] * 2 + [hbm] * (4 + len(loaded)),
-        out_specs=[vmem] * len(loaded) + [smem] + [vmem] * 5,
+        in_specs=[smem] * 2 + [hbm] * (6 + len(loaded)),
+        out_specs=[vmem] * (len(loaded) + 6),
         scratch_shapes=[
+            pltpu.VMEM(w_value.shape, BF16),
+            pltpu.VMEM(w_attn_out.shape, BF16),
             pltpu.VMEM(noise_embed.shape, F32),
             pltpu.VMEM(w_stem.shape, BF16),
             pltpu.VMEM(w_out.T.shape, BF16),
             pltpu.VMEM(place.shape, BF16),
             pltpu.VMEM((256, 256), F32),
-            pltpu.SemaphoreType.DMA((4 + len(loaded),)),
+            pltpu.SemaphoreType.DMA((6 + len(loaded),)),
         ],
         compiler_params=limit,
         cost_estimate=pl.CostEstimate(flops=10**9, bytes_accessed=8 * 10**6, transcendentals=0),
         name="prepare",
-    )(counts, sigma, *in_hbm(noise_embed, w_stem, w_out.T, place, *loaded))
+    )(counts, sigma, *in_hbm(noise_embed, w_stem, w_out.T, place, w_value, w_attn_out, *loaded))
     state, mean_field, basis, along, along_side = prepared[:5]
-    weights = prepared[5:11]
-    held, first, second, levels, stem_right, out_right = prepared[11:]
+    first, second, levels, stem_right, out_right, w_joint = prepared[9:]
+    weights = [*prepared[5:8], w_joint, prepared[8]]
 
     second, first, mix_own = pl.pallas_call(
         pack_kernel,
@@ -623,7 +661,7 @@
         scratch_shapes=[pltpu.VMEM((MEMBERS, 8, 128), F32)],
         compiler_params=limit,
         name="pack",
-    )(held, *chips, first, second)
+    )(counts, *chips, first, second)
     pairs = [(i, i ^ 1) for i in range(owners)]
     others = []
     for i in range(1, owners - 1, 2):
@@ -631,28 +669,30 @@
     second = lax.ppermute(second, "space", others)
     first = lax.ppermute(first, "space", pairs)
 
-    features, pooled, total = pl.pallas_call(
+    features, pooled, lifted, total = pl.pallas_call(
         own_kernel,
         out_shape=in_vmem(
-            ((OWN_ROWS, W * CH), BF16), ((OWN_TOKENS, CH), F32), ((OWN_ROWS, 128), F32)
+            ((OWN_ROWS, W * CH), BF16),
+            ((OWN_TOKENS, CH), F32),
+            ((4 * TOKENS, CH), F32),
+            ((OWN_ROWS, 128), F32),
         ),
-        in_specs=[smem] + [vmem] * 14,
-        out_specs=[vmem] * 3,
+        in_specs=[smem] + [vmem] * 13,
+        out_specs=[vmem] * 4,
         scratch_shapes=[
             pltpu.VMEM((2, OWN_ROWS, 256), BF16),
             pltpu.VMEM((4, OWN_ROWS + 16, 128), F32),
             pltpu.VMEM((OWN_ROWS, STEM_LANES), BF16),
             pltpu.VMEM((OWN_TOKENS + 16, CH), F32),
-            pltpu.VMEM((4 * TOKENS, CH), F32),
-            pltpu.VMEM((2, 4 * DOM, HALF_LANES), BF16),
-            pltpu.VMEM((2, 4 * DOM, 256), F32),
+            pltpu.VMEM((1, 2 * EARLY * DOM, HALF_LANES), BF16),
+            pltpu.VMEM((1, 2 * EARLY * DOM, 256), F32),
             pltpu.VMEM((2, 80, 384), F32),
         ],
         compiler_params=limit,
         cost_estimate=pl.CostEstimate(flops=10**9, bytes_accessed=10**7, transcendentals=2 * 10**6),
         name="own",
     )(
-        held, state, mean_field, mix_own, along, levels, basis, stem_right, out_right, *weights
+        counts, state, mean_field, mix_own, along, levels, basis, stem_right, out_right, *weights
     )
 
     denoised, stepped = pl.pallas_call(
@@ -675,15 +715,17 @@
             pltpu.VMEM((4 * TOKENS, CH), F32),
             pltpu.VMEM((2, 2 * 96, HALF_LANES), BF16),
             pltpu.VMEM((2, 2 * 96, 256), F32),
-            pltpu.VMEM((2, 80, 384), F32),
+            pltpu.VMEM((4, 80, 384), F32),
             pltpu.VMEM((OWN_ROWS, 128), F32),
+            pltpu.VMEM((1, 2 * LATE * DOM, HALF_LANES), BF16),
+            pltpu.VMEM((1, 2 * LATE * DOM, 256), F32),
         ],
         compiler_params=limit,
         cost_estimate=pl.CostEstimate(flops=10**9, bytes_accessed=10**7, transcendentals=2 * 10**6),
         name="main",
     )(
-        held, sigma_next, state, mean_field, second, first, mix_own, levels, along_side, basis, stem_right,
-        pooled, features, total, *weights, out_right,
+        counts, sigma_next, state, mean_field, second, first, mix_own, levels, along_side, basis, stem_right,
+        pooled, features, lifted, total, *weights, out_right,
     )
     return denoised[None], stepped[None]
 

time: 27.8 us -> 25.4 us (0.914)
  Pallas kernels: 13.9 us -> 11.3 us
    pallas_call x1, Pallas kernels: 5.08 us -> 3.88 us  [shards(): pl.pallas_call(own_kernel, out_shape=in_vmem(((OWN_ROWS, W * CH), BF16),...]
    pallas_call x1, Pallas kernels: 4.98 us -> 4.36 us  [shards(): pl.pallas_call(main_kernel, out_shape=(jax.ShapeDtypeStruct((SLOTS, P_SIZ...]
    pallas_call x1, Pallas kernels: 0.58 us -> 0.03 us  [shards(): pl.pallas_call(pack_kernel, out_shape=in_vmem(((PIECE, 128), BF16), ((PIE...]
  transfers between devices with their start and end apart: 6 -> 6, of which waited for: 1 -> 1; matrix products, arithmetic and copies ran while one was open for 0% -> 0% of each run, Pallas kernels for 27% -> 24%
where the time goes in v4:
time: 25.4 us; the launch traced here: 25.2 us
  Pallas kernels  11.3 us (44%)
  starting transfers between devices  10.4 us (41%)
  between operations  2.66 us (10%)
  waiting for transfers between devices  0.88 us (3%)
    pallas_call x1, Pallas kernels, shards(): pl.pallas_call(main_kernel, out_shape=(jax.ShapeDtypeStruct((SLOTS, P_SIZ...  4.36 us
    ppermute x3, starting transfers between devices, shards(): lax.ppermute(merged, 'member', [(i, i ^ 2 * distance) for i in range(MEMB...  4.25 us
    pallas_call x1, Pallas kernels, shards(): pl.pallas_call(own_kernel, out_shape=in_vmem(((OWN_ROWS, W * CH), BF16),...  3.88 us
    ppermute x1, starting transfers between devices, shards(): first = lax.ppermute(first, 'space', pairs)  3.71 us
    ppermute x1, starting transfers between devices, shards(): second = lax.ppermute(second, 'space', others)  2.36 us
    pallas_call x1, Pallas kernels, shards(): pl.pallas_call(prepare_kernel, out_shape=in_vmem(*((array.shape, array.dt...  2.18 us
    ppermute x3, waiting for transfers between devices, shards(): lax.ppermute(merged, 'member', [(i, i ^ 2 * distance) for i in range(MEMB...  0.87 us
    pallas_call x1, Pallas kernels, shards(): pl.pallas_call(mix_kernel, out_shape=pltpu.VMEM((8, 128), F32), in_specs=...  0.8 us
  transfers between devices with their start and end apart: 6, of which 1 were waited for; matrix products, arithmetic and copies ran while one was open for 0% of the time, Pallas kernels for 24%

profile of v4, /device:TPU:112, one launch (start us, length us, event | category | flops | bytes accessed | tf_op | source)
XLA Modules:
  0.0 25.2 jit_solution(12347758387685060687)
XLA Ops:
  0.6 0.8 %mix.1.mixed = f32[8,128]{1,0:T(8,128)S(1)} custom-call(s32[4,6]{1,0:T(4,128)} %bitcast.6, s32[4,6]{1,0:T(4,128)} %bitcast.7, f32[16]{0:T(128)} %table.1, f32[8,24]{1,0:T(8,128)} %coarse.1), custom_call_target="tpu_custom_call" | custom-call | tf_op jit(solution)/shard_map/mix/pallas_call | solution.py:591
  1.4 0.1 collective-permute-start
  2.8 0.0 collective-permute-done.partners
  2.9 3.1 %collective-permute-start.3 = (f32[16,128]{1,0:T(8,128)S(1)}, f32[16,128]{1,0:T(8,128)S(1)}, u32[]{:S(2)}, u32[]{:S(2)}) collective-permute-start(f32[16,128]{1,0:T(8,128)S(1)} %merge.1.chip0), channel_id=1, source_target_pairs={{0,128},{32,160},{64,192},{96,224},{128,0},{160,32},{192,64},{224,... | collective-permute-start | bytes 24584 | tf_op jit(solution)/shard_map/ppermute | solution.py:616
  6.0 1.1 %collective-permute-start.2 = (f32[16,128]{1,0:T(8,128)S(1)}, f32[16,128]{1,0:T(8,128)S(1)}, u32[]{:S(2)}, u32[]{:S(2)}) collective-permute-start(f32[16,128]{1,0:T(8,128)S(1)} %merge.1.chip0), channel_id=1, source_target_pairs={{0,192},{32,224},{64,128},{96,160},{128,64},{160,96},{192,0},{224,... | collective-permute-start | bytes 24584 | tf_op jit(solution)/shard_map/ppermute | solution.py:616
  7.1 0.0 collective-permute-start.1
  7.1 2.2 %prepare.1 = (f32[6,32,128]{2,1,0:T(8,128)S(1)}, f32[6,32,128]{2,1,0:T(8,128)S(1)}, bf16[2,256,1152]{2,1,0:T(8,128)(2,1)S(1)}, bf16[192,48]{1,0:T(8,128)(2,1)S(1...) custom-call(s32[1]{0:T(128)S(6)} %copy.24.counts, ...), custom_call_target="tpu_custom_call" | custom-call | flops 1000000000 | bytes 8000000 | tf_op jit(solution)/shard_map/prepare/pallas_call | solution.py:623
  10.0 0.0 collective-permute-done.3.chip3
  10.0 0.9 %collective-permute-done.2.chip2 = f32[16,128]{1,0:T(8,128)S(1)} collective-permute-done((f32[16,128]{1,0:T(8,128)S(1)}, f32[16,128]{1,0:T(8,128)S(1)}, u32[]{:S(2)}, u32[]{:S(2)}) %collective-permute-start.2) | collective-permute-done | bytes 8224 | tf_op jit(solution)/shard_map/ppermute | solution.py:616
  10.8 0.0 collective-permute-done.1.chip1
  10.9 2.4 %collective-permute-start.4 = (bf16[160,128]{1,0:T(8,128)(2,1)S(1)}, bf16[160,128]{1,0:T(8,128)(2,1)S(1)}, u32[]{:S(2)}, u32[]{:S(2)}) collective-permute-start(bf16[160,128]{1,0:T(8,128)(2,1)S(1)} %get-tuple-element.30), channel_id=1, source_target_pairs={{1,2},{2,1},{3,4},{4,3},{5,6},{6,5},{7,8},{8,7},{9,10},{10,9},{11,... | collective-permute-start | bytes 122888 | tf_op jit(solution)/shard_map/ppermute | solution.py:669
  13.2 3.7 %collective-permute-start.5 = (bf16[160,128]{1,0:T(8,128)(2,1)S(1)}, bf16[160,128]{1,0:T(8,128)(2,1)S(1)}, u32[]{:S(2)}, u32[]{:S(2)}) collective-permute-start(bf16[160,128]{1,0:T(8,128)(2,1)S(1)} %get-tuple-element.31), channel_id=1, source_target_pairs={{0,1},{1,0},{2,3},{3,2},{4,5},{5,4},{6,7},{7,6},{8,9},{9,8},{10,11... | collective-permute-start | bytes 122888 | tf_op jit(solution)/shard_map/ppermute | solution.py:670
  17.0 3.9 %own.1 = (bf16[192,4096]{1,0:T(8,128)(2,1)S(1)}, f32[96,128]{1,0:T(8,128)S(1)}, f32[128,128]{1,0:T(8,128)S(1)}, f32[192,128]{1,0:T(8,128)S(1)}) custom-call(s32[1]{0:T(128)S(6)} %copy.24.counts, f32[6,32,128]{2,1,0:T(8,128)S(1)} %get-tuple-element.26.noisy, f32[6,32,128]{2,1,0:T(8,128)S(1)} %get-tuple-element.27.mean_field, ...), custom_call_target="tpu_custom_call" | custom-call | flops 1000000000 | bytes 10000000 | tf_op jit(solution)/shard_map/own/pallas_call | solution.py:672
  20.8 0.0 collective-permute-done.4.second_in
  20.9 0.0 collective-permute-done.5.first_in
  20.9 4.4 %main.1 = (f32[6,32,128]{2,1,0:T(8,128)}, f32[6,32,128]{2,1,0:T(8,128)}) custom-call(s32[1]{0:T(128)S(6)} %copy.24.counts, f32[1]{0:T(128)S(6)} %copy.26.sigma_next, f32[6,32,128]{2,1,0:T(8,128)S(1)} %get-tuple-element.26.noisy, f32[6,32,128]{2,1,0:T(8,128)S(1)} %get-tuple-element.27.mean_field, bf16[160,128]{1,0:T(8,128)(2,1)S(1)} %collective-permute-done.4.second_in, ...), custom_call_target="tpu_custom_call" | custom-call | flops 1000000000 | bytes 10000000 | tf_op jit(solution)/shard_map/main/pallas_call | solution.py:698
  (2 shorter events, 0.1 us)
Async XLA Ops:
  1.4 1.4 %collective-permute-start = (f32[8,128]{1,0:T(8,128)S(1)}, f32[8,128]{1,0:T(8,128)S(1)}, u32[]{:S(2)}, u32[]{:S(2)}) collective-permute-start(f32[8,128]{1,0:T(8,128)S(1)} %mix.1.mixed), channel_id=1, source_target_pairs={{0,32},{32,0},{64,96},{96,64},{128,160},{160,128},{192,224},{224,1... | collective-permute-start | bytes 12296 | tf_op jit(solution)/shard_map/ppermute | solution.py:606
  2.9 7.1 %collective-permute-start.3 = (f32[16,128]{1,0:T(8,128)S(1)}, f32[16,128]{1,0:T(8,128)S(1)}, u32[]{:S(2)}, u32[]{:S(2)}) collective-permute-start(f32[16,128]{1,0:T(8,128)S(1)} %merge.1.chip0), channel_id=1, source_target_pairs={{0,128},{32,160},{64,192},{96,224},{128,0},{160,32},{192,64},{224,... | collective-permute-start | bytes 24584 | tf_op jit(solution)/shard_map/ppermute | solution.py:616
  6.0 4.9 %collective-permute-start.2 = (f32[16,128]{1,0:T(8,128)S(1)}, f32[16,128]{1,0:T(8,128)S(1)}, u32[]{:S(2)}, u32[]{:S(2)}) collective-permute-start(f32[16,128]{1,0:T(8,128)S(1)} %merge.1.chip0), channel_id=1, source_target_pairs={{0,192},{32,224},{64,128},{96,160},{128,64},{160,96},{192,0},{224,... | collective-permute-start | bytes 24584 | tf_op jit(solution)/shard_map/ppermute | solution.py:616
  7.1 3.7 %collective-permute-start.1 = (f32[16,128]{1,0:T(8,128)S(1)}, f32[16,128]{1,0:T(8,128)S(1)}, u32[]{:S(2)}, u32[]{:S(2)}) collective-permute-start(f32[16,128]{1,0:T(8,128)S(1)} %merge.1.chip0), channel_id=1, source_target_pairs={{0,64},{32,96},{64,0},{96,32},{128,192},{160,224},{192,128},{224,1... | collective-permute-start | bytes 24584 | tf_op jit(solution)/shard_map/ppermute | solution.py:616
  10.9 10.0 %collective-permute-start.4 = (bf16[160,128]{1,0:T(8,128)(2,1)S(1)}, bf16[160,128]{1,0:T(8,128)(2,1)S(1)}, u32[]{:S(2)}, u32[]{:S(2)}) collective-permute-start(bf16[160,128]{1,0:T(8,128)(2,1)S(1)} %get-tuple-element.30), channel_id=1, source_target_pairs={{1,2},{2,1},{3,4},{4,3},{5,6},{6,5},{7,8},{8,7},{9,10},{10,9},{11,... | collective-permute-start | bytes 122888 | tf_op jit(solution)/shard_map/ppermute | solution.py:669
  13.2 7.6 %collective-permute-start.5 = (bf16[160,128]{1,0:T(8,128)(2,1)S(1)}, bf16[160,128]{1,0:T(8,128)(2,1)S(1)}, u32[]{:S(2)}, u32[]{:S(2)}) collective-permute-start(bf16[160,128]{1,0:T(8,128)(2,1)S(1)} %get-tuple-element.31), channel_id=1, source_target_pairs={{0,1},{1,0},{2,3},{3,2},{4,5},{5,4},{6,7},{7,6},{8,9},{9,8},{10,11... | collective-permute-start | bytes 122888 | tf_op jit(solution)/shard_map/ppermute | solution.py:670

commit v5 on v4

--- a/solution.py
+++ b/solution.py
@@ -47,7 +47,7 @@
 HALF = W // 2
 HALF_LANES = HALF * CH
 TAP_LANES = (HALF + 2) * VARS
-EARLY = 3
+EARLY = 2
 LATE = SLOTS - 2 - EARLY
 VMEM_LIMIT = 24 * 1024 * 1024
 
@@ -305,10 +305,16 @@
 
 
 def bottleneck(pooled, starts, weights):
+    *_, lifted = bottleneck_steps(pooled, starts, weights)
+    return lifted
+
+
+def bottleneck_steps(pooled, starts, weights):
     w_down, w_query, w_key, w_joint, w_up = weights
     zeta = silu(dot(pooled.astype(BF16), w_down[...]))
     scale = lax.rsqrt(jnp.mean(zeta * zeta, axis=-1, keepdims=True) + NORM_EPS)
     given = zeta.astype(BF16)
+    yield None
     query = (scale * HEAD_DIM**-0.5 * dot(given, w_query[...])).astype(BF16)
     keyed = (scale * dot(given, w_key[...])).astype(BF16)
     valued = (scale * dot(given, w_joint[...])).astype(BF16)
@@ -320,31 +326,41 @@
     lane = lax.broadcasted_iota(jnp.int32, (HEADS * TOKENS, HEADS * TOKENS), 1) // TOKENS
     same_head = (row == lane).astype(F32).astype(BF16)
     head_of_lane = lax.broadcasted_iota(jnp.int32, (TOKENS, HEADS * TOKENS), 1) // TOKENS
-    lifted = []
+    yield None
+    scores = []
     for start in starts:
         rows = slice(start, start + TOKENS)
         keys = jnp.concatenate([keyed[rows]] * HEADS, axis=0) * own_head
+        scores.append(
+            lax.dot_general(
+                query[rows], keys, (((1,), (1,)), ((), ())), preferred_element_type=F32
+            )
+        )
+    yield None
+    weighted = []
+    for score in scores:
+        top = jnp.zeros_like(score)
+        for head in range(HEADS):
+            inside = head_of_lane == head
+            largest = jnp.max(jnp.where(inside, score, -jnp.inf), axis=1, keepdims=True)
+            top = jnp.where(inside, largest, top)
+        weighted.append(jnp.exp(score - top))
+    yield None
+    lifted = []
+    for start, weight in zip(starts, weighted):
+        rows = slice(start, start + TOKENS)
         values = jnp.concatenate(
             [valued[rows, head * CH : (head + 1) * CH] for head in range(HEADS)], axis=0
         )
-        scores = lax.dot_general(
-            query[rows], keys, (((1,), (1,)), ((), ())), preferred_element_type=F32
-        )
-        top = jnp.zeros_like(scores)
-        for head in range(HEADS):
-            inside = head_of_lane == head
-            largest = jnp.max(jnp.where(inside, scores, -jnp.inf), axis=1, keepdims=True)
-            top = jnp.where(inside, largest, top)
-        weight = jnp.exp(scores - top)
         weight = (weight / dot(weight.astype(BF16), same_head)).astype(BF16)
         lifted.append(0.5 * (raised[rows] + dot(weight, values)))
-    return jnp.concatenate(lifted, axis=0)
-
-
-def activate(number, sources, first, lifted, active, base):
+    yield jnp.concatenate(lifted, axis=0)
+
+
+def activate(number, sources, first, lifted, active, base, block_cols=range(4)):
     half_rows = active.shape[0] // 2
     count = sum(rows for _, _, rows in sources) // 8
-    for block_col in range(4):
+    for block_col in block_cols:
         raised = lifted[pl.ds(number * TOKENS + first * 4 + block_col, count, stride=4)].reshape(
             count, 1, CH
         )
@@ -380,14 +396,15 @@
     return field * jnp.minimum(row + 1, DOM - row).astype(F32)
 
 
-def convolve(plans, group_rows, lifted, active, halves, padded, out_right, total):
+def convolve(plans, group_rows, lifted, active, halves, padded, out_right, total, ready=False):
     groups = active.shape[0]
     each = len(plans) // groups
     for group in range(groups):
         base = 0
         for number in range(each * group, each * group + each):
             first, stop, sources = plans[number][:3]
-            activate(number, sources, first, lifted, active.at[group], base)
+            if not ready:
+                activate(number, sources, first, lifted, active.at[group], base)
             base += (stop - first) * 8
         halves[group] = dot(active[group], out_right[...])
     for group in range(groups):
@@ -516,15 +533,22 @@
         ends[80:128] = jnp.zeros((48, W * CH), BF16)
         pooled[72:96] = jnp.zeros((24, CH), F32)
 
-    lifted[...] = bottleneck(pooled[...], [0, 16, 48, 64], weights)
-    total[...] = total_own[...]
     plans = [
         (first, stop, [(features, start, DOM)], *rest)
         for first, stop, start, *rest in inner_plans(range(EARLY, SLOTS - 2), held)
     ]
     late = lifted_own.at[EARLY * TOKENS :]
+    parts = [(number, block_col) for number in range(LATE) for block_col in range(4)]
+    for done in bottleneck_steps(pooled[...], [0, 16, 48, 64], weights):
+        for number, block_col in parts[:2]:
+            activate(
+                number, plans[number][2], 0, late, active_inner.at[0], number * DOM, [block_col]
+            )
+        parts = parts[2:]
+    lifted[...] = done
+    total[...] = total_own[...]
     convolve(
-        plans, LATE * DOM, late, active_inner, halves_inner, padded.at[0:2], out_right, total
+        plans, LATE * DOM, late, active_inner, halves_inner, padded.at[0:2], out_right, total, True
     )
     near = pl.multiple_of(P_SIZE * held - 48, 16)
     last = pl.multiple_of(P_SIZE * held - M, 16)

time: 25.4 us -> 25.1 us (0.988)
  Pallas kernels: 11.3 us -> 11 us
    pallas_call x1, Pallas kernels: 3.88 us -> 3.42 us  [shards(): pl.pallas_call(own_kernel, out_shape=in_vmem(((OWN_ROWS, W * CH), BF16),...]
  transfers between devices with their start and end apart: 6 -> 6, of which waited for: 1 -> 1; matrix products, arithmetic and copies ran while one was open for 0% -> 0% of each run, Pallas kernels for 24% -> 23%
where the time goes in v5:
time: 25.1 us; the launch traced here: 24.9 us
  Pallas kernels  11 us (44%)
  starting transfers between devices  10.4 us (41%)
  between operations  2.66 us (11%)
  waiting for transfers between devices  0.88 us (4%)
    pallas_call x1, Pallas kernels, shards(): pl.pallas_call(main_kernel, out_shape=(jax.ShapeDtypeStruct((SLOTS, P_SIZ...  4.52 us
    ppermute x3, starting transfers between devices, shards(): lax.ppermute(merged, 'member', [(i, i ^ 2 * distance) for i in range(MEMB...  4.25 us
    ppermute x1, starting transfers between devices, shards(): first = lax.ppermute(first, 'space', pairs)  3.71 us
    pallas_call x1, Pallas kernels, shards(): pl.pallas_call(own_kernel, out_shape=in_vmem(((OWN_ROWS, W * CH), BF16),...  3.42 us
    ppermute x1, starting transfers between devices, shards(): second = lax.ppermute(second, 'space', others)  2.36 us
    pallas_call x1, Pallas kernels, shards(): pl.pallas_call(prepare_kernel, out_shape=in_vmem(*((array.shape, array.dt...  2.18 us
    ppermute x3, waiting for transfers between devices, shards(): lax.ppermute(merged, 'member', [(i, i ^ 2 * distance) for i in range(MEMB...  0.87 us
    pallas_call x1, Pallas kernels, shards(): pl.pallas_call(mix_kernel, out_shape=pltpu.VMEM((8, 128), F32), in_specs=...  0.8 us
  transfers between devices with their start and end apart: 6, of which 1 were waited for; matrix products, arithmetic and copies ran while one was open for 0% of the time, Pallas kernels for 23%

profile of v5, /device:TPU:112, one launch (start us, length us, event | category | flops | bytes accessed | tf_op | source)
XLA Modules:
  0.0 24.9 jit_solution(7455579210939332947)
XLA Ops:
  0.6 0.8 %mix.1.mixed = f32[8,128]{1,0:T(8,128)S(1)} custom-call(s32[4,6]{1,0:T(4,128)} %bitcast.6, s32[4,6]{1,0:T(4,128)} %bitcast.7, f32[16]{0:T(128)} %table.1, f32[8,24]{1,0:T(8,128)} %coarse.1), custom_call_target="tpu_custom_call" | custom-call | tf_op jit(solution)/shard_map/mix/pallas_call | solution.py:615
  1.4 0.1 collective-permute-start
  2.8 0.0 collective-permute-done.partners
  2.9 3.1 %collective-permute-start.3 = (f32[16,128]{1,0:T(8,128)S(1)}, f32[16,128]{1,0:T(8,128)S(1)}, u32[]{:S(2)}, u32[]{:S(2)}) collective-permute-start(f32[16,128]{1,0:T(8,128)S(1)} %merge.1.chip0), channel_id=1, source_target_pairs={{0,128},{32,160},{64,192},{96,224},{128,0},{160,32},{192,64},{224,... | collective-permute-start | bytes 24584 | tf_op jit(solution)/shard_map/ppermute | solution.py:640
  6.0 1.1 %collective-permute-start.2 = (f32[16,128]{1,0:T(8,128)S(1)}, f32[16,128]{1,0:T(8,128)S(1)}, u32[]{:S(2)}, u32[]{:S(2)}) collective-permute-start(f32[16,128]{1,0:T(8,128)S(1)} %merge.1.chip0), channel_id=1, source_target_pairs={{0,192},{32,224},{64,128},{96,160},{128,64},{160,96},{192,0},{224,... | collective-permute-start | bytes 24584 | tf_op jit(solution)/shard_map/ppermute | solution.py:640
  7.1 0.0 collective-permute-start.1
  7.1 2.2 %prepare.1 = (f32[6,32,128]{2,1,0:T(8,128)S(1)}, f32[6,32,128]{2,1,0:T(8,128)S(1)}, bf16[2,256,1152]{2,1,0:T(8,128)(2,1)S(1)}, bf16[192,48]{1,0:T(8,128)(2,1)S(1...) custom-call(s32[1]{0:T(128)S(6)} %copy.24.counts, ...), custom_call_target="tpu_custom_call" | custom-call | flops 1000000000 | bytes 8000000 | tf_op jit(solution)/shard_map/prepare/pallas_call | solution.py:647
  10.0 0.0 collective-permute-done.3.chip3
  10.0 0.9 %collective-permute-done.2.chip2 = f32[16,128]{1,0:T(8,128)S(1)} collective-permute-done((f32[16,128]{1,0:T(8,128)S(1)}, f32[16,128]{1,0:T(8,128)S(1)}, u32[]{:S(2)}, u32[]{:S(2)}) %collective-permute-start.2) | collective-permute-done | bytes 8224 | tf_op jit(solution)/shard_map/ppermute | solution.py:640
  10.8 0.0 collective-permute-done.1.chip1
  10.9 2.4 %collective-permute-start.4 = (bf16[160,128]{1,0:T(8,128)(2,1)S(1)}, bf16[160,128]{1,0:T(8,128)(2,1)S(1)}, u32[]{:S(2)}, u32[]{:S(2)}) collective-permute-start(bf16[160,128]{1,0:T(8,128)(2,1)S(1)} %get-tuple-element.30), channel_id=1, source_target_pairs={{1,2},{2,1},{3,4},{4,3},{5,6},{6,5},{7,8},{8,7},{9,10},{10,9},{11,... | collective-permute-start | bytes 122888 | tf_op jit(solution)/shard_map/ppermute | solution.py:693
  13.2 3.7 %collective-permute-start.5 = (bf16[160,128]{1,0:T(8,128)(2,1)S(1)}, bf16[160,128]{1,0:T(8,128)(2,1)S(1)}, u32[]{:S(2)}, u32[]{:S(2)}) collective-permute-start(bf16[160,128]{1,0:T(8,128)(2,1)S(1)} %get-tuple-element.31), channel_id=1, source_target_pairs={{0,1},{1,0},{2,3},{3,2},{4,5},{5,4},{6,7},{7,6},{8,9},{9,8},{10,11... | collective-permute-start | bytes 122888 | tf_op jit(solution)/shard_map/ppermute | solution.py:694
  17.0 3.4 %own.1 = (bf16[192,4096]{1,0:T(8,128)(2,1)S(1)}, f32[96,128]{1,0:T(8,128)S(1)}, f32[128,128]{1,0:T(8,128)S(1)}, f32[192,128]{1,0:T(8,128)S(1)}) custom-call(s32[1]{0:T(128)S(6)} %copy.24.counts, f32[6,32,128]{2,1,0:T(8,128)S(1)} %get-tuple-element.26.noisy, f32[6,32,128]{2,1,0:T(8,128)S(1)} %get-tuple-element.27.mean_field, ...), custom_call_target="tpu_custom_call" | custom-call | flops 1000000000 | bytes 10000000 | tf_op jit(solution)/shard_map/own/pallas_call | solution.py:696
  20.4 0.0 collective-permute-done.4.second_in
  20.4 0.0 collective-permute-done.5.first_in
  20.4 4.5 %main.1 = (f32[6,32,128]{2,1,0:T(8,128)}, f32[6,32,128]{2,1,0:T(8,128)}) custom-call(s32[1]{0:T(128)S(6)} %copy.24.counts, f32[1]{0:T(128)S(6)} %copy.26.sigma_next, f32[6,32,128]{2,1,0:T(8,128)S(1)} %get-tuple-element.26.noisy, f32[6,32,128]{2,1,0:T(8,128)S(1)} %get-tuple-element.27.mean_field, bf16[160,128]{1,0:T(8,128)(2,1)S(1)} %collective-permute-done.4.second_in, ...), custom_call_target="tpu_custom_call" | custom-call | flops 1000000000 | bytes 10000000 | tf_op jit(solution)/shard_map/main/pallas_call | solution.py:722
  (2 shorter events, 0.1 us)
Async XLA Ops:
  1.4 1.4 %collective-permute-start = (f32[8,128]{1,0:T(8,128)S(1)}, f32[8,128]{1,0:T(8,128)S(1)}, u32[]{:S(2)}, u32[]{:S(2)}) collective-permute-start(f32[8,128]{1,0:T(8,128)S(1)} %mix.1.mixed), channel_id=1, source_target_pairs={{0,32},{32,0},{64,96},{96,64},{128,160},{160,128},{192,224},{224,1... | collective-permute-start | bytes 12296 | tf_op jit(solution)/shard_map/ppermute | solution.py:630
  2.9 7.1 %collective-permute-start.3 = (f32[16,128]{1,0:T(8,128)S(1)}, f32[16,128]{1,0:T(8,128)S(1)}, u32[]{:S(2)}, u32[]{:S(2)}) collective-permute-start(f32[16,128]{1,0:T(8,128)S(1)} %merge.1.chip0), channel_id=1, source_target_pairs={{0,128},{32,160},{64,192},{96,224},{128,0},{160,32},{192,64},{224,... | collective-permute-start | bytes 24584 | tf_op jit(solution)/shard_map/ppermute | solution.py:640
  6.0 4.9 %collective-permute-start.2 = (f32[16,128]{1,0:T(8,128)S(1)}, f32[16,128]{1,0:T(8,128)S(1)}, u32[]{:S(2)}, u32[]{:S(2)}) collective-permute-start(f32[16,128]{1,0:T(8,128)S(1)} %merge.1.chip0), channel_id=1, source_target_pairs={{0,192},{32,224},{64,128},{96,160},{128,64},{160,96},{192,0},{224,... | collective-permute-start | bytes 24584 | tf_op jit(solution)/shard_map/ppermute | solution.py:640
  7.1 3.7 %collective-permute-start.1 = (f32[16,128]{1,0:T(8,128)S(1)}, f32[16,128]{1,0:T(8,128)S(1)}, u32[]{:S(2)}, u32[]{:S(2)}) collective-permute-start(f32[16,128]{1,0:T(8,128)S(1)} %merge.1.chip0), channel_id=1, source_target_pairs={{0,64},{32,96},{64,0},{96,32},{128,192},{160,224},{192,128},{224,1... | collective-permute-start | bytes 24584 | tf_op jit(solution)/shard_map/ppermute | solution.py:640
  10.9 9.5 %collective-permute-start.4 = (bf16[160,128]{1,0:T(8,128)(2,1)S(1)}, bf16[160,128]{1,0:T(8,128)(2,1)S(1)}, u32[]{:S(2)}, u32[]{:S(2)}) collective-permute-start(bf16[160,128]{1,0:T(8,128)(2,1)S(1)} %get-tuple-element.30), channel_id=1, source_target_pairs={{1,2},{2,1},{3,4},{4,3},{5,6},{6,5},{7,8},{8,7},{9,10},{10,9},{11,... | collective-permute-start | bytes 122888 | tf_op jit(solution)/shard_map/ppermute | solution.py:693
  13.2 7.1 %collective-permute-start.5 = (bf16[160,128]{1,0:T(8,128)(2,1)S(1)}, bf16[160,128]{1,0:T(8,128)(2,1)S(1)}, u32[]{:S(2)}, u32[]{:S(2)}) collective-permute-start(bf16[160,128]{1,0:T(8,128)(2,1)S(1)} %get-tuple-element.31), channel_id=1, source_target_pairs={{0,1},{1,0},{2,3},{3,2},{4,5},{5,4},{6,7},{7,6},{8,9},{9,8},{10,11... | collective-permute-start | bytes 122888 | tf_op jit(solution)/shard_map/ppermute | solution.py:694

commit v6 on v5

--- a/solution.py
+++ b/solution.py
@@ -220,7 +220,7 @@
         cells[member] = given[0:8]
         cells[member + 1] = given[8:16]
     for member in range(MEMBERS):
-        mix_out[pl.ds(member, SLOTS, stride=MEMBERS)] = cells[member, 0:SLOTS]
+        mix_out[pl.ds(member, 8, stride=MEMBERS)] = cells[member]
     even = lax.rem(lax.axis_index("space"), 2) == 0
     for out, given, to_right in (
         (first_out, first_in, even),
@@ -678,7 +678,7 @@
     second, first, mix_own = pl.pallas_call(
         pack_kernel,
         out_shape=in_vmem(
-            ((PIECE, 128), BF16), ((PIECE, 128), BF16), ((SLOTS * MEMBERS, 128), F32)
+            ((PIECE, 128), BF16), ((PIECE, 128), BF16), ((8 * MEMBERS, 128), F32)
         ),
         in_specs=[smem] + [vmem] * 6,
         out_specs=[vmem] * 3,

time: 25.1 us -> 25.1 us (level)
  transfers between devices with their start and end apart: 6 -> 6, of which waited for: 1 -> 1; matrix products, arithmetic and copies ran while one was open for 0% -> 0% of each run, Pallas kernels for 23% -> 22%
where the time goes in v6:
time: 25.1 us; the launch traced here: 24.9 us
  Pallas kernels  10.9 us (43%)
  starting transfers between devices  10.4 us (41%)
  between operations  2.65 us (11%)
  waiting for transfers between devices  0.88 us (4%)
    pallas_call x1, Pallas kernels, shards(): pl.pallas_call(main_kernel, out_shape=(jax.ShapeDtypeStruct((SLOTS, P_SIZ...  4.48 us
    ppermute x3, starting transfers between devices, shards(): lax.ppermute(merged, 'member', [(i, i ^ 2 * distance) for i in range(MEMB...  4.25 us
    ppermute x1, starting transfers between devices, shards(): first = lax.ppermute(first, 'space', pairs)  3.71 us
    pallas_call x1, Pallas kernels, shards(): pl.pallas_call(own_kernel, out_shape=in_vmem(((OWN_ROWS, W * CH), BF16),...  3.4 us
    ppermute x1, starting transfers between devices, shards(): second = lax.ppermute(second, 'space', others)  2.36 us
    pallas_call x1, Pallas kernels, shards(): pl.pallas_call(prepare_kernel, out_shape=in_vmem(*((array.shape, array.dt...  2.18 us
    ppermute x3, waiting for transfers between devices, shards(): lax.ppermute(merged, 'member', [(i, i ^ 2 * distance) for i in range(MEMB...  0.87 us
    pallas_call x1, Pallas kernels, shards(): pl.pallas_call(mix_kernel, out_shape=pltpu.VMEM((8, 128), F32), in_specs=...  0.8 us
  transfers between devices with their start and end apart: 6, of which 1 were waited for; matrix products, arithmetic and copies ran while one was open for 0% of the time, Pallas kernels for 22%

profile of v6, /device:TPU:112, one launch (start us, length us, event | category | flops | bytes accessed | tf_op | source)
XLA Modules:
  0.0 24.9 jit_solution(13514001756015544795)
XLA Ops:
  0.6 0.8 %mix.1.mixed = f32[8,128]{1,0:T(8,128)S(1)} custom-call(s32[4,6]{1,0:T(4,128)} %bitcast.6, s32[4,6]{1,0:T(4,128)} %bitcast.7, f32[16]{0:T(128)} %table.1, f32[8,24]{1,0:T(8,128)} %coarse.1), custom_call_target="tpu_custom_call" | custom-call | tf_op jit(solution)/shard_map/mix/pallas_call | solution.py:615
  1.4 0.1 collective-permute-start
  2.8 0.0 collective-permute-done.partners
  2.9 3.1 %collective-permute-start.3 = (f32[16,128]{1,0:T(8,128)S(1)}, f32[16,128]{1,0:T(8,128)S(1)}, u32[]{:S(2)}, u32[]{:S(2)}) collective-permute-start(f32[16,128]{1,0:T(8,128)S(1)} %merge.1.chip0), channel_id=1, source_target_pairs={{0,128},{32,160},{64,192},{96,224},{128,0},{160,32},{192,64},{224,... | collective-permute-start | bytes 24584 | tf_op jit(solution)/shard_map/ppermute | solution.py:640
  6.0 1.1 %collective-permute-start.2 = (f32[16,128]{1,0:T(8,128)S(1)}, f32[16,128]{1,0:T(8,128)S(1)}, u32[]{:S(2)}, u32[]{:S(2)}) collective-permute-start(f32[16,128]{1,0:T(8,128)S(1)} %merge.1.chip0), channel_id=1, source_target_pairs={{0,192},{32,224},{64,128},{96,160},{128,64},{160,96},{192,0},{224,... | collective-permute-start | bytes 24584 | tf_op jit(solution)/shard_map/ppermute | solution.py:640
  7.1 0.0 collective-permute-start.1
  7.1 2.2 %prepare.1 = (f32[6,32,128]{2,1,0:T(8,128)S(1)}, f32[6,32,128]{2,1,0:T(8,128)S(1)}, bf16[2,256,1152]{2,1,0:T(8,128)(2,1)S(1)}, bf16[192,48]{1,0:T(8,128)(2,1)S(1...) custom-call(s32[1]{0:T(128)S(6)} %copy.24.counts, ...), custom_call_target="tpu_custom_call" | custom-call | flops 1000000000 | bytes 8000000 | tf_op jit(solution)/shard_map/prepare/pallas_call | solution.py:647
  10.0 0.0 collective-permute-done.3.chip3
  10.0 0.9 %collective-permute-done.2.chip2 = f32[16,128]{1,0:T(8,128)S(1)} collective-permute-done((f32[16,128]{1,0:T(8,128)S(1)}, f32[16,128]{1,0:T(8,128)S(1)}, u32[]{:S(2)}, u32[]{:S(2)}) %collective-permute-start.2) | collective-permute-done | bytes 8224 | tf_op jit(solution)/shard_map/ppermute | solution.py:640
  10.8 0.0 collective-permute-done.1.chip1
  10.9 2.4 %collective-permute-start.4 = (bf16[160,128]{1,0:T(8,128)(2,1)S(1)}, bf16[160,128]{1,0:T(8,128)(2,1)S(1)}, u32[]{:S(2)}, u32[]{:S(2)}) collective-permute-start(bf16[160,128]{1,0:T(8,128)(2,1)S(1)} %get-tuple-element.30), channel_id=1, source_target_pairs={{1,2},{2,1},{3,4},{4,3},{5,6},{6,5},{7,8},{8,7},{9,10},{10,9},{11,... | collective-permute-start | bytes 122888 | tf_op jit(solution)/shard_map/ppermute | solution.py:693
  13.2 3.7 %collective-permute-start.5 = (bf16[160,128]{1,0:T(8,128)(2,1)S(1)}, bf16[160,128]{1,0:T(8,128)(2,1)S(1)}, u32[]{:S(2)}, u32[]{:S(2)}) collective-permute-start(bf16[160,128]{1,0:T(8,128)(2,1)S(1)} %get-tuple-element.31), channel_id=1, source_target_pairs={{0,1},{1,0},{2,3},{3,2},{4,5},{5,4},{6,7},{7,6},{8,9},{9,8},{10,11... | collective-permute-start | bytes 122888 | tf_op jit(solution)/shard_map/ppermute | solution.py:694
  17.0 3.4 %own.1 = (bf16[192,4096]{1,0:T(8,128)(2,1)S(1)}, f32[96,128]{1,0:T(8,128)S(1)}, f32[128,128]{1,0:T(8,128)S(1)}, f32[192,128]{1,0:T(8,128)S(1)}) custom-call(s32[1]{0:T(128)S(6)} %copy.24.counts, f32[6,32,128]{2,1,0:T(8,128)S(1)} %get-tuple-element.26.noisy, f32[6,32,128]{2,1,0:T(8,128)S(1)} %get-tuple-element.27.mean_field, ...), custom_call_target="tpu_custom_call" | custom-call | flops 1000000000 | bytes 10000000 | tf_op jit(solution)/shard_map/own/pallas_call | solution.py:696
  20.4 0.0 collective-permute-done.4.second_in
  20.4 0.0 collective-permute-done.5.first_in
  20.4 4.5 %main.1 = (f32[6,32,128]{2,1,0:T(8,128)}, f32[6,32,128]{2,1,0:T(8,128)}) custom-call(s32[1]{0:T(128)S(6)} %copy.24.counts, f32[1]{0:T(128)S(6)} %copy.26.sigma_next, f32[6,32,128]{2,1,0:T(8,128)S(1)} %get-tuple-element.26.noisy, f32[6,32,128]{2,1,0:T(8,128)S(1)} %get-tuple-element.27.mean_field, bf16[160,128]{1,0:T(8,128)(2,1)S(1)} %collective-permute-done.4.second_in, ...), custom_call_target="tpu_custom_call" | custom-call | flops 1000000000 | bytes 10000000 | tf_op jit(solution)/shard_map/main/pallas_call | solution.py:722
  (2 shorter events, 0.1 us)
Async XLA Ops:
  1.4 1.4 %collective-permute-start = (f32[8,128]{1,0:T(8,128)S(1)}, f32[8,128]{1,0:T(8,128)S(1)}, u32[]{:S(2)}, u32[]{:S(2)}) collective-permute-start(f32[8,128]{1,0:T(8,128)S(1)} %mix.1.mixed), channel_id=1, source_target_pairs={{0,32},{32,0},{64,96},{96,64},{128,160},{160,128},{192,224},{224,1... | collective-permute-start | bytes 12296 | tf_op jit(solution)/shard_map/ppermute | solution.py:630
  2.9 7.1 %collective-permute-start.3 = (f32[16,128]{1,0:T(8,128)S(1)}, f32[16,128]{1,0:T(8,128)S(1)}, u32[]{:S(2)}, u32[]{:S(2)}) collective-permute-start(f32[16,128]{1,0:T(8,128)S(1)} %merge.1.chip0), channel_id=1, source_target_pairs={{0,128},{32,160},{64,192},{96,224},{128,0},{160,32},{192,64},{224,... | collective-permute-start | bytes 24584 | tf_op jit(solution)/shard_map/ppermute | solution.py:640
  6.0 4.9 %collective-permute-start.2 = (f32[16,128]{1,0:T(8,128)S(1)}, f32[16,128]{1,0:T(8,128)S(1)}, u32[]{:S(2)}, u32[]{:S(2)}) collective-permute-start(f32[16,128]{1,0:T(8,128)S(1)} %merge.1.chip0), channel_id=1, source_target_pairs={{0,192},{32,224},{64,128},{96,160},{128,64},{160,96},{192,0},{224,... | collective-permute-start | bytes 24584 | tf_op jit(solution)/shard_map/ppermute | solution.py:640
  7.1 3.7 %collective-permute-start.1 = (f32[16,128]{1,0:T(8,128)S(1)}, f32[16,128]{1,0:T(8,128)S(1)}, u32[]{:S(2)}, u32[]{:S(2)}) collective-permute-start(f32[16,128]{1,0:T(8,128)S(1)} %merge.1.chip0), channel_id=1, source_target_pairs={{0,64},{32,96},{64,0},{96,32},{128,192},{160,224},{192,128},{224,1... | collective-permute-start | bytes 24584 | tf_op jit(solution)/shard_map/ppermute | solution.py:640
  10.9 9.5 %collective-permute-start.4 = (bf16[160,128]{1,0:T(8,128)(2,1)S(1)}, bf16[160,128]{1,0:T(8,128)(2,1)S(1)}, u32[]{:S(2)}, u32[]{:S(2)}) collective-permute-start(bf16[160,128]{1,0:T(8,128)(2,1)S(1)} %get-tuple-element.30), channel_id=1, source_target_pairs={{1,2},{2,1},{3,4},{4,3},{5,6},{6,5},{7,8},{8,7},{9,10},{10,9},{11,... | collective-permute-start | bytes 122888 | tf_op jit(solution)/shard_map/ppermute | solution.py:693
  13.2 7.1 %collective-permute-start.5 = (bf16[160,128]{1,0:T(8,128)(2,1)S(1)}, bf16[160,128]{1,0:T(8,128)(2,1)S(1)}, u32[]{:S(2)}, u32[]{:S(2)}) collective-permute-start(bf16[160,128]{1,0:T(8,128)(2,1)S(1)} %get-tuple-element.31), channel_id=1, source_target_pairs={{0,1},{1,0},{2,3},{3,2},{4,5},{5,4},{6,7},{7,6},{8,9},{9,8},{10,11... | collective-permute-start | bytes 122888 | tf_op jit(solution)/shard_map/ppermute | solution.py:694
